TPU v7x, 32 devices: a whole 2x2x4 slice. The times are simulated.
32 devices in a mesh: dp: 8 (over y, x, core), mp: 4 (over z).
Axes of the slice: x: 2, y: 2, z: 4, core: 2. Of those that a mesh axis runs over, the one named last changes fastest.
Arguments:
- slot_owner: int32 [512, 2, 32, 1], P('dp'), may hold values from 0 to 7; in each aligned block of 4096 rows (0 to 4095, 4096 to 8191, ..., all dimensions but the last counted through in order) at most 1024 rows name the same one
- slot_row: int32 [512, 2, 32], P('dp'), may hold values from 0 to 4095
- slot_count: int32 [512, 2], P('dp'), may hold values from 1 to 32
- item_qid: int32 [512], replicated, may hold values from 0 to 4095
- positive: int32 [512], P('dp'), may hold values from 0 to 511, each once
- log_prior: float32 [4096], replicated, may hold values from -12 to -6
- embedding: float32 [32768, 128], P('dp'), may hold values from -6 to 6
- embedding_mom: float32 [32768, 128], P('dp'), may hold values from -1.1444092e-05 to 1.1444092e-05
- embedding_avg: float32 [32768, 128], P('dp'), may hold values from -6 to 6
- w_in: float32 [2, 128, 256], replicated, may hold values from -0.5 to 0.5
- w_in_mom: float32 [2, 128, 256], replicated, may hold values from -3.8146973e-05 to 3.8146973e-05
- w_in_avg: float32 [2, 128, 256], replicated, may hold values from -0.5 to 0.5
- norm_gain: float32 [2, 256], replicated, may hold values from 0.5 to 1.5
- norm_gain_mom: float32 [2, 256], replicated, may hold values from -0.00012207031 to 0.00012207031
- norm_gain_avg: float32 [2, 256], replicated, may hold values from 0.5 to 1.5
- w_qkv: float32 [2, 256, 3, 512], P(None, None, None, 'mp'), may hold values from -0.375 to 0.375
- w_qkv_mom: float32 [2, 256, 3, 512], P(None, None, None, 'mp'), may hold values from -3.8146973e-05 to 3.8146973e-05
- w_qkv_avg: float32 [2, 256, 3, 512], P(None, None, None, 'mp'), may hold values from -0.375 to 0.375
- w_out: float32 [2, 512, 256], P(None, 'mp'), may hold values from -0.5 to 0.5
- w_out_mom: float32 [2, 512, 256], P(None, 'mp'), may hold values from -3.8146973e-05 to 3.8146973e-05
- w_out_avg: float32 [2, 512, 256], P(None, 'mp'), may hold values from -0.5 to 0.5
- w_one: float32 [2, 256, 1024], P(None, None, 'mp'), may hold values from -0.375 to 0.375
- w_one_mom: float32 [2, 256, 1024], P(None, None, 'mp'), may hold values from -3.8146973e-05 to 3.8146973e-05
- w_one_avg: float32 [2, 256, 1024], P(None, None, 'mp'), may hold values from -0.375 to 0.375
- w_two: float32 [2, 1024, 512], P(None, 'mp'), may hold values from -0.1875 to 0.1875
- w_two_mom: float32 [2, 1024, 512], P(None, 'mp'), may hold values from -3.8146973e-05 to 3.8146973e-05
- w_two_avg: float32 [2, 1024, 512], P(None, 'mp'), may hold values from -0.1875 to 0.1875
- w_three: float32 [2, 512, 256], replicated, may hold values from -0.25 to 0.25
- w_three_mom: float32 [2, 512, 256], replicated, may hold values from -3.8146973e-05 to 3.8146973e-05
- w_three_avg: float32 [2, 512, 256], replicated, may hold values from -0.25 to 0.25
Outputs:
- loss_sum: float32 [], replicated
- clip_norm: float32 [], replicated
- new_embedding: float32 [32768, 128], P('dp')
- new_embedding_mom: float32 [32768, 128], P('dp')
- new_embedding_avg: float32 [32768, 128], P('dp')
- new_w_in: float32 [2, 128, 256], replicated
- new_w_in_mom: float32 [2, 128, 256], replicated
- new_w_in_avg: float32 [2, 128, 256], replicated
- new_norm_gain: float32 [2, 256], replicated
- new_norm_gain_mom: float32 [2, 256], replicated
- new_norm_gain_avg: float32 [2, 256], replicated
- new_w_qkv: float32 [2, 256, 3, 512], P(None, None, None, 'mp')
- new_w_qkv_mom: float32 [2, 256, 3, 512], P(None, None, None, 'mp')
- new_w_qkv_avg: float32 [2, 256, 3, 512], P(None, None, None, 'mp')
- new_w_out: float32 [2, 512, 256], P(None, 'mp')
- new_w_out_mom: float32 [2, 512, 256], P(None, 'mp')
- new_w_out_avg: float32 [2, 512, 256], P(None, 'mp')
- new_w_one: float32 [2, 256, 1024], P(None, None, 'mp')
- new_w_one_mom: float32 [2, 256, 1024], P(None, None, 'mp')
- new_w_one_avg: float32 [2, 256, 1024], P(None, None, 'mp')
- new_w_two: float32 [2, 1024, 512], P(None, 'mp')
- new_w_two_mom: float32 [2, 1024, 512], P(None, 'mp')
- new_w_two_avg: float32 [2, 1024, 512], P(None, 'mp')
- new_w_three: float32 [2, 512, 256], replicated
- new_w_three_mom: float32 [2, 512, 256], replicated
- new_w_three_avg: float32 [2, 512, 256], replicated
Inputs may be any that keep to these rules, and one draw needn't show every extreme that they name: `slot_owner`: in the rows of one index of dp (4096 slots) no owner is named more than 1024 times, a bound that some block reaches. `positive`: each pair index appears once.
All inputs are finite; a program needn't handle non-finite values.
Results may differ from a plain program's by a relative error of at most 0.028.
Values may be sent and summed in bfloat16 or wider, within the bound.
A program may use at most 128 MiB of HBM per device.

v0:
```python
import jax
import jax.numpy as jnp
from jax import lax
from jax.sharding import PartitionSpec as P

DH = 64


EPS = 1e-06
INV_TEMP = 20.0
CLIP_NORM = 0.1
ROW_RATE = 150000.0
GAIN_RATE = 8000.0
MATRIX_RATE = 600.0
MOMENTUM = 0.9
AVERAGE_DECAY = 0.6


def contract(spec, left, right):
    return jnp.einsum(spec, left, right, preferred_element_type=jnp.float32)


def rms_norm(hidden, gains):
    return (
        hidden
        * lax.rsqrt(jnp.mean(hidden * hidden, -1, keepdims=True) + EPS)
        * gains[None, :, None, :]
    )


def unit_length(vector):
    return vector * lax.rsqrt(jnp.sum(vector * vector, -1, keepdims=True) + EPS)


def softmax_last(scores):
    return jax.nn.softmax(scores, -1)


def pull_back(func, point, cotangent):
    return jax.vjp(func, point)[1](cotangent.astype(jnp.float32))[0]


def update(weight, grad, moment, average, factor, rate):
    clipped = grad * factor
    moment_new = MOMENTUM * moment + clipped
    weight_new = weight - rate * (clipped + MOMENTUM * moment_new)
    average_new = AVERAGE_DECAY * average + (1.0 - AVERAGE_DECAY) * weight_new
    return [weight_new, moment_new, average_new]


def shards(
    slot_owner,
    slot_row,
    slot_count,
    item_qid,
    positive,
    log_prior,
    embedding,
    embedding_mom,
    embedding_avg,
    w_in,
    w_in_mom,
    w_in_avg,
    norm_gain,
    norm_gain_mom,
    norm_gain_avg,
    w_qkv,
    w_qkv_mom,
    w_qkv_avg,
    w_out,
    w_out_mom,
    w_out_avg,
    w_one,
    w_one_mom,
    w_one_avg,
    w_two,
    w_two_mom,
    w_two_avg,
    w_three,
    w_three_mom,
    w_three_avg,
):
    peers = lax.axis_size("dp")
    groups = lax.axis_size("mp")
    batch, towers, slots = slot_row.shape
    capacity = max(2, 2 * batch * towers * slots // peers)
    pair_count = batch * peers
    part = lax.axis_index("mp")
    row_place = lax.axis_index("dp")
    last_row = (row_place == peers - 1).astype(jnp.float32)
    last_part = (part == groups - 1).astype(jnp.float32)

    def sum_heads(value):
        return lax.psum(value, "mp")

    def sum_units(value):
        return lax.psum(value, "mp")

    local_owner, local_row, local_count, local_positive = (
        slot_owner,
        slot_row,
        slot_count,
        positive,
    )
    low_qkv = w_qkv.astype(jnp.bfloat16)
    low_out = w_out.astype(jnp.bfloat16)
    low_one = w_one.astype(jnp.bfloat16)
    low_two = w_two.astype(jnp.bfloat16)
    low_in = w_in.astype(jnp.bfloat16)
    low_three = w_three.astype(jnp.bfloat16)
    local_batch = local_row.shape[0]
    requests = local_batch * towers * slots
    owners = local_owner.reshape(requests)
    onehot = (owners[:, None] == jnp.arange(peers)[None, :]).astype(jnp.int32)
    earlier = jnp.cumsum(onehot, 0) - onehot
    place = owners * capacity + jnp.sum(earlier * onehot, 1)
    request_ids = (
        jnp.full((peers * capacity,), -1, jnp.int32)
        .at[place]
        .set(local_row.reshape(requests))
        .reshape(peers, capacity)
    )
    table_low = embedding.astype(jnp.bfloat16)
    live_mask = (jnp.arange(slots)[None, None, :] < local_count[:, :, None]).astype(jnp.float32)
    live_count = local_count.astype(jnp.float32)
    heads = low_qkv.shape[-1] // DH

    def serve(asked):
        found = table_low[jnp.maximum(asked, 0)]
        return (lax.all_to_all(found, "dp", split_axis=0, concat_axis=0, tiled=True), asked)

    def fetch():
        replies, served = serve(
            lax.all_to_all(request_ids, "dp", split_axis=0, concat_axis=0, tiled=True)
        )
        embedded = replies.reshape(peers * capacity, -1)[place].reshape(
            local_batch, towers, slots, -1
        )
        return (embedded, served)

    def encode(embedded):
        hidden = contract("btse,ted->btsd", embedded, low_in)
        normed = rms_norm(hidden, norm_gain).astype(jnp.bfloat16)
        qkv = contract("btsd,tdcf->btscf", normed, low_qkv).astype(jnp.bfloat16)
        split_heads = qkv.reshape(local_batch, towers, slots, 3, heads, DH)
        scores = (
            contract("btshd,btrhd->bthsr", split_heads[:, :, :, 0], split_heads[:, :, :, 1]) * 0.125
        )
        scores = jnp.where(live_mask[:, :, None, None, :] > 0, scores, -1000000000.0)
        attention = softmax_last(scores)
        mixture = contract(
            "bthsr,btrhd->btshd", attention.astype(jnp.bfloat16), split_heads[:, :, :, 2]
        ).astype(jnp.bfloat16)
        mixture = mixture.reshape(local_batch, towers, slots, heads * DH)
        summed = hidden + sum_heads(contract("btsf,tfd->btsd", mixture, low_out))
        pooled = (jnp.sum(summed * live_mask[..., None], 2) / live_count[..., None]).astype(
            jnp.bfloat16
        )
        first_pre = contract("btd,tdf->btf", pooled, low_one)
        act_one = jax.nn.gelu(first_pre).astype(jnp.bfloat16)
        second_pre = sum_units(contract("btf,tfg->btg", act_one, low_two))
        act_two = jax.nn.gelu(second_pre).astype(jnp.bfloat16)
        third_pre = contract("btg,tgd->btd", act_two, low_three)
        vectors = unit_length(third_pre).astype(jnp.bfloat16)
        return (
            embedded,
            hidden,
            normed,
            split_heads,
            scores,
            attention,
            mixture,
            pooled,
            first_pre,
            act_one,
            second_pre,
            act_two,
            third_pre,
            vectors,
        )

    embedded, served = fetch()
    kept = encode(embedded)
    vectors = kept[13]
    all_items = lax.all_gather(vectors[:, 1], "dp", axis=0, tiled=True)
    prior = jnp.sum(
        jnp.where(
            item_qid[:, None] == jnp.arange(log_prior.shape[0])[None, :], log_prior[None, :], 0.0
        ),
        1,
    )
    logits = INV_TEMP * contract("bd,jd->bj", vectors[:, 0], all_items) - prior[None, :]
    peak = jnp.max(logits, 1, keepdims=True)
    expo = jnp.exp(logits - peak)
    total = jnp.sum(expo, 1, keepdims=True)
    target = (local_positive[:, None] == jnp.arange(pair_count)[None, :]).astype(jnp.float32)
    loss_part = jnp.sum(peak[:, 0] + jnp.log(total[:, 0]) - jnp.sum(target * logits, 1))
    dlogits = ((expo / total - target) / pair_count).astype(jnp.bfloat16)
    dquery = INV_TEMP * contract("bj,jd->bd", dlogits, all_items)
    ditems = lax.psum_scatter(
        INV_TEMP * contract("bj,bd->jd", dlogits, vectors[:, 0]),
        "dp",
        scatter_dimension=0,
        tiled=True,
    )
    embedded, served = fetch()
    kept = encode(embedded)
    (
        embedded,
        hidden,
        normed,
        split_heads,
        scores,
        attention,
        mixture,
        pooled,
        first_pre,
        act_one,
        second_pre,
        act_two,
        third_pre,
        vectors,
    ) = kept
    dvectors = jnp.stack([dquery, ditems], 1).astype(jnp.bfloat16)
    dthird = pull_back(unit_length, third_pre, dvectors).astype(jnp.bfloat16)
    d_three = contract("btg,btd->tgd", act_two, dthird)
    dact_two = contract("btd,tgd->btg", dthird, low_three).astype(jnp.bfloat16)
    dsecond = pull_back(jax.nn.gelu, second_pre, dact_two).astype(jnp.bfloat16)
    d_two = contract("btf,btg->tfg", act_one, dsecond)
    dact_one = contract("btg,tfg->btf", dsecond, low_two).astype(jnp.bfloat16)
    dfirst = pull_back(jax.nn.gelu, first_pre, dact_one).astype(jnp.bfloat16)
    d_one = contract("btd,btf->tdf", pooled, dfirst)
    dpooled = lax.psum(contract("btf,tdf->btd", dfirst, low_one), "mp").astype(jnp.bfloat16)
    dsummed = (dpooled.astype(jnp.float32) / live_count[..., None])[:, :, None, :] * live_mask[
        ..., None
    ]
    dbranch = dsummed.astype(jnp.bfloat16)
    d_out = contract("btsf,btsd->tfd", mixture, dbranch)
    dmixture = (
        contract("btsd,tfd->btsf", dbranch, low_out)
        .astype(jnp.bfloat16)
        .reshape(local_batch, towers, slots, heads, DH)
    )
    dattention = contract("btshd,btrhd->bthsr", dmixture, split_heads[:, :, :, 2]).astype(
        jnp.bfloat16
    )
    dscores = pull_back(softmax_last, scores, dattention).astype(jnp.bfloat16)
    dqueries = contract("bthsr,btrhd->btshd", dscores, split_heads[:, :, :, 1]) * 0.125
    dkeys = contract("bthsr,btshd->btrhd", dscores, split_heads[:, :, :, 0]) * 0.125
    dvalues = contract("bthsr,btshd->btrhd", attention.astype(jnp.bfloat16), dmixture)
    dqkv = (
        jnp.stack([dqueries, dkeys, dvalues], 3)
        .astype(jnp.bfloat16)
        .reshape(local_batch, towers, slots, 3, heads * DH)
    )
    d_qkv = contract("btsd,btscf->tdcf", normed, dqkv)
    dnormed = lax.psum(contract("btscf,tdcf->btsd", dqkv, low_qkv), "mp").astype(jnp.bfloat16)
    dh_norm, d_gain = jax.vjp(rms_norm, hidden, norm_gain)[1](dnormed.astype(jnp.float32))
    dhidden = (dsummed + dh_norm).astype(jnp.bfloat16)
    d_in = contract("btse,btsd->ted", embedded, dhidden)
    dembedded = contract("btsd,ted->btse", dhidden, low_in)
    outgoing = (
        jnp.zeros((peers * capacity, dembedded.shape[-1]), jnp.float32)
        .at[place]
        .set(dembedded.reshape(requests, -1))
    )
    incoming = lax.all_to_all(
        outgoing.reshape(peers, capacity, -1).astype(jnp.bfloat16),
        "dp",
        split_axis=0,
        concat_axis=0,
        tiled=True,
    ).astype(jnp.float32)
    table_grad = (
        jnp.zeros_like(embedding)
        .at[jnp.maximum(served, 0).reshape(-1)]
        .add(incoming.reshape(-1, embedding.shape[1]))
    )
    d_in, d_gain, d_qkv, d_out, d_one, d_two, d_three, loss_sum = (
        lax.psum(d_in.astype(jnp.bfloat16), "dp").astype(jnp.float32),
        lax.psum(d_gain.astype(jnp.bfloat16), "dp").astype(jnp.float32),
        lax.psum(d_qkv.astype(jnp.bfloat16), "dp").astype(jnp.float32),
        lax.psum(d_out.astype(jnp.bfloat16), "dp").astype(jnp.float32),
        lax.psum(d_one.astype(jnp.bfloat16), "dp").astype(jnp.float32),
        lax.psum(d_two.astype(jnp.bfloat16), "dp").astype(jnp.float32),
        lax.psum(d_three.astype(jnp.bfloat16), "dp").astype(jnp.float32),
        lax.psum(loss_part.astype(jnp.bfloat16), "dp").astype(jnp.float32),
    )
    whole_sq = jnp.sum(d_in * d_in) + jnp.sum(d_gain * d_gain) + jnp.sum(d_three * d_three)
    shard_sq = (
        jnp.sum(d_qkv * d_qkv)
        + jnp.sum(d_out * d_out)
        + jnp.sum(d_one * d_one)
        + jnp.sum(d_two * d_two)
    )
    local_sq = (
        last_row * (whole_sq * last_part + shard_sq) + jnp.sum(table_grad * table_grad) / groups
    )
    norm = jnp.sqrt(lax.psum(local_sq, ("dp", "mp")))
    factor = jnp.minimum(1.0, CLIP_NORM / norm)
    done = []
    done.extend(update(embedding, table_grad, embedding_mom, embedding_avg, factor, ROW_RATE))
    done.extend(update(w_in, d_in, w_in_mom, w_in_avg, factor, MATRIX_RATE))
    done.extend(update(norm_gain, d_gain, norm_gain_mom, norm_gain_avg, factor, GAIN_RATE))
    done.extend(update(w_qkv, d_qkv, w_qkv_mom, w_qkv_avg, factor, MATRIX_RATE))
    done.extend(update(w_out, d_out, w_out_mom, w_out_avg, factor, MATRIX_RATE))
    done.extend(update(w_one, d_one, w_one_mom, w_one_avg, factor, MATRIX_RATE))
    done.extend(update(w_two, d_two, w_two_mom, w_two_avg, factor, MATRIX_RATE))
    done.extend(update(w_three, d_three, w_three_mom, w_three_avg, factor, MATRIX_RATE))
    return (
        loss_sum,
        norm,
        done[0],
        done[1],
        done[2],
        done[3],
        done[4],
        done[5],
        done[6],
        done[7],
        done[8],
        done[9],
        done[10],
        done[11],
        done[12],
        done[13],
        done[14],
        done[15],
        done[16],
        done[17],
        done[18],
        done[19],
        done[20],
        done[21],
        done[22],
        done[23],
    )


def solution(mesh):
    in_specs = (
        P("dp", None, None, None),
        P("dp", None, None),
        P("dp", None),
        P(),
        P("dp"),
        P(),
        P("dp", None),
        P("dp", None),
        P("dp", None),
        P(),
        P(),
        P(),
        P(),
        P(),
        P(),
        P(None, None, None, "mp"),
        P(None, None, None, "mp"),
        P(None, None, None, "mp"),
        P(None, "mp", None),
        P(None, "mp", None),
        P(None, "mp", None),
        P(None, None, "mp"),
        P(None, None, "mp"),
        P(None, None, "mp"),
        P(None, "mp", None),
        P(None, "mp", None),
        P(None, "mp", None),
        P(),
        P(),
        P(),
    )
    out_specs = (
        P(),
        P(),
        P("dp", None),
        P("dp", None),
        P("dp", None),
        P(),
        P(),
        P(),
        P(),
        P(),
        P(),
        P(None, None, None, "mp"),
        P(None, None, None, "mp"),
        P(None, None, None, "mp"),
        P(None, "mp", None),
        P(None, "mp", None),
        P(None, "mp", None),
        P(None, None, "mp"),
        P(None, None, "mp"),
        P(None, None, "mp"),
        P(None, "mp", None),
        P(None, "mp", None),
        P(None, "mp", None),
        P(),
        P(),
        P(),
    )
    return jax.shard_map(shards, mesh=mesh, in_specs=in_specs, out_specs=out_specs, check_vma=False)
```

profile of v0, /device:TPU:0, one launch (start us, length us, event | category | flops | bytes accessed | tf_op | source)
XLA Modules:
  0.0 875.9 jit_solution(8939698279231663636)
XLA Ops:
  13.4 16.1 %scatter_custom_fusion = s32[8192]{0:T(1024)} fusion(s32[4096]{0:T(1024)S(1)} %bitcast.214, s32[4096]{0:T(1024)S(1)} %reshape.267, s32[]{:T(128)} %constant.32.clone.1), kind=kCustom, calls=%fused_computation.226 | custom fusion | bytes 32772 | tf_op jit(solution)/shard_map/scatter | solution.py:120
  29.5 5.2 all-to-all-start
  40.1 29.5 %gather_fusion = bf16[8192,128]{1,0:T(8,128)(2,1)} fusion(bf16[4096,128]{1,0:T(8,128)(2,1)S(1)} %convert_element_type.211, s32[8192]{0:T(1024)S(1)} %broadcast_clamp_fusion), kind=kCustom, calls=%fused_computation | custom fusion | bytes 4227072 | tf_op jit(solution)/shard_map/gather | solution.py:129
  74.1 25.8 %all-to-all-done.1 = bf16[8,1024,128]{2,1,0:T(8,128)(2,1)S(1)} async-done(((bf16[8,1024,128]{2,1,0:T(8,128)(2,1)}), bf16[8,1024,128]{2,1,0:T(8,128)(2,1)S(1)}, u32[]{:S(2)}, u32[]{:S(2)}) %all-to-all-start.1) | async-done | bytes 2097184 | tf_op jit(solution)/shard_map/all_to_all | solution.py:130
  99.9 12.1 %gather_fusion.1 = bf16[4096,128]{1,0:T(8,128)(2,1)S(1)} fusion(bf16[8192,128]{1,0:T(8,128)(2,1)S(1)} %bitcast.205, s32[4096]{0:T(1024)S(1)} %broadcast_clamp_fusion.1), kind=kCustom, calls=%fused_computation.1 | custom fusion | bytes 2113536 | tf_op jit(solution)/shard_map/gather | solution.py:136
  116.6 5.4 reshape.239
  122.0 7.0 fusion.157
  130.4 15.1 %fusion.158 = (f32[64,2,2,32]{3,2,1,0:T(2,128)S(1)}, f32[64,2,2,32,32]{3,4,2,1,0:T(8,128)S(1)}) fusion(f32[64,2,2,32,32]{3,4,2,1,0:T(8,128)S(1)} %fusion.27, pred[64,2,32]{2,1,0:T(4,128)(4,1)S(1)} %copy.105), kind=kOutput, calls=%fused_computation.246 | output fusion | flops 1572895 | bytes 2134016 | tf_op jit(solution)/shard_map/sub | solution.py:36
  159.1 154.5 %all-reduce.8.cloned.1.call-done = f32[64,2,32,256]{3,2,0,1:T(8,128)} async-done(((f32[64,2,32,256]{3,2,0,1:T(8,128)}), f32[64,2,32,256]{3,2,0,1:T(8,128)}) %all-reduce.8.cloned.1.call-update) | async-done | bytes 4194320 | tf_op jit(solution)/shard_map/psum | solution.py:94
  313.5 4.1 fusion.15
  322.0 32.5 %all-reduce.10.cloned.1.call-done = f32[64,2,512]{2,0,1:T(8,128)} async-done(((f32[64,2,512]{2,0,1:T(8,128)}), f32[64,2,512]{2,0,1:T(8,128)}) %all-reduce.10.cloned.1.call-update) | async-done | bytes 262160 | tf_op jit(solution)/shard_map/psum | solution.py:97
  356.7 9.3 %all-gather = bf16[512,1,256]{2,0,1:T(8,128)(2,1)S(1)} all-gather(bf16[64,1,256]{2,0,1:T(8,128)(2,1)S(1)} %slice.44), channel_id=2, replica_groups=mesh['dp'=8,'mp'=4] {'dp'}, dimensions={0}, use_global_device_ids=true | all-gather | bytes 294912 | tf_op jit(solution)/shard_map/all_gather | solution.py:185
  375.0 29.6 %reduce-scatter.2.cloned.1.call-done = f32[64,256]{1,0:T(8,128)} async-done(((f32[512,256]{1,0:T(8,128)}), f32[64,256]{1,0:T(8,128)}) %reduce-scatter.2.cloned.1.call-update) | async-done | bytes 65552 | tf_op jit(solution)/shard_map/reduce_scatter | solution.py:200
  411.7 21.7 %all-reduce.13 = bf16[64,2,256]{2,0,1:T(8,128)(2,1)S(1)} all-reduce(f32[64,2,256]{2,0,1:T(8,128)} %convolution_bitcast_fusion.6), channel_id=1, replica_groups=mesh['dp'=8,'mp'=4] {'mp'}, use_global_device_ids=true, to_apply=%region_19.20 | all-reduce | flops 32768 | bytes 196608 | tf_op jit(solution)/shard_map/psum | solution.py:233
  437.6 5.0 reshape.241
  459.4 5.1 reshape.301
  468.2 4.9 reshape.300
  488.5 140.4 %all-reduce.14 = bf16[64,2,32,256]{3,2,0,1:T(8,128)(2,1)S(1)} all-reduce(f32[64,2,32,256]{3,2,0,1:T(8,128)} %convolution_bitcast_fusion), channel_id=1, replica_groups=mesh['dp'=8,'mp'=4] {'mp'}, use_global_device_ids=true, to_apply=%region_21.22 | all-reduce | flops 1048576 | bytes 6291456 | tf_op jit(solution)/shard_map/psum | solution.py:257
  640.0 12.8 %scatter_custom_fusion.1 = f32[8192,128]{1,0:T(8,128)} fusion(s32[4096]{0:T(1024)S(1)} %bitcast.216, f32[4096,128]{1,0:T(8,128)S(1)} %bitcast.210, f32[]{:T(128)} %constant.36.clone.1), kind=kCustom, calls=%fused_computation.56 | custom fusion | bytes 4194308 | tf_op jit(solution)/shard_map/scatter | solution.py:265
  666.3 35.5 %all-reduce = (bf16[]{:T(256)}, bf16[2,256]{1,0:T(2,128)(2,1)S(1)}) all-reduce(bf16[]{:T(256)} %subtract_reduce_fusion, bf16[2,256]{1,0:T(2,128)(2,1)S(1)} %copy-done.87), channel_id=1, replica_groups=mesh['dp'=8,'mp'=4] {'dp'}, use_global_device_ids=true, to_apply=%region_16.17 | all-reduce | flops 513 | bytes 2052 | tf_op jit(solution)/shard_map/psum | solution.py:287
  702.4 34.6 %all-reduce.12.cloned.1.call-done = (bf16[2,128,256]{2,1,0:T(8,128)(2,1)}, bf16[2,512,256]{2,1,0:T(8,128)(2,1)}, bf16[2,256,3,128]{3,1,2,0:T(8,128)(2,1)}, bf16[...) async-done(((bf16[2,128,256]{2,1,0:T(8,128)(2,1)}, bf16[2,512,256]{2,1,0:T(8,128)(2,1)}, bf16[2,256,3,128]{3,1,2,0:T(8,128)(2,1)}, ...) | async-done | bytes 1966096 | tf_op jit(solution)/shard_map/psum | solution.py:280
  753.4 54.9 %scatter_custom_fusion.2 = f32[4096,128]{1,0:T(8,128)S(1)} fusion(s32[8192]{0:T(1024)} %bitcast.212, bf16[8192,128]{1,0:T(8,128)(2,1)} %bitcast.207, f32[]{:T(128)} %constant.36.clone.1), kind=kCustom, calls=%fused_computation.25 | custom fusion | flops 2097152 | bytes 4194816 | tf_op jit(solution)/shard_map/scatter-add | solution.py:277
  810.7 39.5 %psum.109 = f32[]{:T(128)} all-reduce(f32[]{:T(128)S(6)} %add.225), channel_id=1, replica_groups=mesh['dp'=8,'mp'=4] {'dp','mp'}, use_global_device_ids=true, to_apply=%region_41.42 | all-reduce | flops 1 | bytes 8 | tf_op jit(solution)/shard_map/psum | solution.py:299
  851.0 4.1 multiply_add_fusion.3
  (284 shorter events, 147.5 us)
Async XLA Ops:
  29.5 10.0 %all-to-all-start = ((s32[8,1,1024]{2,1,0:T(1,128)}), s32[8,1,1024]{2,1,0:T(1,128)S(1)}, u32[]{:S(2)}, u32[]{:S(2)}) async-start(s32[8,1,1024]{2,1,0:T(1,128)} %bitcast.3), calls=%async_computation | async-start | bytes 65536 | tf_op jit(solution)/shard_map/all_to_all | solution.py:134
  69.6 30.3 %all-to-all-start.1 = ((bf16[8,1024,128]{2,1,0:T(8,128)(2,1)}), bf16[8,1024,128]{2,1,0:T(8,128)(2,1)S(1)}, u32[]{:S(2)}, u32[]{:S(2)}) async-start(bf16[8,1024,128]{2,1,0:T(8,128)(2,1)} %bitcast.206), calls=%async_computation.1 | async-start | bytes 4194304 | tf_op jit(solution)/shard_map/all_to_all | solution.py:130
  73.4 240.2 %all-reduce.8.cloned.1.call-start = ((), (), s32[]{:S(2)}) async-start(), calls=%async_computation.4 | async-start | bytes 8388608 | tf_op jit(solution)/shard_map/psum | solution.py:94
  74.0 239.5 %copy-start.44 = (f32[64,2,32]{2,0,1:T(8,128)}, f32[64,2,32]{2,0,1:T(8,128)S(1)}, u32[]{:S(2)}) copy-start(f32[64,2,32]{2,0,1:T(8,128)S(1)} %get-tuple-element.67) | copy-start | bytes 49156
  99.9 12.1 %copy-start.26 = (f32[2,128,256]{2,1,0:T(8,128)S(1)}, f32[2,128,256]{2,1,0:T(8,128)}, u32[]{:S(2)}) copy-start(f32[2,128,256]{2,1,0:T(8,128)} %param.39) | copy-start | bytes 786436
  129.1 16.4 %copy-start.13 = (bf16[64,2,32,1,2,64]{5,4,2,3,0,1:T(2,128)(2,1)}, bf16[64,2,32,1,2,64]{5,4,2,3,0,1:T(2,128)(2,1)S(1)}, u32[]{:S(2)}) copy-start(bf16[64,2,32,1,2,64]{5,4,2,3,0,1:T(2,128)(2,1)S(1)} %get-tuple-element.64) | copy-start | bytes 3145732
  159.0 195.4 %all-reduce.10.cloned.1.call-start = ((), (), s32[]{:S(2)}) async-start(), calls=%async_computation.5 | async-start | bytes 524288 | tf_op jit(solution)/shard_map/psum | solution.py:97
  159.0 158.6 %copy-start.75 = (f32[64,2]{0,1:T(2,128)}, f32[64,2]{0,1:T(2,128)S(1)}, u32[]{:S(2)}) copy-start(f32[64,2]{0,1:T(2,128)S(1)} %convert_element_type.224) | copy-start | bytes 1540
  313.5 5.5 copy-start.7
  319.9 84.6 %reduce-scatter.2.cloned.1.call-start = ((), (), s32[]{:S(2)}) async-start(), calls=%async_computation.6 | async-start | bytes 589824 | tf_op jit(solution)/shard_map/reduce_scatter | solution.py:200
  356.1 11.6 %copy-start.78 = (f32[64,2]{0,1:T(2,128)}, f32[64,2]{0,1:T(2,128)S(1)}, u32[]{:S(2)}) copy-start(f32[64,2]{0,1:T(2,128)S(1)} %get-tuple-element.73) | copy-start | bytes 1540
  404.5 5.0 copy-start.31
  404.5 6.3 copy-start.19
  407.9 27.0 %copy-start.45 = (f32[64,2,32]{2,0,1:T(8,128)S(1)}, f32[64,2,32]{2,0,1:T(8,128)}, u32[]{:S(2)}) copy-start(f32[64,2,32]{2,0,1:T(8,128)} %copy-done.44) | copy-start | bytes 49156
  442.6 4.8 copy-start.12
  442.6 5.4 copy-start.14
  442.6 5.4 copy-start.52
  459.4 5.1 copy-start.9
  468.2 4.9 copy-start.8
  656.5 95.6 %all-to-all-start.2 = ((bf16[8,1024,128]{2,1,0:T(8,128)(2,1)}), bf16[8,1024,128]{2,1,0:T(8,128)(2,1)S(1)}, u32[]{:S(2)}, u32[]{:S(2)}) async-start(bf16[8,1024,128]{2,1,0:T(8,128)(2,1)} %bitcast.50), calls=%async_computation.3 | async-start | bytes 4194304 | tf_op jit(solution)/shard_map/all_to_all | solution.py:267
  660.1 76.9 %all-reduce.12.cloned.1.call-start = ((), (), s32[]{:S(2)}) async-start(), calls=%async_computation.7 | async-start | bytes 3932160 | tf_op jit(solution)/shard_map/psum | solution.py:280
  660.2 4.4 copy-start.54
  660.2 4.4 copy-start.69
  660.2 4.4 copy-start.76
  (73 other events, 175.3 us)
Sparse Core Ops, SparseCore 0:
  159.1 154.3 all-reduce.7
  320.1 34.3 all-reduce.9
  371.5 32.9 reduce-scatter.1
  666.4 70.6 all-reduce.11
where the time goes:
time: 880 us; the launch traced here: 876 us
  waiting for transfers between devices  280 us (32%)
  blocking collectives  246 us (28%)
  local copies, waits for them, and re-layouts  139 us (16%)
  other arithmetic  128 us (15%)
  matrix products  45.7 us (5%)
  between operations  23.9 us (3%)
  starting transfers between devices  13.4 us (2%)
    psum x1, waiting for transfers between devices, sum_heads(): return lax.psum(value, 'mp')  154 us
    psum x1, blocking collectives, shards(): lax.psum(contract('btscf,tdcf->btsd', dqkv, low_qkv), 'mp')  140 us
    scatter-add x1, other arithmetic, shards(): table_grad = jnp.zeros_like(embedding).at[jnp.maximum(served, 0).reshape(...  54.9 us
    dot_general x27, matrix products, contract(): return jnp.einsum(spec, left, right, preferred_element_type=jnp.float32)  45.7 us
    psum x1, blocking collectives, shards(): norm = jnp.sqrt(lax.psum(local_sq, ('dp', 'mp')))  39.5 us
    psum x1, blocking collectives, shards(): lax.psum(loss_part.astype(jnp.bfloat16), 'dp').astype(jnp.float32)  35.5 us
    psum x1, waiting for transfers between devices, shards(): lax.psum(d_in.astype(jnp.bfloat16), 'dp').astype(jnp.float32)  34.6 us
    psum x1, waiting for transfers between devices, sum_units(): return lax.psum(value, 'mp')  32.5 us
  transfers between devices with their start and end apart: 7, of which 6 were waited for; matrix products, arithmetic and copies ran while one was open for 3% of the time, Pallas kernels for 0%

commit v1 on v0

v1 whole, which is shorter than its diff:
```python
import functools

import jax
import jax.numpy as jnp
from jax import lax
from jax.experimental import pallas as pl
from jax.experimental.pallas import tpu as pltpu
from jax.sharding import PartitionSpec as P

DH = 64
EPS = 1e-06
INV_TEMP = 20.0
CLIP_NORM = 0.1
ROW_RATE = 150000.0
GAIN_RATE = 8000.0
MATRIX_RATE = 600.0
MOMENTUM = 0.9
AVERAGE_DECAY = 0.6

MESH = pl.DeviceIdType.MESH
LANES = 128
F32 = jnp.float32
BF16 = jnp.bfloat16
I32 = jnp.int32
VMEM = pl.BlockSpec(memory_space=pltpu.VMEM)
SMEM = pl.BlockSpec(memory_space=pltpu.SMEM)
DMA = pltpu.SemaphoreType.DMA


def nn(a, b):
    return lax.dot_general(a, b, (((1,), (0,)), ((), ())), preferred_element_type=F32)


def nt(a, b):
    return lax.dot_general(a, b, (((1,), (1,)), ((), ())), preferred_element_type=F32)


def tn(a, b):
    return lax.dot_general(a, b, (((0,), (0,)), ((), ())), preferred_element_type=F32)


def iota(shape, dim):
    return lax.broadcasted_iota(I32, shape, dim)


def split(value):
    high = value.astype(BF16)
    return high, (value - high.astype(F32)).astype(BF16)


def shape(dims, dtype):
    return jax.ShapeDtypeStruct(tuple(dims), dtype)


def params(limit, **more):
    return pltpu.CompilerParams(vmem_limit_bytes=limit << 20, **more)


def lists_of(owner, row, owners, capacity):
    chunks = owner.shape[0]
    width = owners * capacity
    his = width // LANES
    sub = iota((owners, LANES), 0)
    hot = [(owner[c : c + 1, :] == sub).astype(BF16) for c in range(chunks)]
    hots = jnp.concatenate([h.astype(F32) for h in hot], 0).astype(BF16)
    before = (iota((LANES, LANES), 0) < iota((LANES, LANES), 1)).astype(BF16)
    earlier = nn(hots, before)
    totals = nn(hots, jnp.ones((LANES, LANES), BF16))
    base = (sub * capacity).astype(F32)
    places = []
    for c in range(chunks):
        cut = slice(c * owners, (c + 1) * owners)
        at = hots[cut].astype(F32) * (earlier[cut] + base)
        here = jnp.sum(at, 0, keepdims=True).astype(I32)
        places.append(jnp.where(owner[c : c + 1, :] < owners, here, width))
        base = base + totals[cut]
    acc = jnp.zeros((his, 4 * LANES), F32)
    for c in range(chunks):
        place = places[c]
        value = row[c : c + 1, :]
        token = iota((1, LANES), 1) + c * LANES
        left = (lax.shift_right_logical(place, 7) == iota((his, LANES), 0)).astype(BF16)
        low = (place & 127) == iota((LANES, LANES), 0)
        parts = [lax.shift_right_logical(value, 6), value & 63, lax.shift_right_logical(token, 6), token & 63]
        right = jnp.concatenate([jnp.where(low, part.astype(F32), 0.0) for part in parts], 0)
        acc = acc + nt(left, right.astype(BF16))
    cuts = [acc[:, k * LANES : (k + 1) * LANES].astype(I32) for k in range(4)]
    return places, cuts[0] * 64 + cuts[1], cuts[2] * 64 + cuts[3]


def prep_kernel(owners, capacity, owner, row, own_owner, own_row, lists, inverse, own_place):
    per = capacity // LANES
    _, rows, tokens = lists_of(owner[...], row[...] + 1, owners, capacity)
    places, own_rows, _ = lists_of(own_owner[...], own_row[...], owners, capacity)
    rows = rows - 1
    inverse[...] = tokens
    for d in range(owners):
        lists[d, 0:per, :] = rows[d * per : (d + 1) * per, :]
        lists[d, per : 2 * per, :] = own_rows[d * per : (d + 1) * per, :]
    for c, place in enumerate(places):
        own_place[c : c + 1, :] = jnp.where(place < owners * capacity, place, 0)


def enter(plane, line):
    me, part = lax.axis_index("dp"), lax.axis_index("mp")
    barrier = pltpu.get_barrier_semaphore()
    for k in range(1, plane):
        pl.semaphore_signal(barrier, inc=1, device_id=(lax.rem(me + k, plane), part), device_id_type=MESH)
    for k in range(1, line):
        pl.semaphore_signal(barrier, inc=1, device_id=(me, lax.rem(part + k, line)), device_id_type=MESH)
    pl.semaphore_wait(barrier, max(plane - 1, 0) + max(line - 1, 0))
    return me, part


def send(source, target, out_sem, in_sem, device):
    copy = pltpu.make_async_remote_copy(
        src_ref=source, dst_ref=target, send_sem=out_sem, recv_sem=in_sem, device_id=device, device_id_type=MESH
    )
    copy.start()
    return copy


def asks_kernel(plane, lists, extra, got_lists, got_extra, out_sems, in_sems, own_sems):
    me, part = enter(plane, 0)
    copies = []
    for k in range(1, plane):
        peer = lax.rem(me + k, plane)
        copies.append(send(lists.at[peer], got_lists.at[me], out_sems.at[0, k], in_sems.at[0, k], (peer, part)))
        copies.append(send(extra, got_extra.at[me], out_sems.at[1, k], in_sems.at[1, k], (peer, part)))
    mine = [
        pltpu.make_async_copy(lists.at[me], got_lists.at[me], own_sems.at[0]),
        pltpu.make_async_copy(extra, got_extra.at[me], own_sems.at[1]),
    ]
    for copy in mine:
        copy.start()
    for copy in mine + copies:
        copy.wait()


def gather_rows(capacity, ids, table, target):
    def body(i, carry):
        at = pl.multiple_of(i * 16, 16)
        rows = [table[pl.ds(ids(at + u), 1), :] for u in range(16)]
        target[pl.ds(at, 16), :] = jnp.concatenate(rows, 0).astype(BF16)
        return carry

    lax.fori_loop(0, capacity // 16, body, 0)


def fetch_kernel(plane, capacity, ids, place, table, out, sent, got, wide, out_sems, in_sems):
    me, part = enter(plane, 0)
    copies = []
    for k in range(1, plane):
        peer = lax.rem(me + k, plane)
        gather_rows(capacity, lambda j, peer=peer: ids[peer, j], table, sent.at[peer])
        copies.append(send(sent.at[peer], got.at[me], out_sems.at[k], in_sems.at[k], (peer, part)))
    gather_rows(capacity, lambda j: ids[me, j], table, sent.at[me])
    wide[pl.ds(pl.multiple_of(me * capacity, capacity), capacity), :] = sent[me].astype(F32)
    for k in range(1, plane):
        peer = lax.rem(me - k + plane, plane)
        copies[k - 1].wait_recv()
        wide[pl.ds(pl.multiple_of(peer * capacity, capacity), capacity), :] = got[peer].astype(F32)
    gather_rows(out.shape[0], lambda j: place[j], wide, out)
    for copy in copies:
        copy.wait_send()


def slots_kernel(line, mine, out, out_sems, in_sems, own_sem):
    me, part = enter(0, line)
    copies = []
    for k in range(1, line):
        peer = lax.rem(part + k, line)
        copies.append(send(mine, out.at[part], out_sems.at[k], in_sems.at[k], (me, peer)))
    own = pltpu.make_async_copy(mine, out.at[part], own_sem)
    own.start()
    own.wait()
    for copy in copies:
        copy.wait()


def return_kernel(plane, capacity, tokens, rows, out, wide, sent, out_sems, in_sems, own_sem):
    me, part = enter(plane, 0)
    wide[...] = rows[...].astype(F32)
    copies = []
    for k in range(1, plane):
        peer = lax.rem(me + k, plane)
        gather_rows(capacity, lambda j, peer=peer: tokens[peer, j], wide, sent.at[peer])
        copies.append(send(sent.at[peer], out.at[me], out_sems.at[k], in_sems.at[k], (peer, part)))
    gather_rows(capacity, lambda j: tokens[me, j], wide, sent.at[me])
    own = pltpu.make_async_copy(sent.at[me], out.at[me], own_sem)
    own.start()
    own.wait()
    for copy in copies:
        copy.wait()


def scatter_kernel(capacity, ids, counts, rows, out, square, wide):
    out[...] = jnp.zeros_like(out)
    for d in range(rows.shape[0]):
        wide[...] = rows[d].astype(F32)
        count = counts[d]

        def one(j):
            at = ids[d, j]
            out[pl.ds(at, 1), :] = out[pl.ds(at, 1), :] + wide[pl.ds(j, 1), :]

        def body(i, carry):
            for u in range(8):
                one(i * 8 + u)
            return carry

        def rest(j, carry):
            one(j)
            return carry

        full = lax.shift_right_logical(count, 3)
        lax.fori_loop(0, full, body, 0)
        lax.fori_loop(full * 8, count, rest, 0)

    def add(i, total):
        block = out[pl.ds(pl.multiple_of(i * 64, 64), 64), :]
        block = block * block
        for r in range(8):
            total = total + block[r * 8 : (r + 1) * 8, :]
        return total

    square[...] = lax.fori_loop(0, out.shape[0] // 64, add, jnp.zeros((8, LANES), F32))


def norm_kernel(plane, line, table_sq, dense_sq, got_table, got_dense, out_sems, in_sems, own_sems):
    me, part = enter(plane, line)
    copies = []
    for k in range(1, plane):
        peer = lax.rem(me + k, plane)
        copies.append(send(table_sq, got_table.at[me], out_sems.at[0, k], in_sems.at[0, k], (peer, part)))
    for k in range(1, line):
        peer = lax.rem(part + k, line)
        copies.append(send(dense_sq, got_dense.at[part], out_sems.at[1, k], in_sems.at[1, k], (me, peer)))
    mine = [
        pltpu.make_async_copy(table_sq, got_table.at[me], own_sems.at[0]),
        pltpu.make_async_copy(dense_sq, got_dense.at[part], own_sems.at[1]),
    ]
    for copy in mine:
        copy.start()
    for copy in mine + copies:
        copy.wait()


def chain(index, values):
    out = jnp.full(index.shape, values[0], values[0].dtype)
    for k in range(1, len(values)):
        out = jnp.where(index >= k, values[k], out)
    return out


def forward_kernel(slots, cnt, x, w_in, gain, w_qkv, w_out, pooled, pm_out, normed_out, qkv, prob, a_out, pm_acc):
    tower = pl.program_id(0)
    pairs = pooled.shape[1]
    parts = w_qkv.shape[0]
    per = LANES // slots
    groups = pairs // per
    heads = 2 * parts
    xs = x[0]
    hidden = nn(xs, w_in[0].astype(BF16))
    inverse = lax.rsqrt(jnp.mean(hidden * hidden, -1, keepdims=True) + EPS)
    normed = (hidden * inverse * gain[0]).astype(BF16)
    normed_out[0] = normed
    for c in range(3):
        for m in range(parts):
            qkv[0, c * parts + m] = nn(normed, w_qkv[m, 0, c]).astype(BF16)
    lane = iota((LANES, LANES), 1)
    line = iota((LANES, LANES), 0)
    shift = slots.bit_length() - 1
    pair_r, pair_s = lax.shift_right_logical(lane, shift), lax.shift_right_logical(line, shift)
    same = pair_r == pair_s
    halves = [lane < DH, lane >= DH]
    own_head = iota((per * heads, LANES), 0) & (heads - 1)

    def group(g, carry):
        counts = [cnt[tower * pairs + g * per + k] for k in range(per)]
        live_r = same & ((lane & (slots - 1)) < chain(pair_r, counts))
        live_s = (line & (slots - 1)) < chain(pair_s, counts)
        rows = pl.ds(pl.multiple_of(g * LANES, LANES), LANES)
        sums = []
        for m in range(parts):
            query, key = qkv[0, m, rows, :], qkv[0, parts + m, rows, :]
            for half in range(2):
                scores = nt(jnp.where(halves[half], query, jnp.zeros_like(query)), key) * 0.125
                scores = jnp.where(live_r, scores, -1000000000.0)
                expo = jnp.exp(scores - jnp.max(scores, 1, keepdims=True))
                p = (expo * (1.0 / jnp.sum(expo, 1, keepdims=True))).astype(BF16)
                prob[0, g, 2 * m + half] = p
                sums.append(jnp.sum(jnp.where(live_s, p.astype(F32), 0.0), 0, keepdims=True))
        sums = jnp.concatenate(sums, 0)
        pair_l = lax.shift_right_logical(iota((heads, LANES), 1), shift)
        stack = jnp.concatenate([jnp.where(pair_l == k, sums, 0.0) for k in range(per)], 0).astype(BF16)
        a_out[0, g] = stack
        for m in range(parts):
            mix = nn(stack, qkv[0, 2 * parts + m, rows, :])
            head = iota((per * heads, LANES), 1) // DH + 2 * m
            mix = jnp.where(own_head == head, mix, 0.0)
            pm_acc[g, :, m * LANES : (m + 1) * LANES] = jnp.concatenate(
                [jnp.sum(mix[k * heads : (k + 1) * heads], 0, keepdims=True) for k in range(per)], 0
            )
        return carry

    lax.fori_loop(0, groups, group, 0)
    pm = jnp.concatenate([pm_acc[g] for g in range(groups)], 0).astype(BF16)
    pm_out[0] = pm
    every = [cnt[tower * pairs + k] for k in range(pairs)]
    tokens = iota((pairs, pairs * slots), 1)
    mine = lax.shift_right_logical(tokens, shift) == iota(tokens.shape, 0)
    live = mine & ((tokens & (slots - 1)) < chain(iota(tokens.shape, 0), every))
    high, low = split(nn(live.astype(BF16), xs))
    w = w_in[0].astype(BF16)
    total = nn(high, w) + nn(low, w)
    for m in range(parts):
        total = total + nn(pm[:, m * LANES : (m + 1) * LANES], w_out[m, 0])
    count = chain(iota(total.shape, 0), every).astype(F32)
    pooled[0] = (total / count).astype(BF16)


def backward_kernel(
    slots, cnt, x, w_in, gain, w_qkv, w_out, normed_in, qkv, prob, a_in, pm_in, dpooled, demb, d_in, d_gain, d_qkv, d_out, dqkv
):
    tower = pl.program_id(0)
    pairs, width = dpooled.shape[1:]
    parts = w_qkv.shape[0]
    per = LANES // slots
    groups = pairs // per
    heads = 2 * parts
    shift = slots.bit_length() - 1
    tokens = pairs * slots
    every = [cnt[tower * pairs + k] for k in range(pairs)]
    count = chain(iota((pairs, width), 0), every).astype(F32)
    dsum = dpooled[0].astype(F32) / count
    branch = dsum.astype(BF16)
    dmix = []
    for m in range(parts):
        d_out[0, m] = tn(pm_in[0, :, m * LANES : (m + 1) * LANES], branch).astype(BF16)
        dmix.append(nt(branch, w_out[m, 0]))
    lane = iota((LANES, LANES), 1)
    line = iota((LANES, LANES), 0)
    pair_s = lax.shift_right_logical(line, shift)
    halves = [lane < DH, lane >= DH]
    own_head = iota((per * heads, LANES), 0) & (heads - 1)
    own_pair = lax.shift_right_logical(iota((per * heads, LANES), 0), heads.bit_length() - 1)
    token_pair = lax.shift_right_logical(iota((per * heads, LANES), 1), shift)
    for g in range(groups):
        rows = slice(g * LANES, (g + 1) * LANES)
        live_s = (line & (slots - 1)) < chain(pair_s, every[g * per : (g + 1) * per])
        scale = jnp.where(live_s, 0.125, 0.0)
        dots = jnp.zeros((per * heads, LANES), F32)
        stacks = []
        for m in range(parts):
            cut = dmix[m][g * per : (g + 1) * per]
            spread = jnp.concatenate([jnp.broadcast_to(cut[k : k + 1], (heads, LANES)) for k in range(per)], 0)
            head = iota((per * heads, LANES), 1) // DH + 2 * m
            stack = jnp.where(own_head == head, spread, 0.0).astype(BF16)
            stacks.append(stack)
            dots = dots + nt(stack, qkv[0, 2 * parts + m, rows, :])
        dots = jnp.where(own_pair == token_pair, dots, 0.0)
        pull = dots[0:heads]
        for k in range(1, per):
            pull = pull + dots[k * heads : (k + 1) * heads]
        for m in range(parts):
            query, key = qkv[0, m, rows, :], qkv[0, parts + m, rows, :]
            none = jnp.zeros_like(query)
            dq = jnp.zeros((LANES, LANES), F32)
            dk = jnp.zeros((LANES, LANES), F32)
            for half in range(2):
                h = 2 * m + half
                p = prob[0, g, h].astype(F32)
                t = p * pull[h : h + 1, :]
                ds = ((t - p * jnp.sum(t, 1, keepdims=True)) * scale).astype(BF16)
                dq = dq + nn(ds, jnp.where(halves[half], key, none))
                dk = dk + tn(ds, jnp.where(halves[half], query, none))
            dqkv[m, rows, :] = dq.astype(BF16)
            dqkv[parts + m, rows, :] = dk.astype(BF16)
            dqkv[2 * parts + m, rows, :] = tn(a_in[0, g], stacks[m]).astype(BF16)
    normed = normed_in[0]
    dnormed = jnp.zeros((tokens, width), F32)
    for m in range(parts):
        for c in range(3):
            grad = dqkv[c * parts + m]
            dnormed = dnormed + nt(grad, w_qkv[m, 0, c])
            d_qkv[0, m, c] = tn(normed, grad).astype(BF16)
    dnormed = dnormed.astype(BF16).astype(F32)
    xs = x[0]
    w = w_in[0].astype(BF16)
    hidden = nn(xs, w)
    inverse = lax.rsqrt(jnp.mean(hidden * hidden, -1, keepdims=True) + EPS)
    unit = hidden * inverse
    d_gain[0] = jnp.sum(dnormed * unit, 0, keepdims=True)
    scaled = dnormed * gain[0]
    dh = inverse * (scaled - unit * jnp.mean(scaled * unit, -1, keepdims=True))
    spread = jnp.broadcast_to(dsum[:, None, :], (pairs, slots, width))
    slot = iota((pairs, slots, width), 1)
    counts = chain(iota((pairs, slots, width), 0), every)
    spread = jnp.where(slot < counts, spread, 0.0).reshape(tokens, width)
    dhidden = (spread + dh).astype(BF16)
    d_in[0] = tn(xs, dhidden).astype(BF16)
    demb[0] = nt(dhidden, w).astype(BF16)


def gelu_parts(v):
    c = 0.7978845608028654
    inner = jnp.tanh(c * (v + 0.044715 * (v * v * v)))
    value = 0.5 * v * (1.0 + inner)
    slope = 0.5 * (1.0 + inner) + 0.5 * v * (1.0 - inner * inner) * (c * (1.0 + 3.0 * 0.044715 * (v * v)))
    return value, slope


def upper_kernel(
    plane,
    line,
    pooled,
    w_one,
    w_two,
    w_three,
    prior_row,
    prior_col,
    pos_row,
    pos_own,
    dpooled,
    d_one,
    d_two,
    d_three,
    loss,
    pooled_all,
    second_send,
    second_got,
    vec,
    dsec_send,
    dsec_all,
    dpool_send,
    dpool_got,
    out_sems,
    in_sems,
    vec_out,
    vec_in,
):
    me, part = enter(plane, line)
    towers, own, width = pooled.shape
    rows = own * line
    pairs = rows * plane
    peers = [lax.rem(part + k, line) for k in range(1, line)]

    pooled_all[:, part] = pooled[...]
    first = [
        send(pooled_all.at[:, part], pooled_all.at[:, part], out_sems.at[0, k], in_sems.at[0, k], (me, peers[k]))
        for k in range(line - 1)
    ]
    one = [w_one[t].astype(BF16) for t in range(towers)]
    two = [w_two[t].astype(BF16) for t in range(towers)]
    three = [w_three[t].astype(BF16) for t in range(towers)]
    for copy in first:
        copy.wait()
    act_one, slope_one, pools = [], [], []
    for t in range(towers):
        pools.append(pooled_all[t].reshape(rows, width))
        value, slope = gelu_parts(nn(pools[t], one[t]))
        act_one.append(value.astype(BF16))
        slope_one.append(slope)
        second_send[t] = nn(act_one[t], two[t]).reshape(line, own, -1)
    second = [
        send(
            second_send.at[:, peers[k]], second_got.at[:, part], out_sems.at[1, k], in_sems.at[1, k], (me, peers[k])
        )
        for k in range(line - 1)
    ]
    for copy in second:
        copy.wait()
    act_two, slope_two, third, length, vectors = [], [], [], [], []
    for t in range(towers):
        total = second_send[t, part]
        for peer in peers:
            total = total + second_got[t, peer]
        value, slope = gelu_parts(total)
        act_two.append(value.astype(BF16))
        slope_two.append(slope)
        third.append(nn(act_two[t], three[t]))
        length.append(lax.rsqrt(jnp.sum(third[t] * third[t], -1, keepdims=True) + EPS))
        vectors.append((third[t] * length[t]).astype(BF16))
        vec[t, me, part] = vectors[t]
    along = [
        send(vec.at[:, me, part], vec.at[:, me, part], out_sems.at[2, k], in_sems.at[2, k], (me, peers[k]))
        for k in range(line - 1)
    ]
    for copy in along:
        copy.wait()
    across = [
        send(vec.at[:, me], vec.at[:, me], vec_out.at[k], vec_in.at[k], (lax.rem(me + k, plane), part))
        for k in range(1, plane)
    ]
    for copy in across:
        copy.wait()

    queries = vec[0].reshape(pairs, width)
    items = vec[1].reshape(pairs, width)
    logits = INV_TEMP * nt(items, queries) - prior_col[...]
    peak = jnp.max(logits, 0, keepdims=True)
    log_total = peak + jnp.log(jnp.sum(jnp.exp(logits - peak), 0, keepdims=True))
    picked = jnp.where(iota((pairs, pairs), 0) == pos_row[...], logits, 0.0)
    gap = log_total - jnp.sum(picked, 0, keepdims=True)
    loss[...] = jnp.broadcast_to(jnp.sum(gap, 1, keepdims=True), loss.shape)
    ahead = me * rows + part * own
    mine = INV_TEMP * nt(vectors[0], items) - prior_row[...]
    top = jnp.max(mine, 1, keepdims=True)
    expo = jnp.exp(mine - top)
    chance = expo / jnp.sum(expo, 1, keepdims=True)
    target = (iota(mine.shape, 1) == pos_own[...]).astype(F32)
    dlog = ((chance - target) / pairs).astype(BF16)
    dvec = [(INV_TEMP * nn(dlog, items)).astype(BF16)]
    own_prior = prior_col[pl.ds(pl.multiple_of(ahead, own), own), :]
    theirs = INV_TEMP * nt(vectors[1], queries) - own_prior
    target = (iota(theirs.shape, 0) + ahead == pos_row[...]).astype(F32)
    dlog = ((jnp.exp(theirs - log_total) - target) / pairs).astype(BF16)
    dvec.append((INV_TEMP * nn(dlog, queries)).astype(BF16))

    dthirds = []
    for t in range(towers):
        dv = dvec[t].astype(F32)
        inner = jnp.sum(dv * third[t], -1, keepdims=True)
        dthird = (length[t] * dv - third[t] * (length[t] * length[t] * length[t] * inner)).astype(BF16)
        dact = nt(dthird, three[t]).astype(BF16).astype(F32)
        dsec_all[t, part] = (dact * slope_two[t]).astype(BF16)
        dthirds.append(dthird)
    spread = [
        send(dsec_all.at[:, part], dsec_all.at[:, part], out_sems.at[3, k], in_sems.at[3, k], (me, peers[k]))
        for k in range(line - 1)
    ]
    for t in range(towers):
        d_three[t] = tn(act_two[t], dthirds[t]).astype(BF16)
    for copy in spread:
        copy.wait()
    dfirsts = []
    for t in range(towers):
        dsecond = dsec_all[t].reshape(rows, -1)
        dact = nt(dsecond, two[t]).astype(BF16).astype(F32)
        dfirst = (dact * slope_one[t]).astype(BF16)
        dpool_send[t] = nt(dfirst, one[t]).reshape(line, own, width)
        dfirsts.append(dfirst)
    back = [
        send(dpool_send.at[:, peers[k]], dpool_got.at[:, part], out_sems.at[4, k], in_sems.at[4, k], (me, peers[k]))
        for k in range(line - 1)
    ]
    for t in range(towers):
        dsecond = dsec_all[t].reshape(rows, -1)
        d_two[t] = tn(act_one[t], dsecond).astype(BF16)
        d_one[t] = tn(pools[t], dfirsts[t]).astype(BF16)
    for copy in back:
        copy.wait()
    for t in range(towers):
        total = dpool_send[t, part]
        for peer in peers:
            total = total + dpool_got[t, peer]
        dpooled[t] = total.astype(BF16)


def update(weight, grad, moment, average, factor, rate):
    clipped = grad * factor
    moment_new = MOMENTUM * moment + clipped
    weight_new = weight - rate * (clipped + MOMENTUM * moment_new)
    average_new = AVERAGE_DECAY * average + (1.0 - AVERAGE_DECAY) * weight_new
    return [weight_new, moment_new, average_new]


def shards(
    slot_owner,
    slot_row,
    slot_count,
    item_qid,
    positive,
    log_prior,
    embedding,
    embedding_mom,
    embedding_avg,
    w_in,
    w_in_mom,
    w_in_avg,
    norm_gain,
    norm_gain_mom,
    norm_gain_avg,
    w_qkv,
    w_qkv_mom,
    w_qkv_avg,
    w_out,
    w_out_mom,
    w_out_avg,
    w_one,
    w_one_mom,
    w_one_avg,
    w_two,
    w_two_mom,
    w_two_avg,
    w_three,
    w_three_mom,
    w_three_avg,
):
    plane = lax.axis_size("dp")
    line = lax.axis_size("mp")
    batch, towers, slots = slot_row.shape
    own = batch // line
    requests = batch * towers * slots
    own_requests = requests // line
    tokens = own * slots
    capacity = max(LANES, 2 * requests // plane)
    pairs = batch * plane
    part = lax.axis_index("mp")
    me = lax.axis_index("dp")
    width = w_in.shape[2]
    depth = w_in.shape[1]
    units = w_one.shape[2]
    seconds = w_two.shape[2]

    wide_qkv = lax.all_gather(jnp.transpose(w_qkv.astype(BF16), (0, 2, 1, 3)), "mp", axis=0)
    wide_out = lax.all_gather(w_out.astype(BF16), "mp", axis=0)

    def ordered(value):
        value = value.reshape(line, own, towers, slots)
        return jnp.transpose(value, (0, 2, 1, 3)).reshape(requests // LANES, LANES)

    owner = ordered(slot_owner)
    row = ordered(slot_row)
    own_chunks = own_requests // LANES
    own_owner = lax.dynamic_slice_in_dim(owner, part * own_chunks, own_chunks, 0)
    own_row = lax.dynamic_slice_in_dim(row, part * own_chunks, own_chunks, 0)
    per = capacity // LANES
    lists, inverse, own_place = pl.pallas_call(
        functools.partial(prep_kernel, plane, capacity),
        out_shape=[
            shape((plane, 2 * per, LANES), I32),
            shape((plane * per, LANES), I32),
            shape((own_chunks, LANES), I32),
        ],
        in_specs=[VMEM] * 4,
        out_specs=[VMEM] * 3,
        compiler_params=params(32),
        name="request_lists",
    )(owner, row, own_owner, own_row)
    lone = jnp.pad(positive[None, :], ((0, 7), (0, LANES - batch)))
    got_lists, got_pos = pl.pallas_call(
        functools.partial(asks_kernel, plane),
        out_shape=[shape(lists.shape, I32), shape((plane, 8, LANES), I32)],
        in_specs=[VMEM] * 2,
        out_specs=[VMEM] * 2,
        scratch_shapes=[DMA((2, plane)), DMA((2, plane)), DMA((2,))],
        compiler_params=params(32, collective_id=1, has_side_effects=True),
        name="ask",
    )(lists, lone)
    ids = got_lists[:, per:, :].reshape(plane, capacity)
    embedded = pl.pallas_call(
        functools.partial(fetch_kernel, plane, capacity),
        out_shape=shape((own_requests, depth), BF16),
        in_specs=[SMEM, SMEM, VMEM],
        out_specs=VMEM,
        scratch_shapes=[
            pltpu.VMEM((plane, capacity, depth), BF16),
            pltpu.VMEM((plane, capacity, depth), BF16),
            pltpu.VMEM((plane * capacity, depth), F32),
            DMA((plane,)),
            DMA((plane,)),
        ],
        compiler_params=params(48, collective_id=2, has_side_effects=True),
        name="fetch",
    )(ids, own_place.reshape(own_requests), embedding)
    embedded = embedded.reshape(towers, tokens, depth)

    counts = jnp.transpose(slot_count).reshape(towers, line, own)
    counts = lax.dynamic_index_in_dim(counts, part, 1, keepdims=False).reshape(towers * own)
    heads = 2 * line
    gains = norm_gain.reshape(towers, 1, width)
    groups = tokens // LANES
    per_group = LANES // slots
    lead = lambda *dims: pl.BlockSpec((1,) + dims, lambda t: (t,) + (0,) * len(dims))
    qkv_spec = pl.BlockSpec((line, 1, 3, width, LANES), lambda t: (0, t, 0, 0, 0))
    out_spec = pl.BlockSpec((line, 1, LANES, width), lambda t: (0, t, 0, 0))
    pooled, pm, normed, qkv, prob, spread = pl.pallas_call(
        functools.partial(forward_kernel, slots),
        grid=(towers,),
        out_shape=[
            shape((towers, own, width), BF16),
            shape((towers, own, line * LANES), BF16),
            shape((towers, tokens, width), BF16),
            shape((towers, 3 * line, tokens, LANES), BF16),
            shape((towers, groups, heads, LANES, LANES), BF16),
            shape((towers, groups, per_group * heads, LANES), BF16),
        ],
        in_specs=[SMEM, lead(tokens, depth), lead(depth, width), lead(1, width), qkv_spec, out_spec],
        out_specs=[
            lead(own, width),
            lead(own, line * LANES),
            lead(tokens, width),
            lead(3 * line, tokens, LANES),
            lead(groups, heads, LANES, LANES),
            lead(groups, per_group * heads, LANES),
        ],
        scratch_shapes=[pltpu.VMEM((groups, per_group, line * LANES), F32)],
        compiler_params=params(48),
        name="attention_forward",
    )(counts, embedded, w_in, gains, wide_qkv, wide_out)

    prior = jnp.sum(
        jnp.where(item_qid[:, None] == jnp.arange(log_prior.shape[0])[None, :], log_prior[None, :], 0.0), 1
    )
    positions = got_pos[:, 0, :batch].reshape(1, pairs)
    own_positions = lax.dynamic_slice_in_dim(positive, part * own, own, 0).reshape(own, 1)
    dpooled, d_one, d_two, d_three, loss = pl.pallas_call(
        functools.partial(upper_kernel, plane, line),
        out_shape=[
            shape((towers, own, width), BF16),
            shape((towers, width, units), BF16),
            shape((towers, units, seconds), BF16),
            shape((towers, seconds, width), BF16),
            shape((8, LANES), F32),
        ],
        in_specs=[VMEM] * 8,
        out_specs=[VMEM] * 5,
        scratch_shapes=[
            pltpu.VMEM((towers, line, own, width), BF16),
            pltpu.VMEM((towers, line, own, seconds), F32),
            pltpu.VMEM((towers, line, own, seconds), F32),
            pltpu.VMEM((towers, plane, line, own, width), BF16),
            pltpu.VMEM((towers, line, own, seconds), BF16),
            pltpu.VMEM((towers, line, own, seconds), BF16),
            pltpu.VMEM((towers, line, own, width), F32),
            pltpu.VMEM((towers, line, own, width), F32),
            DMA((5, line)),
            DMA((5, line)),
            DMA((plane,)),
            DMA((plane,)),
        ],
        compiler_params=params(56, collective_id=3, has_side_effects=True),
        name="upper",
    )(pooled, w_one, w_two, w_three, prior.reshape(1, pairs), prior.reshape(pairs, 1), positions, own_positions)

    demb, d_in, d_gain, d_qkv, d_out = pl.pallas_call(
        functools.partial(backward_kernel, slots),
        grid=(towers,),
        out_shape=[
            shape((towers, tokens, depth), BF16),
            shape((towers, depth, width), BF16),
            shape((towers, 1, width), F32),
            shape((towers, line, 3, width, LANES), BF16),
            shape((towers, line, LANES, width), BF16),
        ],
        in_specs=[
            SMEM,
            lead(tokens, depth),
            lead(depth, width),
            lead(1, width),
            qkv_spec,
            out_spec,
            lead(tokens, width),
            lead(3 * line, tokens, LANES),
            lead(groups, heads, LANES, LANES),
            lead(groups, per_group * heads, LANES),
            lead(own, line * LANES),
            lead(own, width),
        ],
        out_specs=[
            lead(tokens, depth),
            lead(depth, width),
            lead(1, width),
            lead(line, 3, width, LANES),
            lead(line, LANES, width),
        ],
        scratch_shapes=[pltpu.VMEM((3 * line, tokens, LANES), BF16)],
        compiler_params=params(56),
        name="attention_backward",
    )(counts, embedded, w_in, gains, wide_qkv, wide_out, normed, qkv, prob, spread, pm, dpooled)

    both = ("dp", "mp")
    d_one = lax.psum(d_one, "dp").astype(F32)
    d_two = lax.psum(d_two, "dp").astype(F32)
    d_three = lax.psum(d_three, both).astype(F32)
    d_in = lax.psum(d_in, both).astype(F32)
    d_gain = lax.psum(d_gain.reshape(towers, width).astype(BF16), both).astype(F32)
    d_qkv = lax.psum(lax.psum_scatter(d_qkv, "mp", scatter_dimension=1, tiled=False), "dp")
    d_qkv = jnp.transpose(d_qkv, (0, 2, 1, 3)).astype(F32)
    d_out = lax.psum(lax.psum_scatter(d_out, "mp", scatter_dimension=1, tiled=False), "dp").astype(F32)

    every = pl.pallas_call(
        functools.partial(slots_kernel, line),
        out_shape=shape((line, own_requests, depth), BF16),
        in_specs=[VMEM],
        out_specs=VMEM,
        scratch_shapes=[DMA((line,)), DMA((line,)), DMA],
        compiler_params=params(32, collective_id=4, has_side_effects=True),
        name="line_slots",
    )(demb.reshape(own_requests, depth))
    incoming = pl.pallas_call(
        functools.partial(return_kernel, plane, capacity),
        out_shape=shape((plane, capacity, depth), BF16),
        in_specs=[SMEM, VMEM],
        out_specs=VMEM,
        scratch_shapes=[
            pltpu.VMEM((requests, depth), F32),
            pltpu.VMEM((plane, capacity, depth), BF16),
            DMA((plane,)),
            DMA((plane,)),
            DMA,
        ],
        compiler_params=params(48, collective_id=5, has_side_effects=True),
        name="return_rows",
    )(inverse.reshape(plane, capacity), every.reshape(requests, depth))
    served = got_lists[:, :per, :].reshape(plane, capacity)
    table_grad, table_sq = pl.pallas_call(
        functools.partial(scatter_kernel, capacity),
        out_shape=[shape(embedding.shape, F32), shape((8, LANES), F32)],
        in_specs=[SMEM, SMEM, VMEM],
        out_specs=[VMEM, VMEM],
        scratch_shapes=[pltpu.VMEM((capacity, depth), F32)],
        compiler_params=params(48),
        name="add_rows",
    )(jnp.maximum(served, 0), jnp.sum((served >= 0).astype(I32), 1), incoming)

    whole_sq = jnp.sum(d_in * d_in) + jnp.sum(d_gain * d_gain) + jnp.sum(d_three * d_three)
    shard_sq = jnp.sum(d_qkv * d_qkv) + jnp.sum(d_out * d_out) + jnp.sum(d_one * d_one) + jnp.sum(d_two * d_two)
    got_table, got_dense = pl.pallas_call(
        functools.partial(norm_kernel, plane, line),
        out_shape=[shape((plane, 8, LANES), F32), shape((line, 8, LANES), F32)],
        in_specs=[VMEM] * 2,
        out_specs=[VMEM] * 2,
        scratch_shapes=[DMA((2, plane)), DMA((2, plane)), DMA((2,))],
        compiler_params=params(32, collective_id=6, has_side_effects=True),
        name="norm_parts",
    )(table_sq, jnp.broadcast_to(shard_sq, (8, LANES)))
    norm = jnp.sqrt(jnp.sum(got_table) + jnp.sum(got_dense[:, 0, 0]) + whole_sq)
    factor = jnp.minimum(1.0, CLIP_NORM / norm)
    done = []
    done.extend(update(embedding, table_grad, embedding_mom, embedding_avg, factor, ROW_RATE))
    done.extend(update(w_in, d_in, w_in_mom, w_in_avg, factor, MATRIX_RATE))
    done.extend(update(norm_gain, d_gain, norm_gain_mom, norm_gain_avg, factor, GAIN_RATE))
    done.extend(update(w_qkv, d_qkv, w_qkv_mom, w_qkv_avg, factor, MATRIX_RATE))
    done.extend(update(w_out, d_out, w_out_mom, w_out_avg, factor, MATRIX_RATE))
    done.extend(update(w_one, d_one, w_one_mom, w_one_avg, factor, MATRIX_RATE))
    done.extend(update(w_two, d_two, w_two_mom, w_two_avg, factor, MATRIX_RATE))
    done.extend(update(w_three, d_three, w_three_mom, w_three_avg, factor, MATRIX_RATE))
    return (loss[0, 0], norm, *done)


def solution(mesh):
    rows = P("dp", None)
    qkv = P(None, None, None, "mp")
    deep = P(None, "mp", None)
    wide = P(None, None, "mp")
    weights = (rows,) * 3 + (P(),) * 6 + (qkv,) * 3 + (deep,) * 3 + (wide,) * 3 + (deep,) * 3 + (P(),) * 3
    inputs = (P("dp", None, None, None), P("dp", None, None), P("dp", None), P(), P("dp"), P())
    return jax.shard_map(
        shards, mesh=mesh, in_specs=inputs + weights, out_specs=(P(), P()) + weights, check_vma=False
    )
```

time: 880 us -> 494 us (0.56)
  Pallas kernels: 0 us -> 181 us
  blocking collectives: 246 us -> 82.8 us
  waiting for transfers between devices: 280 us -> 154 us
  local copies, waits for them, and re-layouts: 139 us -> 22.7 us
  other arithmetic: 128 us -> 31.5 us
  matrix products: 45.7 us -> 0 us
  starting transfers between devices: 13.4 us -> 0.16 us
    pallas_call x0 -> x10, Pallas kernels: none -> 181 us  [the longest x1 41.7 us: shards(): pl.pallas_call(functools.partial(upper_kernel, plane, line), out_shape=[s...]
    psum x4 -> x1, blocking collectives: 237 us -> 66.2 us  [shards(): lax.psum(d_gain.reshape(towers, width).astype(BF16), both).astype(F32)]
    psum x3 -> x2, waiting for transfers between devices: 222 us -> 68.6 us  [the longest x1 56.4 us: shards(): lax.psum(lax.psum_scatter(d_qkv, 'mp', scatter_dimension=1, tiled=False),...]
    unnamed x4 -> x5, waiting for transfers between devices: 0.07 us -> 85.8 us
    scatter-add x1 -> x0, other arithmetic: 54.9 us -> none  [shards(): table_grad = jnp.zeros_like(embedding).at[jnp.maximum(served, 0).reshape(...]
    dot_general x27 -> x0, matrix products: 45.7 us -> none  [contract(): return jnp.einsum(spec, left, right, preferred_element_type=jnp.float32)]
    gather x2 -> x0, local copies, waits for them, and re-layouts: 41.6 us -> none  [the longest x1 29.5 us: serve(): found = table_low[jnp.maximum(asked, 0)]]
    reduce_scatter x1 -> x0, waiting for transfers between devices: 29.6 us -> none  [shards(): lax.psum_scatter(INV_TEMP * contract('bj,bd->jd', dlogits, vectors[:, 0])...]
  transfers between devices with their start and end apart: 7 -> 4, of which waited for: 6 -> 3; matrix products, arithmetic and copies ran while one was open for 3% -> 4% of each run, Pallas kernels for 0% -> 22%
where the time goes in v1:
time: 494 us
  Pallas kernels  181 us (37%)
  waiting for transfers between devices  154 us (31%)
  blocking collectives  82.8 us (17%)
  other arithmetic  31.5 us (6%)
  local copies, waits for them, and re-layouts  22.7 us (5%)
  between operations  21.4 us (4%)
    unnamed x5, waiting for transfers between devices  85.8 us
    psum x1, blocking collectives, shards(): lax.psum(d_gain.reshape(towers, width).astype(BF16), both).astype(F32)  66.2 us
    psum x1, waiting for transfers between devices, shards(): lax.psum(lax.psum_scatter(d_qkv, 'mp', scatter_dimension=1, tiled=False),...  56.4 us
    pallas_call x1, Pallas kernels, shards(): pl.pallas_call(functools.partial(upper_kernel, plane, line), out_shape=[s...  41.7 us
    pallas_call x1, Pallas kernels, shards(): pl.pallas_call(functools.partial(return_kernel, plane, capacity), out_sha...  31.9 us
    pallas_call x1, Pallas kernels, shards(): pl.pallas_call(functools.partial(fetch_kernel, plane, capacity), out_shap...  31.6 us
    pallas_call x1, Pallas kernels, shards(): pl.pallas_call(functools.partial(slots_kernel, line), out_shape=shape((li...  22.4 us
    all_gather x1, blocking collectives, shards(): wide_out = lax.all_gather(w_out.astype(BF16), 'mp', axis=0)  16.6 us
  transfers between devices with their start and end apart: 4, of which 3 were waited for; matrix products, arithmetic and copies ran while one was open for 4% of the time, Pallas kernels for 22%

profile of v1, /device:TPU:0, one launch (start us, length us, event | category | flops | bytes accessed | tf_op | source)
XLA Modules:
  0.0 493.6 jit_solution(11216561337176739833)
XLA Ops:
  7.3 2.1 convert_bitcast_fusion
  12.3 2.3 request_lists.1
  14.6 6.8 %ask.1 = (s32[8,16,128]{2,1,0:T(8,128)S(1)}, s32[8,8,128]{2,1,0:T(8,128)S(1)}) custom-call(s32[8,16,128]{2,1,0:T(8,128)S(1)} %get-tuple-element.51.lists, s32[8,128]{1,0:T(8,128)S(1)} %pad.4.extra), custom_call_target="tpu_custom_call" | custom-call | tf_op jit(solution)/shard_map/ask/pallas_call | solution.py:643
  25.9 31.6 %fetch.1 = bf16[1024,128]{1,0:T(8,128)(2,1)S(1)} custom-call(s32[8,1024]{1,0:T(8,128)S(1)} %bitcast.75, s32[1024]{0:T(1024)S(1)} %bitcast.77, f32[4096,128]{1,0:T(8,128)S(1)} %copy-done), custom_call_target="tpu_custom_call" | custom-call | tf_op jit(solution)/shard_map/fetch/pallas_call | solution.py:653
  57.5 16.6 %all-gather.1 = bf16[8,128,256]{2,1,0:T(8,128)(2,1)S(1)} all-gather(bf16[2,128,256]{2,1,0:T(8,128)(2,1)S(1)} %copy-done.32), channel_id=3, replica_groups=mesh['dp'=8,'mp'=4] {'mp'}, dimensions={0}, use_global_device_ids=true | all-gather | bytes 655360 | tf_op jit(solution)/shard_map/all_gather | solution.py:618
  75.8 10.2 %attention_forward.1 = (bf16[2,16,256]{2,1,0:T(8,128)(2,1)S(1)}, bf16[2,16,512]{2,1,0:T(8,128)(2,1)S(1)}, bf16[2,512,256]{2,1,0:T(8,128)(2,1)S(1)}, bf16[2,12,51...) custom-call(s32[32]{0:T(128)S(1)} %reshape.109.cnt, ...), custom_call_target="tpu_custom_call" | custom-call | tf_op jit(solution)/shard_map/attention_forward/pallas_call | solution.py:679
  89.9 41.7 %upper.1 = (bf16[2,16,256]{2,1,0:T(8,128)(2,1)}, bf16[2,256,256]{2,1,0:T(8,128)(2,1)}, bf16[2,256,512]{2,1,0:T(8,128)(2,1)}, bf16[2,512,256]{2,1,0:T(8,128)(2,1)}, f32[8,128]{1,0:T(8,128)}) custom-call(bf16[2,16,256]{2,1,0:T(8,128)(2,1)} %copy-done.14, f32[2,256,256]{2,1,0:T(8,128)} %w_one.1, f32[2,256,512]{2,1,0:T(8,128)} %w_two.1, f32[2,512,256]{2,1,0:T(8,128)} %w_three.1, ...), custom_call_target="tpu_custom_call" | custom-call | tf_op jit(solution)/shard_map/upper/pallas_call | solution.py:709
  131.6 12.6 %attention_backward.1 = (bf16[2,512,128]{2,1,0:T(8,128)(2,1)}, bf16[2,128,256]{2,1,0:T(8,128)(2,1)}, f32[2,1,256]{2,1,0:T(1,128)}, bf16[2,4,3,256,128]{4,3,2,1,0:T(8,128)(2,1)}, bf16[2,4,128,256]{3,2,1,0:T(8,128)(2,1)}) custom-call(s32[32]{0:T(128)} %copy-done.15, bf16[2,512,128]{2,1,0:T(8,128)(2,1)} %bitcast.73, f32[2,128,256]{2,1,0:T(8,128)} %w_in.3, ...), custom_call_target="tpu_custom_call" | custom-call | tf_op jit(solution)/shard_map/attention_backward/pallas_call | solution.py:738
  145.6 85.1 %all-reduce.14.cloned.1.call-done = (bf16[2,4,3,256,128]{4,3,2,1,0:T(8,128)(2,1)}, bf16[2,4,128,256]{3,2,1,0:T(8,128)(2,1)}) async-done(((bf16[2,4,3,256,128]{4,3,2,1,0:T(8,128)(2,1)}, bf16[2,4,128,256]{3,2,1,0:T(8,128)(2,1)}), (bf16[2,4,3,256,128]{4,3,2,1,0:T(8,128)(2,1)}, bf16[2,4,128,256]{3,2,1,0:T(8,128)(2,1)})) %all-reduce.14.cloned.1.call-update) | async-done | bytes 2097168
  230.7 2.2 dynamic-slice_bitcast_fusion.1
  232.9 2.4 dynamic-slice_bitcast_fusion
  236.6 22.4 %line_slots.1 = bf16[4,1024,128]{2,1,0:T(8,128)(2,1)S(1)} custom-call(bf16[1024,128]{1,0:T(8,128)(2,1)S(1)} %bitcast.74), custom_call_target="tpu_custom_call" | custom-call | tf_op jit(solution)/shard_map/line_slots/pallas_call | solution.py:784
  259.0 31.9 %return_rows.1.rows = bf16[8,1024,128]{2,1,0:T(8,128)(2,1)S(1)} custom-call(s32[8,1024]{1,0:T(8,128)S(1)} %reshape.121.tokens, bf16[4096,128]{1,0:T(8,128)(2,1)S(1)} %bitcast.71), custom_call_target="tpu_custom_call" | custom-call | tf_op jit(solution)/shard_map/return_rows/pallas_call | solution.py:793
  290.9 15.3 %add_rows.1 = (f32[4096,128]{1,0:T(8,128)S(1)}, f32[8,128]{1,0:T(8,128)S(1)}) custom-call(s32[8,1024]{1,0:T(8,128)S(1)} %bitcast.76, s32[8]{0:T(128)S(1)} %get-tuple-element.108.counts, bf16[8,1024,128]{2,1,0:T(8,128)(2,1)S(1)} %return_rows.1.rows), custom_call_target="tpu_custom_call" | custom-call | tf_op jit(solution)/shard_map/add_rows/pallas_call | solution.py:809
  307.5 66.2 %psum.54 = bf16[2,256]{1,0:T(2,128)(2,1)S(1)} all-reduce(bf16[2,256]{1,0:T(2,128)(2,1)S(1)} %bitcast.82), channel_id=1, replica_groups=mesh['dp'=8,'mp'=4] {'dp','mp'}, use_global_device_ids=true, to_apply=%region_16.17 | all-reduce | flops 512 | bytes 2048 | tf_op jit(solution)/shard_map/psum | solution.py:779
  374.3 12.2 %all-reduce.10.cloned.1.call-done = (bf16[2,128,256]{2,1,0:T(8,128)(2,1)}, bf16[2,512,256]{2,1,0:T(8,128)(2,1)}) async-done(((bf16[2,128,256]{2,1,0:T(8,128)(2,1)}, bf16[2,512,256]{2,1,0:T(8,128)(2,1)}), (bf16[2,128,256]{2,1,0:T(8,128)(2,1)}, bf16[2,512,256]{2,1,0:T(8,128)(2,1)})) %all-reduce.10.cloned.1.call-update) | async-done | bytes 655376 | tf_op jit(solution)/shard_map/psum | solution.py:778
  389.4 1.9 fusion.9
  391.9 56.4 %all-reduce.12.cloned.1.call-done = (bf16[2,3,256,128]{3,2,1,0:T(8,128)(2,1)}, bf16[2,128,256]{2,1,0:T(8,128)(2,1)}, bf16[2,256,256]{2,1,0:T(8,128)(2,1)}, bf16[2,256,512]{2,1,0:T(8,128)(2,1)}) async-done(((bf16[2,3,256,128]{3,2,1,0:T(8,128)(2,1)}, bf16[2,128,256]{2,1,0:T(8,128)(2,1)}, bf16[2,256,256]{2,1,0:T(8,128)(2,1)}, bf16[2,256,512]{2,1,0:T(8,128)(2,1)}), (bf16[2,3,256,128]{3,2,1,0:T(8,128)(2,1)}, ...) | async-done | bytes 1310736 | tf_op jit(solution)/shard_map/psum | solution.py:780
  457.9 6.0 %norm_parts.1 = (f32[8,8,128]{2,1,0:T(8,128)S(1)}, f32[4,8,128]{2,1,0:T(8,128)S(1)}) custom-call(f32[8,128]{1,0:T(8,128)S(1)} %get-tuple-element.65.table_sq, f32[8,128]{1,0:T(8,128)S(1)} %broadcast_in_dim.24.dense_sq), custom_call_target="tpu_custom_call" | custom-call | tf_op jit(solution)/shard_map/norm_parts/pallas_call | solution.py:821
  466.6 2.2 multiply_add_fusion.7
  469.4 2.8 multiply_add_fusion.4
  475.6 2.0 multiply_add_fusion.3
  478.7 1.9 multiply_add_fusion.2
  482.7 3.2 multiply_add_fusion
  (142 shorter events, 34.3 us)
Async XLA Ops:
  7.2 5.0 %copy-start.43 = (s32[64]{0:T(128)S(1)}, s32[64]{0:T(128)}, u32[]{:S(2)}) copy-start(s32[64]{0:T(128)} %param.34) | copy-start | bytes 772
  7.2 14.4 %copy-start.38 = (f32[2,256]{1,0:T(2,128)S(1)}, f32[2,256]{1,0:T(2,128)}, u32[]{:S(2)}) copy-start(f32[2,256]{1,0:T(2,128)} %param.42) | copy-start | bytes 6148
  7.2 14.4 %copy-start.24 = (f32[2,128,256]{2,1,0:T(8,128)S(1)}, f32[2,128,256]{2,1,0:T(8,128)}, u32[]{:S(2)}) copy-start(f32[2,128,256]{2,1,0:T(8,128)} %param.48) | copy-start | bytes 786436
  7.2 15.1 %copy-start.44 = (f32[4096]{0:T(1024)S(1)}, f32[4096]{0:T(1024)}, u32[]{:S(2)}) copy-start(f32[4096]{0:T(1024)} %param.35) | copy-start | bytes 49156
  7.2 15.1 %copy-start.45 = (s32[512]{0:T(512)S(1)}, s32[512]{0:T(512)}, u32[]{:S(2)}) copy-start(s32[512]{0:T(512)} %param.33) | copy-start | bytes 6148
  7.3 18.6 %copy-start = (f32[4096,128]{1,0:T(8,128)S(1)}, f32[4096,128]{1,0:T(8,128)}, u32[]{:S(2)}) copy-start(f32[4096,128]{1,0:T(8,128)} %table.1) | copy-start | bytes 6291460
  7.3 66.9 %all-gather.4.cloned.1.call-start = ((), (), s32[]{:S(2)}) async-start(), calls=%async_computation | async-start | bytes 1966080 | tf_op jit(solution)/shard_map/all_gather | solution.py:617
  9.4 221.3 %all-reduce.14.cloned.1.call-start = ((), (), s32[]{:S(2)}) async-start(), calls=%async_computation.3 | async-start | bytes 4194304
  10.3 63.8 %copy-start.15 = (s32[32]{0:T(128)}, s32[32]{0:T(128)S(1)}, u32[]{:S(2)}) copy-start(s32[32]{0:T(128)S(1)} %reshape.109.cnt) | copy-start | bytes 388
  12.1 62.0 %copy-start.3 = (f32[2,128,256]{2,1,0:T(8,128)S(1)}, f32[2,128,256]{2,1,0:T(8,128)}, u32[]{:S(2)}) copy-start(f32[2,128,256]{2,1,0:T(8,128)} %w_in.3) | copy-start | bytes 786436
  21.6 64.3 %copy-start.13 = (f32[2,1,256]{2,1,0:T(1,128)}, f32[2,1,256]{2,1,0:T(1,128)S(1)}, u32[]{:S(2)}) copy-start(f32[2,1,256]{2,1,0:T(1,128)S(1)} %reshape.117.gain) | copy-start | bytes 6148
  23.5 62.4 %copy-start.39 = (f32[512]{0:T(512)}, f32[512]{0:T(512)S(1)}, u32[]{:S(2)}) copy-start(f32[512]{0:T(512)S(1)} %select_reduce_fusion) | copy-start | bytes 6148
  25.8 31.6 %copy-start.32 = (bf16[2,128,256]{2,1,0:T(8,128)(2,1)S(1)}, bf16[2,128,256]{2,1,0:T(8,128)(2,1)}, u32[]{:S(2)}) copy-start(bf16[2,128,256]{2,1,0:T(8,128)(2,1)} %convert_element_type.39) | copy-start | bytes 393220
  57.5 74.1 %copy-start.5 = (bf16[1024,128]{1,0:T(8,128)(2,1)}, bf16[1024,128]{1,0:T(8,128)(2,1)S(1)}, u32[]{:S(2)}) copy-start(bf16[1024,128]{1,0:T(8,128)(2,1)S(1)} %fetch.1) | copy-start | bytes 786436
  74.1 57.4 %copy-start.2 = (bf16[8,128,256]{2,1,0:T(8,128)(2,1)}, bf16[8,128,256]{2,1,0:T(8,128)(2,1)S(1)}, u32[]{:S(2)}) copy-start(bf16[8,128,256]{2,1,0:T(8,128)(2,1)S(1)} %all-gather.1) | copy-start | bytes 1572868
  144.2 92.4 %copy-start.10 = (bf16[2,512,128]{2,1,0:T(8,128)(2,1)S(1)}, bf16[2,512,128]{2,1,0:T(8,128)(2,1)}, u32[]{:S(2)}) copy-start(bf16[2,512,128]{2,1,0:T(8,128)(2,1)} %get-tuple-element.64) | copy-start | bytes 786436
  144.2 242.3 %all-reduce.10.cloned.1.call-start = ((), (), s32[]{:S(2)}) async-start(), calls=%async_computation.1 | async-start | bytes 1310720 | tf_op jit(solution)/shard_map/psum | solution.py:778
  144.3 114.7 %copy-start.42 = (f32[2,1,256]{2,1,0:T(1,128)S(1)}, f32[2,1,256]{2,1,0:T(1,128)}, u32[]{:S(2)}) copy-start(f32[2,1,256]{2,1,0:T(1,128)} %get-tuple-element.73) | copy-start | bytes 6148
  144.9 303.4 %all-reduce.12.cloned.1.call-start = ((), (), s32[]{:S(2)}) async-start(), calls=%async_computation.2 | async-start | bytes 2621440 | tf_op jit(solution)/shard_map/psum | solution.py:780
  290.9 175.7 %copy-start.4 = (f32[2,128,256]{2,1,0:T(8,128)S(1)}, f32[2,128,256]{2,1,0:T(8,128)}, u32[]{:S(2)}) copy-start(f32[2,128,256]{2,1,0:T(8,128)} %w_in.3) | copy-start | bytes 786436
  307.5 161.3 %copy-start.40 = (f32[2,256]{1,0:T(2,128)S(1)}, f32[2,256]{1,0:T(2,128)}, u32[]{:S(2)}) copy-start(f32[2,256]{1,0:T(2,128)} %param.44) | copy-start | bytes 6148
  307.5 161.3 %copy-start.41 = (f32[2,256]{1,0:T(2,128)S(1)}, f32[2,256]{1,0:T(2,128)}, u32[]{:S(2)}) copy-start(f32[2,256]{1,0:T(2,128)} %param.43) | copy-start | bytes 6148
  307.5 161.8 %copy-start.18 = (f32[2,256,3,128]{3,1,2,0:T(8,128)S(1)}, f32[2,256,3,128]{3,1,2,0:T(8,128)}, u32[]{:S(2)}) copy-start(f32[2,256,3,128]{3,1,2,0:T(8,128)} %param.45) | copy-start | bytes 2359300
  478.7 4.0 copy-start.20
  (27 other events, 60.8 us)
Sparse Core Ops, SparseCore 0:
  10.2 39.7 all-gather.3
  144.3 86.3 all-reduce.13
  237.6 148.8 all-reduce.9
  391.0 57.2 all-reduce.11

commit v2 on v1

--- a/solution.py
+++ b/solution.py
@@ -120,75 +120,258 @@
     return copy
 
 
-def asks_kernel(plane, lists, extra, got_lists, got_extra, out_sems, in_sems, own_sems):
-    me, part = enter(plane, 0)
-    copies = []
+def gather_rows(ids, table, target):
+    per = LANES // 16
+
+    def body(i, carry):
+        at = pl.multiple_of(i * 16, 16)
+        block = lax.shift_right_logical(i, 3)
+        first = (i & (per - 1)) * 16
+        rows = [table[pl.ds(ids(block, first + u), 1), :] for u in range(16)]
+        target[pl.ds(at, 16), :] = jnp.concatenate(rows, 0).astype(BF16)
+        return carry
+
+    lax.fori_loop(0, target.shape[0] // 16, body, 0)
+
+
+def fetch_kernel(
+    plane,
+    line,
+    capacity,
+    lists,
+    extra,
+    place,
+    table,
+    w_qkv,
+    w_out,
+    out,
+    got_lists,
+    got_extra,
+    wide_qkv,
+    wide_out,
+    ids,
+    sent,
+    got,
+    wide,
+    list_out,
+    list_in,
+    out_sems,
+    in_sems,
+    far_out,
+    far_in,
+    near_out,
+    near_in,
+    own_sems,
+):
+    me, part = enter(plane, line)
+    core = lax.rem(me, 2)
+    sibling = me + 1 - 2 * core
+    wide_qkv[part] = w_qkv[...].astype(BF16)
+    wide_out[part] = w_out[...].astype(BF16)
+    far = []
+    for k in range(1, line):
+        peer = lax.rem(part + k, line)
+        for j, block in enumerate((wide_qkv, wide_out)):
+            at = block.at[part, core]
+            far.append(send(at, at, far_out.at[j, k], far_in.at[j, k], (me, peer)))
+    asked = []
     for k in range(1, plane):
         peer = lax.rem(me + k, plane)
-        copies.append(send(lists.at[peer], got_lists.at[me], out_sems.at[0, k], in_sems.at[0, k], (peer, part)))
-        copies.append(send(extra, got_extra.at[me], out_sems.at[1, k], in_sems.at[1, k], (peer, part)))
+        asked.append(send(lists.at[peer], got_lists.at[me], list_out.at[0, k], list_in.at[0, k], (peer, part)))
+        asked.append(send(extra, got_extra.at[me], list_out.at[1, k], list_in.at[1, k], (peer, part)))
     mine = [
         pltpu.make_async_copy(lists.at[me], got_lists.at[me], own_sems.at[0]),
         pltpu.make_async_copy(extra, got_extra.at[me], own_sems.at[1]),
     ]
     for copy in mine:
         copy.start()
-    for copy in mine + copies:
-        copy.wait()
-
-
-def gather_rows(capacity, ids, table, target):
-    def body(i, carry):
-        at = pl.multiple_of(i * 16, 16)
-        rows = [table[pl.ds(ids(at + u), 1), :] for u in range(16)]
-        target[pl.ds(at, 16), :] = jnp.concatenate(rows, 0).astype(BF16)
-        return carry
-
-    lax.fori_loop(0, capacity // 16, body, 0)
-
-
-def fetch_kernel(plane, capacity, ids, place, table, out, sent, got, wide, out_sems, in_sems):
-    me, part = enter(plane, 0)
+    for copy in mine + asked:
+        copy.wait()
+    numbers = pltpu.make_async_copy(got_lists, ids, own_sems.at[2])
+    numbers.start()
+    numbers.wait()
+    half = capacity // LANES
     copies = []
     for k in range(1, plane):
         peer = lax.rem(me + k, plane)
-        gather_rows(capacity, lambda j, peer=peer: ids[peer, j], table, sent.at[peer])
+        gather_rows(lambda b, j, peer=peer: ids[peer, half + b, j], table, sent.at[peer])
         copies.append(send(sent.at[peer], got.at[me], out_sems.at[k], in_sems.at[k], (peer, part)))
-    gather_rows(capacity, lambda j: ids[me, j], table, sent.at[me])
+    gather_rows(lambda b, j: ids[me, half + b, j], table, sent.at[me])
     wide[pl.ds(pl.multiple_of(me * capacity, capacity), capacity), :] = sent[me].astype(F32)
+    near = []
+    for k in range(1, line):
+        peer = lax.rem(part - k + line, line)
+        for j, block in enumerate((wide_qkv, wide_out)):
+            far[2 * (k - 1) + j].wait_recv()
+            at = block.at[peer, core]
+            near.append(send(at, at, near_out.at[j, k], near_in.at[j, k], (sibling, part)))
     for k in range(1, plane):
         peer = lax.rem(me - k + plane, plane)
         copies[k - 1].wait_recv()
         wide[pl.ds(pl.multiple_of(peer * capacity, capacity), capacity), :] = got[peer].astype(F32)
-    gather_rows(out.shape[0], lambda j: place[j], wide, out)
-    for copy in copies:
+    gather_rows(lambda b, j: place[b, j], wide, out)
+    for copy in copies + far:
         copy.wait_send()
-
-
-def slots_kernel(line, mine, out, out_sems, in_sems, own_sem):
-    me, part = enter(0, line)
+    for copy in near:
+        copy.wait()
+
+
+def spread_kernel(
+    plane,
+    line,
+    mine,
+    d_qkv,
+    d_out,
+    d_three,
+    d_in,
+    d_one,
+    d_two,
+    gain,
+    out,
+    summed,
+    gain_sum,
+    near_split,
+    near_whole,
+    half,
+    got,
+    gains,
+    far_out,
+    far_in,
+    near_out,
+    near_in,
+    sum_out,
+    sum_in,
+    gain_out,
+    gain_in,
+    own_sem,
+):
+    me, part = enter(plane, line)
+    chips = plane // 2
+    core = lax.rem(me, 2)
+    chip = me // 2
+    sibling = me + 1 - 2 * core
     copies = []
     for k in range(1, line):
         peer = lax.rem(part + k, line)
-        copies.append(send(mine, out.at[part], out_sems.at[k], in_sems.at[k], (me, peer)))
+        copies.append(send(mine, out.at[part], far_out.at[k], far_in.at[k], (me, peer)))
+    split_grads, whole_grads = (d_qkv, d_out), (d_three, d_in, d_one, d_two)
+    first = []
+    for j, grad in enumerate(split_grads):
+        first.append(send(grad.at[:, :, 1 - core], near_split[j], near_out.at[j], near_in.at[j], (sibling, part)))
+    for j, grad in enumerate(whole_grads, len(split_grads)):
+        first.append(send(grad.at[:, 1 - core], near_whole[j - 2], near_out.at[j], near_in.at[j], (sibling, part)))
+    for k in range(1, plane):
+        peer = lax.rem(me + k, plane)
+        copies.append(send(gain, gains.at[me], gain_out.at[k], gain_in.at[k], (peer, part)))
     own = pltpu.make_async_copy(mine, out.at[part], own_sem)
     own.start()
+    gains[me] = gain[...]
+    for copy in first:
+        copy.wait()
+    for c in range(chips):
+        at = 0
+        for j, grad in enumerate(split_grads):
+            rows = grad.shape[3]
+            for m in range(line):
+                total = grad[m, c, core].astype(F32) + near_split[j][m, c].astype(F32)
+                half[c, at : at + rows, :] = total.astype(BF16)
+                at += rows
+        for j, grad in enumerate(whole_grads):
+            rows = grad.shape[2]
+            total = grad[c, core].astype(F32) + near_whole[j][c].astype(F32)
+            half[c, at : at + rows, :] = total.astype(BF16)
+            at += rows
+    sums = []
+    for k in range(1, chips):
+        to = lax.rem(chip + k, chips)
+        sums.append(send(half.at[to], got.at[k - 1], sum_out.at[k], sum_in.at[k], (2 * to + core, part)))
+    for copy in sums:
+        copy.wait()
+    total = half[chip].astype(F32)
+    for k in range(chips - 1):
+        total = total + got[k].astype(F32)
+    summed[...] = total.astype(BF16)
     own.wait()
     for copy in copies:
         copy.wait()
-
-
-def return_kernel(plane, capacity, tokens, rows, out, wide, sent, out_sems, in_sems, own_sem):
-    me, part = enter(plane, 0)
+    total = gains[0]
+    for d in range(1, plane):
+        total = total + gains[d]
+    gain_sum[...] = total
+
+
+def return_kernel(
+    plane,
+    line,
+    capacity,
+    cuts,
+    tokens,
+    rows,
+    summed,
+    gain,
+    out,
+    dense,
+    dense_sq,
+    gain_all,
+    wide,
+    sent,
+    got,
+    gains,
+    out_sems,
+    in_sems,
+    far_out,
+    far_in,
+    gain_out,
+    gain_in,
+    own_sem,
+):
+    me, part = enter(plane, line)
+    far = []
+    split_cuts, (whole_at, whole_rows), (last_at, last_rows) = cuts
+    for k in range(1, line):
+        peer = lax.rem(part + k, line)
+        to = 0
+        for j, (at, count) in enumerate(split_cuts):
+            begin = pl.multiple_of(at + peer * count, 16)
+            far.append(
+                send(summed.at[pl.ds(begin, count)], got.at[part, to : to + count], far_out.at[j, k], far_in.at[j, k], (me, peer))
+            )
+            to += count
+        target = got.at[part, to : to + whole_rows]
+        source = summed.at[whole_at : whole_at + whole_rows]
+        far.append(send(source, target, far_out.at[2, k], far_in.at[2, k], (me, peer)))
+        far.append(send(gain, gains.at[part], gain_out.at[k], gain_in.at[k], (me, peer)))
+    gains[part] = gain[...]
     wide[...] = rows[...].astype(F32)
     copies = []
     for k in range(1, plane):
         peer = lax.rem(me + k, plane)
-        gather_rows(capacity, lambda j, peer=peer: tokens[peer, j], wide, sent.at[peer])
+        gather_rows(lambda b, j, peer=peer: tokens[peer, b, j], wide, sent.at[peer])
         copies.append(send(sent.at[peer], out.at[me], out_sems.at[k], in_sems.at[k], (peer, part)))
-    gather_rows(capacity, lambda j: tokens[me, j], wide, sent.at[me])
+    gather_rows(lambda b, j: tokens[me, b, j], wide, sent.at[me])
     own = pltpu.make_async_copy(sent.at[me], out.at[me], own_sem)
     own.start()
+    to = 0
+    for at, count in split_cuts:
+        got[part, to : to + count] = summed[pl.ds(pl.multiple_of(at + part * count, 16), count), :]
+        to += count
+    got[part, to : to + whole_rows] = summed[whole_at : whole_at + whole_rows, :]
+    for copy in far:
+        copy.wait()
+    total = got[0].astype(F32)
+    for m in range(1, line):
+        total = total + got[m].astype(F32)
+    dense[0 : to + whole_rows, :] = total.astype(BF16)
+    dense[to + whole_rows :, :] = summed[last_at : last_at + last_rows, :]
+    square = jnp.zeros((8, LANES), F32)
+    for begin, count, weight in ((0, to, 1.0), (to, whole_rows, 1.0 / line), (to + whole_rows, last_rows, 1.0)):
+        block = dense[begin : begin + count, :].astype(F32)
+        square = square + weight * jnp.sum((block * block).reshape(count // 8, 8, LANES), 0)
+    dense_sq[...] = square
+    total = gains[0]
+    for m in range(1, line):
+        total = total + gains[m]
+    gain_all[...] = total
     own.wait()
     for copy in copies:
         copy.wait()
@@ -227,22 +410,69 @@
     square[...] = lax.fori_loop(0, out.shape[0] // 64, add, jnp.zeros((8, LANES), F32))
 
 
-def norm_kernel(plane, line, table_sq, dense_sq, got_table, got_dense, out_sems, in_sems, own_sems):
+def norm_kernel(
+    plane,
+    line,
+    table_sq,
+    dense_sq,
+    dense,
+    gain,
+    norm_sq,
+    dense_all,
+    along,
+    across,
+    along_out,
+    along_in,
+    across_out,
+    across_in,
+    far_out,
+    far_in,
+    near_out,
+    near_in,
+    own_sem,
+):
     me, part = enter(plane, line)
-    copies = []
-    for k in range(1, plane):
-        peer = lax.rem(me + k, plane)
-        copies.append(send(table_sq, got_table.at[me], out_sems.at[0, k], in_sems.at[0, k], (peer, part)))
-    for k in range(1, line):
-        peer = lax.rem(part + k, line)
-        copies.append(send(dense_sq, got_dense.at[part], out_sems.at[1, k], in_sems.at[1, k], (me, peer)))
-    mine = [
-        pltpu.make_async_copy(table_sq, got_table.at[me], own_sems.at[0]),
-        pltpu.make_async_copy(dense_sq, got_dense.at[part], own_sems.at[1]),
+    chips = plane // 2
+    core = lax.rem(me, 2)
+    chip = me // 2
+    sibling = me + 1 - 2 * core
+    across[me] = dense_sq[...] + table_sq[...] * (1.0 / line)
+    tiny = [
+        send(across.at[me], across.at[me], across_out.at[k], across_in.at[k], (lax.rem(me + k, plane), part))
+        for k in range(1, plane)
     ]
-    for copy in mine:
-        copy.start()
-    for copy in mine + copies:
+    far = []
+    for k in range(1, chips):
+        to = lax.rem(chip + k, chips)
+        far.append(send(dense, dense_all.at[me], far_out.at[k], far_in.at[k], (2 * to + core, part)))
+    near = [send(dense, dense_all.at[me], near_out.at[0], near_in.at[0], (sibling, part))]
+    own = pltpu.make_async_copy(dense, dense_all.at[me], own_sem)
+    own.start()
+    for copy in tiny:
+        copy.wait()
+    total = across[0]
+    for d in range(1, plane):
+        total = total + across[d]
+    along[part] = total
+    peers = [lax.rem(part + k, line) for k in range(1, line)]
+    tiny = [
+        send(along.at[part], along.at[part], along_out.at[k], along_in.at[k], (me, peer)) for k, peer in enumerate(peers)
+    ]
+    for k in range(1, chips):
+        peer = 2 * lax.rem(chip - k + chips, chips) + core
+        far[k - 1].wait_recv()
+        near.append(send(dense_all.at[peer], dense_all.at[peer], near_out.at[k], near_in.at[k], (sibling, part)))
+    for copy in tiny:
+        copy.wait()
+    total = along[0]
+    for m in range(1, line):
+        total = total + along[m]
+    gains = gain[...]
+    norm_sq[...] = jnp.broadcast_to(jnp.sum(total + gains * gains), norm_sq.shape)
+    own.wait()
+    for copy in far:
+        copy.wait_send()
+    for copy in near:
         copy.wait()
 
 
@@ -337,7 +567,9 @@
     branch = dsum.astype(BF16)
     dmix = []
     for m in range(parts):
-        d_out[0, m] = tn(pm_in[0, :, m * LANES : (m + 1) * LANES], branch).astype(BF16)
+        grad = tn(pm_in[0, :, m * LANES : (m + 1) * LANES], branch).astype(BF16)
+        for j in range(width // LANES):
+            d_out[m, 0, j] = grad[:, j * LANES : (j + 1) * LANES]
         dmix.append(nt(branch, w_out[m, 0]))
     lane = iota((LANES, LANES), 1)
     line = iota((LANES, LANES), 0)
@@ -384,7 +616,7 @@
         for c in range(3):
             grad = dqkv[c * parts + m]
             dnormed = dnormed + nt(grad, w_qkv[m, 0, c])
-            d_qkv[0, m, c] = tn(normed, grad).astype(BF16)
+            d_qkv[m, 0, c] = tn(normed, grad).astype(BF16)
     dnormed = dnormed.astype(BF16).astype(F32)
     xs = x[0]
     w = w_in[0].astype(BF16)
@@ -399,7 +631,9 @@
     counts = chain(iota((pairs, slots, width), 0), every)
     spread = jnp.where(slot < counts, spread, 0.0).reshape(tokens, width)
     dhidden = (spread + dh).astype(BF16)
-    d_in[0] = tn(xs, dhidden).astype(BF16)
+    grad = tn(xs, dhidden).astype(BF16)
+    for j in range(width // LANES):
+        d_in[0, j] = grad[:, j * LANES : (j + 1) * LANES]
     demb[0] = nt(dhidden, w).astype(BF16)
 
 
@@ -531,7 +765,9 @@
         for k in range(line - 1)
     ]
     for t in range(towers):
-        d_three[t] = tn(act_two[t], dthirds[t]).astype(BF16)
+        grad = tn(act_two[t], dthirds[t]).astype(BF16)
+        for j in range(width // LANES):
+            d_three[t, j] = grad[:, j * LANES : (j + 1) * LANES]
     for copy in spread:
         copy.wait()
     dfirsts = []
@@ -547,8 +783,10 @@
     ]
     for t in range(towers):
         dsecond = dsec_all[t].reshape(rows, -1)
-        d_two[t] = tn(act_one[t], dsecond).astype(BF16)
-        d_one[t] = tn(pools[t], dfirsts[t]).astype(BF16)
+        for grads, grad in ((d_two, tn(act_one[t], dsecond)), (d_one, tn(pools[t], dfirsts[t]))):
+            grad = grad.astype(BF16)
+            for j in range(grad.shape[1] // LANES):
+                grads[t, j] = grad[:, j * LANES : (j + 1) * LANES]
     for copy in back:
         copy.wait()
     for t in range(towers):
@@ -614,9 +852,6 @@
     units = w_one.shape[2]
     seconds = w_two.shape[2]
 
-    wide_qkv = lax.all_gather(jnp.transpose(w_qkv.astype(BF16), (0, 2, 1, 3)), "mp", axis=0)
-    wide_out = lax.all_gather(w_out.astype(BF16), "mp", axis=0)
-
     def ordered(value):
         value = value.reshape(line, own, towers, slots)
         return jnp.transpose(value, (0, 2, 1, 3)).reshape(requests // LANES, LANES)
@@ -640,31 +875,35 @@
         name="request_lists",
     )(owner, row, own_owner, own_row)
     lone = jnp.pad(positive[None, :], ((0, 7), (0, LANES - batch)))
-    got_lists, got_pos = pl.pallas_call(
-        functools.partial(asks_kernel, plane),
-        out_shape=[shape(lists.shape, I32), shape((plane, 8, LANES), I32)],
-        in_specs=[VMEM] * 2,
-        out_specs=[VMEM] * 2,
-        scratch_shapes=[DMA((2, plane)), DMA((2, plane)), DMA((2,))],
-        compiler_params=params(32, collective_id=1, has_side_effects=True),
-        name="ask",
-    )(lists, lone)
-    ids = got_lists[:, per:, :].reshape(plane, capacity)
-    embedded = pl.pallas_call(
-        functools.partial(fetch_kernel, plane, capacity),
-        out_shape=shape((own_requests, depth), BF16),
-        in_specs=[SMEM, SMEM, VMEM],
-        out_specs=VMEM,
+    embedded, got_lists, got_pos, wide_qkv, wide_out = pl.pallas_call(
+        functools.partial(fetch_kernel, plane, line, capacity),
+        out_shape=[
+            shape((own_requests, depth), BF16),
+            shape(lists.shape, I32),
+            shape((plane, 8, LANES), I32),
+            shape((line, towers, 3, width, LANES), BF16),
+            shape((line, towers, LANES, width), BF16),
+        ],
+        in_specs=[VMEM, VMEM, SMEM, VMEM, VMEM, VMEM],
+        out_specs=[VMEM] * 5,
         scratch_shapes=[
+            pltpu.SMEM(lists.shape, I32),
             pltpu.VMEM((plane, capacity, depth), BF16),
             pltpu.VMEM((plane, capacity, depth), BF16),
             pltpu.VMEM((plane * capacity, depth), F32),
+            DMA((2, plane)),
+            DMA((2, plane)),
             DMA((plane,)),
             DMA((plane,)),
-        ],
-        compiler_params=params(48, collective_id=2, has_side_effects=True),
+            DMA((2, line)),
+            DMA((2, line)),
+            DMA((2, line)),
+            DMA((2, line)),
+            DMA((3,)),
+        ],
+        compiler_params=params(56, collective_id=2, has_side_effects=True),
         name="fetch",
-    )(ids, own_place.reshape(own_requests), embedding)
+    )(lists, lone, own_place, embedding, jnp.transpose(w_qkv, (0, 2, 1, 3)), w_out)
     embedded = embedded.reshape(towers, tokens, depth)
 
     counts = jnp.transpose(slot_count).reshape(towers, line, own)
@@ -710,9 +949,9 @@
         functools.partial(upper_kernel, plane, line),
         out_shape=[
             shape((towers, own, width), BF16),
-            shape((towers, width, units), BF16),
-            shape((towers, units, seconds), BF16),
-            shape((towers, seconds, width), BF16),
+            shape((towers, units // LANES, width, LANES), BF16),
+            shape((towers, seconds // LANES, units, LANES), BF16),
+            shape((towers, width // LANES, seconds, LANES), BF16),
             shape((8, LANES), F32),
         ],
         in_specs=[VMEM] * 8,
@@ -740,10 +979,10 @@
         grid=(towers,),
         out_shape=[
             shape((towers, tokens, depth), BF16),
-            shape((towers, depth, width), BF16),
+            shape((towers, width // LANES, depth, LANES), BF16),
             shape((towers, 1, width), F32),
-            shape((towers, line, 3, width, LANES), BF16),
-            shape((towers, line, LANES, width), BF16),
+            shape((line, towers, 3, width, LANES), BF16),
+            shape((line, towers, width // LANES, LANES, LANES), BF16),
         ],
         in_specs=[
             SMEM,
@@ -761,50 +1000,87 @@
         ],
         out_specs=[
             lead(tokens, depth),
-            lead(depth, width),
+            lead(width // LANES, depth, LANES),
             lead(1, width),
-            lead(line, 3, width, LANES),
-            lead(line, LANES, width),
+            qkv_spec,
+            pl.BlockSpec((line, 1, width // LANES, LANES, LANES), lambda t: (0, t, 0, 0, 0)),
         ],
         scratch_shapes=[pltpu.VMEM((3 * line, tokens, LANES), BF16)],
         compiler_params=params(56),
         name="attention_backward",
     )(counts, embedded, w_in, gains, wide_qkv, wide_out, normed, qkv, prob, spread, pm, dpooled)
 
-    both = ("dp", "mp")
-    d_one = lax.psum(d_one, "dp").astype(F32)
-    d_two = lax.psum(d_two, "dp").astype(F32)
-    d_three = lax.psum(d_three, both).astype(F32)
-    d_in = lax.psum(d_in, both).astype(F32)
-    d_gain = lax.psum(d_gain.reshape(towers, width).astype(BF16), both).astype(F32)
-    d_qkv = lax.psum(lax.psum_scatter(d_qkv, "mp", scatter_dimension=1, tiled=False), "dp")
-    d_qkv = jnp.transpose(d_qkv, (0, 2, 1, 3)).astype(F32)
-    d_out = lax.psum(lax.psum_scatter(d_out, "mp", scatter_dimension=1, tiled=False), "dp").astype(F32)
-
-    every = pl.pallas_call(
-        functools.partial(slots_kernel, line),
-        out_shape=shape((line, own_requests, depth), BF16),
-        in_specs=[VMEM],
-        out_specs=VMEM,
-        scratch_shapes=[DMA((line,)), DMA((line,)), DMA],
-        compiler_params=params(32, collective_id=4, has_side_effects=True),
-        name="line_slots",
-    )(demb.reshape(own_requests, depth))
-    incoming = pl.pallas_call(
-        functools.partial(return_kernel, plane, capacity),
-        out_shape=shape((plane, capacity, depth), BF16),
-        in_specs=[SMEM, VMEM],
-        out_specs=VMEM,
+    def shares(grad, lead=()):
+        rows = grad.size // (LANES * plane * (lead[0] if lead else 1))
+        return grad.reshape(*lead, plane // 2, 2, rows, LANES)
+
+    grads = [shares(d_qkv, (line,)), shares(d_out, (line,))] + [shares(g) for g in (d_three, d_in, d_one, d_two)]
+    sizes = [g.shape[-2] for g in grads]
+    share = line * (sizes[0] + sizes[1]) + sum(sizes[2:])
+    gain_rows = jnp.pad(d_gain.reshape(-1, LANES), ((0, 8 - d_gain.size // LANES), (0, 0)))
+    every, summed, gain_sum = pl.pallas_call(
+        functools.partial(spread_kernel, plane, line),
+        out_shape=[
+            shape((line, own_requests, depth), BF16),
+            shape((share, LANES), BF16),
+            shape((8, LANES), F32),
+        ],
+        in_specs=[VMEM] * 8,
+        out_specs=[VMEM] * 3,
+        scratch_shapes=[
+            [pltpu.VMEM((line, plane // 2, size, LANES), BF16) for size in sizes[:2]],
+            [pltpu.VMEM((plane // 2, size, LANES), BF16) for size in sizes[2:]],
+            pltpu.VMEM((plane // 2, share, LANES), BF16),
+            pltpu.VMEM((plane // 2 - 1, share, LANES), BF16),
+            pltpu.VMEM((plane, 8, LANES), F32),
+            DMA((line,)),
+            DMA((line,)),
+            DMA((6,)),
+            DMA((6,)),
+            DMA((plane // 2,)),
+            DMA((plane // 2,)),
+            DMA((plane,)),
+            DMA((plane,)),
+            DMA,
+        ],
+        compiler_params=params(48, collective_id=4, has_side_effects=True),
+        name="spread",
+    )(demb.reshape(own_requests, depth), *grads, gain_rows)
+    whole_at = line * (sizes[0] + sizes[1])
+    whole_rows = sizes[2] + sizes[3]
+    last_rows = sizes[4] + sizes[5]
+    cuts = (
+        ((0, sizes[0]), (line * sizes[0], sizes[1])),
+        (whole_at, whole_rows),
+        (whole_at + whole_rows, last_rows),
+    )
+    line_rows = sizes[0] + sizes[1] + whole_rows
+    incoming, dense, dense_sq, gain_all = pl.pallas_call(
+        functools.partial(return_kernel, plane, line, capacity, cuts),
+        out_shape=[
+            shape((plane, capacity, depth), BF16),
+            shape((line_rows + last_rows, LANES), BF16),
+            shape((8, LANES), F32),
+            shape((8, LANES), F32),
+        ],
+        in_specs=[SMEM, VMEM, VMEM, VMEM],
+        out_specs=[VMEM] * 4,
         scratch_shapes=[
             pltpu.VMEM((requests, depth), F32),
             pltpu.VMEM((plane, capacity, depth), BF16),
+            pltpu.VMEM((line, line_rows, LANES), BF16),
+            pltpu.VMEM((line, 8, LANES), F32),
             DMA((plane,)),
             DMA((plane,)),
+            DMA((3, line)),
+            DMA((3, line)),
+            DMA((line,)),
+            DMA((line,)),
             DMA,
         ],
         compiler_params=params(48, collective_id=5, has_side_effects=True),
         name="return_rows",
-    )(inverse.reshape(plane, capacity), every.reshape(requests, depth))
+    )(inverse.reshape(plane, per, LANES), every.reshape(requests, depth), summed, gain_sum)
     served = got_lists[:, :per, :].reshape(plane, capacity)
     table_grad, table_sq = pl.pallas_call(
         functools.partial(scatter_kernel, capacity),
@@ -816,19 +1092,38 @@
         name="add_rows",
     )(jnp.maximum(served, 0), jnp.sum((served >= 0).astype(I32), 1), incoming)
 
-    whole_sq = jnp.sum(d_in * d_in) + jnp.sum(d_gain * d_gain) + jnp.sum(d_three * d_three)
-    shard_sq = jnp.sum(d_qkv * d_qkv) + jnp.sum(d_out * d_out) + jnp.sum(d_one * d_one) + jnp.sum(d_two * d_two)
-    got_table, got_dense = pl.pallas_call(
+    norm_sq, dense_all = pl.pallas_call(
         functools.partial(norm_kernel, plane, line),
-        out_shape=[shape((plane, 8, LANES), F32), shape((line, 8, LANES), F32)],
-        in_specs=[VMEM] * 2,
+        out_shape=[shape((8, LANES), F32), shape((plane, *dense.shape), BF16)],
+        in_specs=[VMEM] * 4,
         out_specs=[VMEM] * 2,
-        scratch_shapes=[DMA((2, plane)), DMA((2, plane)), DMA((2,))],
+        scratch_shapes=[
+            pltpu.VMEM((line, 8, LANES), F32),
+            pltpu.VMEM((plane, 8, LANES), F32),
+            DMA((line,)),
+            DMA((line,)),
+            DMA((plane,)),
+            DMA((plane,)),
+            DMA((plane // 2,)),
+            DMA((plane // 2,)),
+            DMA((plane // 2,)),
+            DMA((plane // 2,)),
+            DMA,
+        ],
         compiler_params=params(32, collective_id=6, has_side_effects=True),
         name="norm_parts",
-    )(table_sq, jnp.broadcast_to(shard_sq, (8, LANES)))
-    norm = jnp.sqrt(jnp.sum(got_table) + jnp.sum(got_dense[:, 0, 0]) + whole_sq)
+    )(table_sq, dense_sq, dense, gain_all)
+    norm = jnp.sqrt(norm_sq[0, 0])
     factor = jnp.minimum(1.0, CLIP_NORM / norm)
+    found, at = [], 0
+    for size in sizes:
+        found.append(dense_all[:, at : at + size].astype(F32))
+        at += size
+    d_qkv = jnp.transpose(found[0].reshape(towers, 3, width, LANES), (0, 2, 1, 3))
+    side = lambda grad, rows: jnp.transpose(grad.reshape(towers, -1, rows, LANES), (0, 2, 1, 3)).reshape(towers, rows, -1)
+    d_out, d_three, d_in = side(found[1], LANES), side(found[2], seconds), side(found[3], depth)
+    d_one, d_two = side(found[4], width), side(found[5], units)
+    d_gain = gain_all[: d_gain.size // LANES].reshape(towers, width)
     done = []
     done.extend(update(embedding, table_grad, embedding_mom, embedding_avg, factor, ROW_RATE))
     done.extend(update(w_in, d_in, w_in_mom, w_in_avg, factor, MATRIX_RATE))

time: 494 us -> 282 us (0.57)
  waiting for transfers between devices: 154 us -> 0 us
  blocking collectives: 82.8 us -> 0 us
  Pallas kernels: 181 us -> 232 us
  between operations: 21.4 us -> 2.94 us
  other arithmetic: 31.5 us -> 19.8 us
    unnamed x5 -> x0, waiting for transfers between devices: 85.8 us -> none
    psum x2 -> x0, waiting for transfers between devices: 68.6 us -> none  [the longest x1 56.4 us: shards(): lax.psum(lax.psum_scatter(d_qkv, 'mp', scatter_dimension=1, tiled=False),...]
    psum x1 -> x0, blocking collectives: 66.2 us -> none  [shards(): lax.psum(d_gain.reshape(towers, width).astype(BF16), both).astype(F32)]
    pallas_call x1, Pallas kernels: 6.04 us -> 46.8 us  [shards(): pl.pallas_call(functools.partial(norm_kernel, plane, line), out_shape=[sh...]
    all_gather x1 -> x0, blocking collectives: 16.6 us -> none  [shards(): wide_out = lax.all_gather(w_out.astype(BF16), 'mp', axis=0)]
    reduce_sum x9 -> x0, other arithmetic: 12.3 us -> none  [the longest x1 1.92 us: shards(): jnp.sum(d_three * d_three)]
    pallas_call x4 -> x3, Pallas kernels: 92.6 us -> 101 us  [the longest x1 43.1 us: shards(): pl.pallas_call(functools.partial(fetch_kernel, plane, line, capacity), ou...]
    unnamed x100 -> x95, local copies, waits for them, and re-layouts: 13.5 us -> 18.6 us
  transfers between devices with their start and end apart: 4 -> 0, of which waited for: 3 -> 0; matrix products, arithmetic and copies ran while one was open for 4% -> 0% of each run, Pallas kernels for 22% -> 0%
where the time goes in v2:
time: 282 us; the launch traced here: 281 us
  Pallas kernels  232 us (82%)
  local copies, waits for them, and re-layouts  26.4 us (9%)
  other arithmetic  19.8 us (7%)
  between operations  2.94 us (1%)
    pallas_call x1, Pallas kernels, shards(): pl.pallas_call(functools.partial(norm_kernel, plane, line), out_shape=[sh...  46.8 us
    pallas_call x1, Pallas kernels, shards(): pl.pallas_call(functools.partial(upper_kernel, plane, line), out_shape=[s...  44.7 us
    pallas_call x1, Pallas kernels, shards(): pl.pallas_call(functools.partial(fetch_kernel, plane, line, capacity), ou...  43.1 us
    pallas_call x1, Pallas kernels, shards(): pl.pallas_call(functools.partial(return_kernel, plane, line, capacity, cu...  30.6 us
    pallas_call x1, Pallas kernels, shards(): pl.pallas_call(functools.partial(spread_kernel, plane, line), out_shape=[...  27.6 us
    unnamed x95, local copies, waits for them, and re-layouts  18.6 us
    add x8, other arithmetic, update(): average_new = AVERAGE_DECAY * average + (1.0 - AVERAGE_DECAY) * weight_new  16.9 us
    pallas_call x1, Pallas kernels, shards(): pl.pallas_call(functools.partial(scatter_kernel, capacity), out_shape=[sh...  13.9 us

profile of v2, /device:TPU:0, one launch (start us, length us, event | category | flops | bytes accessed | tf_op | source)
XLA Modules:
  0.0 281.1 jit_solution(8301609709562036887)
XLA Ops:
  3.5 2.3 request_lists.1
  7.0 1.3 pad.8.extra
  8.3 43.1 %fetch.1 = (bf16[1024,128]{1,0:T(8,128)(2,1)}, s32[8,16,128]{2,1,0:T(8,128)}, s32[8,8,128]{2,1,0:T(8,128)}, bf16[4,2,3,256,128]{4,3,2,1,0:T(8,128)(2,1)}, bf16[4,2,128,256]{3,2,1,0:T(8,128)(2,1)}) custom-call(s32[8,16,128]{2,1,0:T(8,128)} %copy-done.17, s32[8,128]{1,0:T(8,128)} %pad.8.extra, s32[8,128]{1,0:T(8,128)} %copy-done.21, f32[4096,128]{1,0:T(8,128)} %table.1, ...), custom_call_target="tpu_custom_call" | custom-call | tf_op jit(solution)/shard_map/fetch/pallas_call | solution.py:878
  51.4 1.4 copy-done
  52.8 1.0 copy-done.4
  54.8 10.1 %attention_forward.1 = (bf16[2,16,256]{2,1,0:T(8,128)(2,1)S(1)}, bf16[2,16,512]{2,1,0:T(8,128)(2,1)S(1)}, bf16[2,512,256]{2,1,0:T(8,128)(2,1)S(1)}, bf16[2,12,51...) custom-call(s32[32]{0:T(128)S(1)} %reshape.159.cnt, ...), custom_call_target="tpu_custom_call" | custom-call | tf_op jit(solution)/shard_map/attention_forward/pallas_call | solution.py:918
  65.0 1.3 copy-done.3
  68.3 1.2 select_reduce_fusion
  72.6 44.7 %upper.1 = (bf16[2,16,256]{2,1,0:T(8,128)(2,1)}, bf16[2,2,256,128]{3,2,1,0:T(8,128)(2,1)}, bf16[2,4,256,128]{3,2,1,0:T(8,128)(2,1)}, bf16[2,2,512,128]{3,2,1,0:T(8,128)(2,1)}, f32[8,128]{1,0:T(8,128)}) custom-call(bf16[2,16,256]{2,1,0:T(8,128)(2,1)} %copy-done.20, f32[2,256,256]{2,1,0:T(8,128)} %w_one.1, f32[2,256,512]{2,1,0:T(8,128)} %w_two.1, ...), custom_call_target="tpu_custom_call" | custom-call | tf_op jit(solution)/shard_map/upper/pallas_call | solution.py:948
  117.3 1.2 slice.34
  118.8 13.0 %attention_backward.1 = (bf16[2,512,128]{2,1,0:T(8,128)(2,1)}, bf16[2,2,128,128]{3,2,1,0:T(8,128)(2,1)}, f32[2,1,256]{2,1,0:T(1,128)}, bf16[4,2,3,256,128]{4,3,2,1,0:T(8,128)(2,1)}, bf16[4,2,2,128,128]{4,3,2,1,0:T(8,128)(2,1)}) custom-call(s32[32]{0:T(128)} %copy-done.22, bf16[2,512,128]{2,1,0:T(8,128)(2,1)} %bitcast.104, f32[2,128,256]{2,1,0:T(8,128)} %w_in.3, ...), custom_call_target="tpu_custom_call" | custom-call | tf_op jit(solution)/shard_map/attention_backward/pallas_call | solution.py:977
  132.5 1.4 copy-done.7
  133.9 1.0 copy-done.12
  136.8 27.6 %spread.1 = (bf16[4,1024,128]{2,1,0:T(8,128)(2,1)S(1)}, bf16[1728,128]{1,0:T(8,128)(2,1)S(1)}, f32[8,128]{1,0:T(8,128)S(1)}) custom-call(bf16[1024,128]{1,0:T(8,128)(2,1)S(1)} %bitcast.111, bf16[4,4,2,192,128]{4,3,2,1,0:T(8,128)(2,1)S(1)} %bitcast.103, bf16[4,4,2,64,128]{4,3,2,1,0:T(8,128)(2,1)S(1)} %bitcast.109, bf16[4,2,256,128]{3,2,1,0:T(8,128)(2,1)S(1)} %bitcast.108, ...), custom_call_target="tpu_custom_call" | custom-call | tf_op jit(solution)/shard_map/spread/pallas_call | solution.py:1021
  164.4 30.6 %return_rows.1 = (bf16[8,1024,128]{2,1,0:T(8,128)(2,1)S(1)}, bf16[960,128]{1,0:T(8,128)(2,1)S(1)}, f32[8,128]{1,0:T(8,128)S(1)}, f32[8,128]{1,0:T(8,128)S(1)}) custom-call(s32[8,8,128]{2,1,0:T(8,128)S(1)} %bitcast.114, bf16[4096,128]{1,0:T(8,128)(2,1)S(1)} %bitcast.106, bf16[1728,128]{1,0:T(8,128)(2,1)S(1)} %get-tuple-element.86.summed, ...), custom_call_target="tpu_custom_call" | custom-call | tf_op jit(solution)/shard_map/return_rows/pallas_call | solution.py:1058
  195.0 13.9 %add_rows.1 = (f32[4096,128]{1,0:T(8,128)S(1)}, f32[8,128]{1,0:T(8,128)S(1)}) custom-call(s32[8,1024]{1,0:T(8,128)S(1)} %bitcast.112, s32[8]{0:T(128)S(1)} %get-tuple-element.124.counts, bf16[8,1024,128]{2,1,0:T(8,128)(2,1)S(1)} %get-tuple-element.88.rows), custom_call_target="tpu_custom_call" | custom-call | tf_op jit(solution)/shard_map/add_rows/pallas_call | solution.py:1085
  208.9 46.8 %norm_parts.1 = (f32[8,128]{1,0:T(8,128)S(1)}, bf16[8,960,128]{2,1,0:T(8,128)(2,1)S(1)}) custom-call(f32[8,128]{1,0:T(8,128)S(1)} %get-tuple-element.89.table_sq, f32[8,128]{1,0:T(8,128)S(1)} %get-tuple-element.90.dense_sq, bf16[960,128]{1,0:T(8,128)(2,1)S(1)} %get-tuple-element.91.dense, f32[8,128]{1,0:T(8,128)S(1)} %get-tuple-element.92.gain), custom_call_target="tpu_custom_call" | custom-call | tf_op jit(solution)/shard_map/norm_parts/pallas_call | solution.py:1095
  255.7 1.3 copy-done.5
  258.3 6.2 %multiply_add_fusion = (f32[4096,128]{1,0:T(8,128)}, f32[4096,128]{1,0:T(8,128)}, f32[4096,128]{1,0:T(8,128)}) fusion(f32[4096,128]{1,0:T(8,128)} %param.38, f32[4096,128]{1,0:T(8,128)} %table.1, f32[4096,128]{1,0:T(8,128)S(1)} %get-tuple-element.94, f32[]{:T(128)S(6)} %min_shard_map.3, f32[4096,128]{1,0:T(8,128)} %param.37), kind=kLoop, calls=%fused_computation.2 | loop fusion | flops 5242880 | bytes 14680068 | tf_op jit(solution)/shard_map/add | solution.py:803
  264.4 1.2 convert_multiply_fusion.4
  267.3 3.1 %multiply_add_fusion.4 = (f32[2,256,3,128]{3,1,2,0:T(8,128)}, f32[2,256,3,128]{3,1,2,0:T(8,128)}, f32[2,256,3,128]{3,1,2,0:T(8,128)}) fusion(f32[2,256,3,128]{3,1,2,0:T(8,128)} %param.47, f32[2,256,3,128]{3,1,2,0:T(8,128)S(1)} %copy-done.25, f32[2,256,3,128]{3,1,2,0:T(8,128)S(1)} %bitcast.118, f32[2,256,3,128]{3,1,2,0:T(8,128)} %param.46), kind=kLoop, calls=%fused_computation.17 | loop fusion | flops 1769472 | bytes 5505024 | tf_op jit(solution)/shard_map/add | solution.py:803
  272.0 1.3 multiply_add_fusion.6
  275.1 2.0 multiply_add_fusion.3
  278.1 1.9 multiply_add_fusion.2
  (114 shorter events, 19.5 us)
Async XLA Ops:
  0.7 50.8 %copy-start.1 = (f32[2,128,256]{2,1,0:T(8,128)S(1)}, f32[2,128,256]{2,1,0:T(8,128)}, u32[]{:S(2)}) copy-start(f32[2,128,256]{2,1,0:T(8,128)} %w_in.3) | copy-start | bytes 786436
  0.7 50.7 %copy-start.39 = (f32[2,256]{1,0:T(2,128)S(1)}, f32[2,256]{1,0:T(2,128)}, u32[]{:S(2)}) copy-start(f32[2,256]{1,0:T(2,128)} %param.42) | copy-start | bytes 6148
  1.6 63.3 %copy-start.22 = (s32[32]{0:T(128)}, s32[32]{0:T(128)S(1)}, u32[]{:S(2)}) copy-start(s32[32]{0:T(128)S(1)} %reshape.159.cnt) | copy-start | bytes 388
  8.3 60.0 %copy-start.44 = (f32[4096]{0:T(1024)S(1)}, f32[4096]{0:T(1024)}, u32[]{:S(2)}) copy-start(f32[4096]{0:T(1024)} %param.35) | copy-start | bytes 49156
  51.4 17.0 %copy-start.45 = (s32[512]{0:T(512)S(1)}, s32[512]{0:T(512)}, u32[]{:S(2)}) copy-start(s32[512]{0:T(512)} %param.33) | copy-start | bytes 6148
  51.4 20.5 %copy-start.43 = (s32[64]{0:T(128)S(1)}, s32[64]{0:T(128)}, u32[]{:S(2)}) copy-start(s32[64]{0:T(128)} %param.34) | copy-start | bytes 772
  51.4 65.9 %copy-start.19 = (f32[2,1,256]{2,1,0:T(1,128)}, f32[2,1,256]{2,1,0:T(1,128)S(1)}, u32[]{:S(2)}) copy-start(f32[2,1,256]{2,1,0:T(1,128)S(1)} %reshape.165.gain) | copy-start | bytes 6148
  68.3 4.3 %copy-start.20 = (bf16[2,16,256]{2,1,0:T(8,128)(2,1)}, bf16[2,16,256]{2,1,0:T(8,128)(2,1)S(1)}, u32[]{:S(2)}) copy-start(bf16[2,16,256]{2,1,0:T(8,128)(2,1)S(1)} %get-tuple-element.66.pooled) | copy-start | bytes 49156
  68.3 50.2 %copy-start.38 = (s32[8,16,128]{2,1,0:T(8,128)S(1)}, s32[8,16,128]{2,1,0:T(8,128)}, u32[]{:S(2)}) copy-start(s32[8,16,128]{2,1,0:T(8,128)} %get-tuple-element.69) | copy-start | bytes 196612
  69.5 3.1 %copy-start.40 = (f32[512]{0:T(512)}, f32[512]{0:T(512)S(1)}, u32[]{:S(2)}) copy-start(f32[512]{0:T(512)S(1)} %select_reduce_fusion) | copy-start | bytes 6148
  118.8 13.7 %copy-start.10 = (bf16[2,4,256,128]{3,2,1,0:T(8,128)(2,1)S(1)}, bf16[2,4,256,128]{3,2,1,0:T(8,128)(2,1)}, u32[]{:S(2)}) copy-start(bf16[2,4,256,128]{3,2,1,0:T(8,128)(2,1)} %get-tuple-element.83) | copy-start | bytes 1572868
  118.8 13.7 %copy-start.11 = (bf16[2,2,512,128]{3,2,1,0:T(8,128)(2,1)S(1)}, bf16[2,2,512,128]{3,2,1,0:T(8,128)(2,1)}, u32[]{:S(2)}) copy-start(bf16[2,2,512,128]{3,2,1,0:T(8,128)(2,1)} %get-tuple-element.80) | copy-start | bytes 1572868
  118.8 13.7 %copy-start.13 = (bf16[2,2,256,128]{3,2,1,0:T(8,128)(2,1)S(1)}, bf16[2,2,256,128]{3,2,1,0:T(8,128)(2,1)}, u32[]{:S(2)}) copy-start(bf16[2,2,256,128]{3,2,1,0:T(8,128)(2,1)} %get-tuple-element.82) | copy-start | bytes 786436
  258.2 7.4 %copy-start.2 = (f32[2,128,256]{2,1,0:T(8,128)S(1)}, f32[2,128,256]{2,1,0:T(8,128)}, u32[]{:S(2)}) copy-start(f32[2,128,256]{2,1,0:T(8,128)} %w_in.3) | copy-start | bytes 786436
  258.2 7.4 %copy-start.34 = (f32[2,128,256]{2,1,0:T(8,128)S(1)}, f32[2,128,256]{2,1,0:T(8,128)}, u32[]{:S(2)}) copy-start(f32[2,128,256]{2,1,0:T(8,128)} %param.41) | copy-start | bytes 786436
  258.2 7.4 %copy-start.35 = (f32[2,128,256]{2,1,0:T(8,128)S(1)}, f32[2,128,256]{2,1,0:T(8,128)}, u32[]{:S(2)}) copy-start(f32[2,128,256]{2,1,0:T(8,128)} %param.40) | copy-start | bytes 786436
  258.2 8.3 %copy-start.41 = (f32[2,256]{1,0:T(2,128)S(1)}, f32[2,256]{1,0:T(2,128)}, u32[]{:S(2)}) copy-start(f32[2,256]{1,0:T(2,128)} %param.44) | copy-start | bytes 6148
  258.3 8.3 %copy-start.42 = (f32[2,256]{1,0:T(2,128)S(1)}, f32[2,256]{1,0:T(2,128)}, u32[]{:S(2)}) copy-start(f32[2,256]{1,0:T(2,128)} %param.43) | copy-start | bytes 6148
  264.4 2.8 copy-start.6
  264.4 2.8 copy-start.25
  267.3 3.1 %copy-start.31 = (f32[2,128,256]{2,1,0:T(8,128)S(1)}, f32[2,128,256]{2,1,0:T(8,128)}, u32[]{:S(2)}) copy-start(f32[2,128,256]{2,1,0:T(8,128)} %w_out.1) | copy-start | bytes 786436
  267.3 3.1 %copy-start.36 = (f32[2,128,256]{2,1,0:T(8,128)S(1)}, f32[2,128,256]{2,1,0:T(8,128)}, u32[]{:S(2)}) copy-start(f32[2,128,256]{2,1,0:T(8,128)} %param.50) | copy-start | bytes 786436
  267.3 3.1 %copy-start.37 = (f32[2,128,256]{2,1,0:T(8,128)S(1)}, f32[2,128,256]{2,1,0:T(8,128)}, u32[]{:S(2)}) copy-start(f32[2,128,256]{2,1,0:T(8,128)} %param.49) | copy-start | bytes 786436
  275.1 3.0 %copy-start.30 = (f32[2,512,256]{2,1,0:T(8,128)S(1)}, f32[2,512,256]{2,1,0:T(8,128)}, u32[]{:S(2)}) copy-start(f32[2,512,256]{2,1,0:T(8,128)} %param.58) | copy-start | bytes 3145732
  (22 other events, 26.7 us)

commit v3 on v2

--- a/solution.py
+++ b/solution.py
@@ -23,6 +23,7 @@
 BF16 = jnp.bfloat16
 I32 = jnp.int32
 VMEM = pl.BlockSpec(memory_space=pltpu.VMEM)
+HBM = pl.BlockSpec(memory_space=pltpu.HBM)
 SMEM = pl.BlockSpec(memory_space=pltpu.SMEM)
 DMA = pltpu.SemaphoreType.DMA
 
@@ -61,8 +62,7 @@
     width = owners * capacity
     his = width // LANES
     sub = iota((owners, LANES), 0)
-    hot = [(owner[c : c + 1, :] == sub).astype(BF16) for c in range(chunks)]
-    hots = jnp.concatenate([h.astype(F32) for h in hot], 0).astype(BF16)
+    hots = jnp.concatenate([(owner[c : c + 1, :] == sub).astype(F32) for c in range(chunks)], 0).astype(BF16)
     before = (iota((LANES, LANES), 0) < iota((LANES, LANES), 1)).astype(BF16)
     earlier = nn(hots, before)
     totals = nn(hots, jnp.ones((LANES, LANES), BF16))
@@ -85,20 +85,35 @@
         right = jnp.concatenate([jnp.where(low, part.astype(F32), 0.0) for part in parts], 0)
         acc = acc + nt(left, right.astype(BF16))
     cuts = [acc[:, k * LANES : (k + 1) * LANES].astype(I32) for k in range(4)]
-    return places, cuts[0] * 64 + cuts[1], cuts[2] * 64 + cuts[3]
-
-
-def prep_kernel(owners, capacity, owner, row, own_owner, own_row, lists, inverse, own_place):
+    totals = [totals[c * owners : (c + 1) * owners] for c in range(chunks)]
+    return places, cuts[0] * 64 + cuts[1], cuts[2] * 64 + cuts[3], totals
+
+
+def prep_kernel(owners, capacity, small, line, owner, row, own_owner, own_row, positive, lists, inverse, own_place, own_small, extra):
     per = capacity // LANES
-    _, rows, tokens = lists_of(owner[...], row[...] + 1, owners, capacity)
-    places, own_rows, _ = lists_of(own_owner[...], own_row[...], owners, capacity)
+    _, rows, tokens, totals = lists_of(owner[...], row[...] + 1, owners, capacity)
+    places, own_rows, _, _ = lists_of(own_owner[...], own_row[...], owners, capacity)
     rows = rows - 1
     inverse[...] = tokens
     for d in range(owners):
         lists[d, 0:per, :] = rows[d * per : (d + 1) * per, :]
         lists[d, per : 2 * per, :] = own_rows[d * per : (d + 1) * per, :]
+    bits = capacity.bit_length() - 1
     for c, place in enumerate(places):
-        own_place[c : c + 1, :] = jnp.where(place < owners * capacity, place, 0)
+        place = jnp.where(place < owners * capacity, place, 0)
+        own_place[c : c + 1, :] = place
+        rank = jnp.minimum(place & (capacity - 1), small - 1)
+        own_small[c : c + 1, :] = lax.shift_right_logical(place, bits) * small + rank
+    cut = len(totals) // line
+    blocks = [sum(totals[m * cut + 1 : (m + 1) * cut], totals[m * cut]) for m in range(line)]
+    most = jnp.zeros((1, LANES), F32)
+    for block in blocks:
+        most = jnp.maximum(most, jnp.max(block, 0, keepdims=True))
+    every = jnp.max(sum(blocks[1:], blocks[0]), 0, keepdims=True)
+    extra[...] = jnp.zeros_like(extra)
+    extra[0:1, 0 : positive.shape[1]] = positive[...]
+    extra[1:2, :] = most.astype(I32)
+    extra[2:3, :] = every.astype(I32)
 
 
 def enter(plane, line):
@@ -134,10 +149,39 @@
     lax.fori_loop(0, target.shape[0] // 16, body, 0)
 
 
+def send_rows(plane, me, part, ids, table, sent, got, wide, out_sems, in_sems):
+    capacity = sent.shape[1]
+    half = ids.shape[1] // 2
+    copies = []
+    for k in range(1, plane):
+        peer = lax.rem(me + k, plane)
+        gather_rows(lambda b, j, peer=peer: ids[peer, half + b, j], table, sent.at[peer])
+        copies.append(send(sent.at[peer], got.at[me], out_sems.at[k], in_sems.at[k], (peer, part)))
+    gather_rows(lambda b, j: ids[me, half + b, j], table, sent.at[me])
+    wide[pl.ds(pl.multiple_of(me * capacity, capacity), capacity), :] = sent[me].astype(F32)
+    return copies
+
+
+def take_rows(plane, me, copies, place, got, wide, out):
+    capacity = got.shape[1]
+    for k in range(1, plane):
+        peer = lax.rem(me - k + plane, plane)
+        copies[k - 1].wait_recv()
+        wide[pl.ds(pl.multiple_of(peer * capacity, capacity), capacity), :] = got[peer].astype(F32)
+    gather_rows(lambda b, j: place[b, j], wide, out)
+
+
+def refetch_kernel(plane, ids, place, table, out, sent, got, wide, out_sems, in_sems):
+    me, part = enter(plane, 0)
+    copies = send_rows(plane, me, part, ids, table, sent, got, wide, out_sems, in_sems)
+    take_rows(plane, me, copies, place, got, wide, out)
+    for copy in copies:
+        copy.wait_send()
+
+
 def fetch_kernel(
     plane,
     line,
-    capacity,
     lists,
     extra,
     place,
@@ -190,14 +234,7 @@
     numbers = pltpu.make_async_copy(got_lists, ids, own_sems.at[2])
     numbers.start()
     numbers.wait()
-    half = capacity // LANES
-    copies = []
-    for k in range(1, plane):
-        peer = lax.rem(me + k, plane)
-        gather_rows(lambda b, j, peer=peer: ids[peer, half + b, j], table, sent.at[peer])
-        copies.append(send(sent.at[peer], got.at[me], out_sems.at[k], in_sems.at[k], (peer, part)))
-    gather_rows(lambda b, j: ids[me, half + b, j], table, sent.at[me])
-    wide[pl.ds(pl.multiple_of(me * capacity, capacity), capacity), :] = sent[me].astype(F32)
+    copies = send_rows(plane, me, part, ids, table, sent, got, wide, out_sems, in_sems)
     near = []
     for k in range(1, line):
         peer = lax.rem(part - k + line, line)
@@ -205,11 +242,7 @@
             far[2 * (k - 1) + j].wait_recv()
             at = block.at[peer, core]
             near.append(send(at, at, near_out.at[j, k], near_in.at[j, k], (sibling, part)))
-    for k in range(1, plane):
-        peer = lax.rem(me - k + plane, plane)
-        copies[k - 1].wait_recv()
-        wide[pl.ds(pl.multiple_of(peer * capacity, capacity), capacity), :] = got[peer].astype(F32)
-    gather_rows(lambda b, j: place[b, j], wide, out)
+    take_rows(plane, me, copies, place, got, wide, out)
     for copy in copies + far:
         copy.wait_send()
     for copy in near:
@@ -347,9 +380,10 @@
     for k in range(1, plane):
         peer = lax.rem(me + k, plane)
         gather_rows(lambda b, j, peer=peer: tokens[peer, b, j], wide, sent.at[peer])
-        copies.append(send(sent.at[peer], out.at[me], out_sems.at[k], in_sems.at[k], (peer, part)))
+        target = out.at[me, 0:capacity]
+        copies.append(send(sent.at[peer], target, out_sems.at[k], in_sems.at[k], (peer, part)))
     gather_rows(lambda b, j: tokens[me, b, j], wide, sent.at[me])
-    own = pltpu.make_async_copy(sent.at[me], out.at[me], own_sem)
+    own = pltpu.make_async_copy(sent.at[me], out.at[me, 0:capacity], own_sem)
     own.start()
     to = 0
     for at, count in split_cuts:
@@ -377,37 +411,55 @@
         copy.wait()
 
 
-def scatter_kernel(capacity, ids, counts, rows, out, square, wide):
-    out[...] = jnp.zeros_like(out)
+def scatter_kernel(ids, counts, rows, out, square, wide, *others):
+    tables = (out, *others)
+    ways = len(tables)
+    for table in tables:
+        table[...] = jnp.zeros_like(table)
+    step = 4 * ways
+
     for d in range(rows.shape[0]):
-        wide[...] = rows[d].astype(F32)
         count = counts[d]
 
-        def one(j):
+        def widen(i, carry):
+            at = pl.ds(pl.multiple_of(i * 64, 64), 64)
+            wide[at, :] = rows[d, at, :].astype(F32)
+            return carry
+
+        lax.fori_loop(0, lax.shift_right_logical(count + 63, 6), widen, 0)
+
+        def body(i, carry):
+            for u in range(0, step, ways):
+                first = i * step + u
+                at = [ids[d, first + n] for n in range(ways)]
+                sums = [
+                    table[pl.ds(at[n], 1), :] + wide[pl.ds(first + n, 1), :] for n, table in enumerate(tables)
+                ]
+                for n, table in enumerate(tables):
+                    table[pl.ds(at[n], 1), :] = sums[n]
+            return carry
+
+        def rest(j, carry):
             at = ids[d, j]
             out[pl.ds(at, 1), :] = out[pl.ds(at, 1), :] + wide[pl.ds(j, 1), :]
-
-        def body(i, carry):
-            for u in range(8):
-                one(i * 8 + u)
             return carry
 
-        def rest(j, carry):
-            one(j)
-            return carry
-
-        full = lax.shift_right_logical(count, 3)
+        full = lax.div(count, step)
         lax.fori_loop(0, full, body, 0)
-        lax.fori_loop(full * 8, count, rest, 0)
+        lax.fori_loop(full * step, count, rest, 0)
 
     def add(i, total):
-        block = out[pl.ds(pl.multiple_of(i * 64, 64), 64), :]
+        at = pl.ds(pl.multiple_of(i * 32, 32), 32)
+        block = out[at, :]
+        for table in others:
+            block = block + table[at, :]
+        out[at, :] = block
         block = block * block
-        for r in range(8):
+        for r in range(4):
             total = total + block[r * 8 : (r + 1) * 8, :]
         return total
 
-    square[...] = lax.fori_loop(0, out.shape[0] // 64, add, jnp.zeros((8, LANES), F32))
+    square[...] = lax.fori_loop(0, out.shape[0] // 32, add, jnp.zeros((8, LANES), F32))
 
 
 def norm_kernel(
@@ -649,9 +701,9 @@
     plane,
     line,
     pooled,
-    w_one,
-    w_two,
-    w_three,
+    far_one,
+    far_two,
+    far_three,
     prior_row,
     prior_col,
     pos_row,
@@ -673,7 +725,17 @@
     in_sems,
     vec_out,
     vec_in,
+    w_one,
+    w_two,
+    w_three,
+    load_sems,
 ):
+    loads = [
+        pltpu.make_async_copy(source, target, load_sems.at[j])
+        for j, (source, target) in enumerate(((far_one, w_one), (far_two, w_two), (far_three, w_three)))
+    ]
+    for copy in loads:
+        copy.start()
     me, part = enter(plane, line)
     towers, own, width = pooled.shape
     rows = own * line
@@ -685,6 +747,8 @@
         send(pooled_all.at[:, part], pooled_all.at[:, part], out_sems.at[0, k], in_sems.at[0, k], (me, peers[k]))
         for k in range(line - 1)
     ]
+    for copy in loads:
+        copy.wait()
     one = [w_one[t].astype(BF16) for t in range(towers)]
     two = [w_two[t].astype(BF16) for t in range(towers)]
     three = [w_three[t].astype(BF16) for t in range(towers)]
@@ -802,6 +866,75 @@
     weight_new = weight - rate * (clipped + MOMENTUM * moment_new)
     average_new = AVERAGE_DECAY * average + (1.0 - AVERAGE_DECAY) * weight_new
     return [weight_new, moment_new, average_new]
+
+
+def update_kernel(blocks, norm_sq, table_grad, dense, gain, *refs):
+    arrays = 3 * 8
+    sources, targets, norm = refs[:arrays], refs[arrays : 2 * arrays], refs[2 * arrays]
+    held, in_sems, out_sems = refs[2 * arrays + 1 : 3 * arrays + 1], refs[-2], refs[-1]
+    loads = [pltpu.make_async_copy(sources[k], held[k], in_sems.at[k]) for k in range(arrays)]
+    for copy in loads:
+        copy.start()
+    norm[...] = jnp.sqrt(norm_sq[...])
+    factor = jnp.minimum(1.0, CLIP_NORM / norm[0:1, :])
+    stores = []
+
+    def finish(k):
+        for j in range(3 * k, 3 * k + 3):
+            copy = pltpu.make_async_copy(held[j], targets[j], out_sems.at[j])
+            copy.start()
+            stores.append(copy)
+
+    def apply(k, rows, lanes, grad, rate):
+        cells = [ref.at[rows, lanes] for ref in held[3 * k : 3 * k + 3]]
+        new = update(cells[0][...], grad, cells[1][...], cells[2][...], factor, rate)
+        for cell, value in zip(cells, new):
+            cell[...] = value
+
+    def wait(k):
+        for copy in loads[3 * k : 3 * k + 3]:
+            copy.wait()
+
+    wait(0)
+
+    def rows(i, carry):
+        at = pl.ds(pl.multiple_of(i * 32, 32), 32)
+        apply(0, at, slice(0, LANES), table_grad[at, :], ROW_RATE)
+        return carry
+
+    lax.fori_loop(0, table_grad.shape[0] // 32, rows, 0, unroll=2)
+    finish(0)
+    at = 0
+    for k, size, height, wide in blocks:
+        wait(k)
+        total = dense.shape[0] * size
+        step = 32 if size % 32 == 0 else 16
+        for first in range(0, total, min(size, height)):
+            count = min(size, height)
+            share, inside = first // size, first % size
+            block, begin = first // height, first % height
+            t, j = block // wide, block % wide
+            top = t * height + begin
+
+            def piece(i, carry):
+                take = pl.ds(pl.multiple_of(at + inside + i * step, 16), step)
+                rows = pl.ds(pl.multiple_of(top + i * step, 16), step)
+                grad = dense[share, take, :].astype(F32)
+                apply(k, rows, slice(j * LANES, (j + 1) * LANES), grad, MATRIX_RATE)
+                return carry
+
+            lax.fori_loop(0, count // step, piece, 0, unroll=2)
+        at += size
+        finish(k)
+    last = 7
+    wait(last)
+    for t in range(held[3 * last].shape[0]):
+        for j in range(held[3 * last].shape[1] // LANES):
+            r = t * (held[3 * last].shape[1] // LANES) + j
+            apply(last, slice(t, t + 1), slice(j * LANES, (j + 1) * LANES), gain[r : r + 1, :], GAIN_RATE)
+    finish(last)
+    for copy in stores:
+        copy.wait()
 
 
 def shards(
@@ -856,27 +989,38 @@
         value = value.reshape(line, own, towers, slots)
         return jnp.transpose(value, (0, 2, 1, 3)).reshape(requests // LANES, LANES)
 
-    owner = ordered(slot_owner)
+    live = jnp.arange(slots)[None, None, :] < slot_count[:, :, None]
+    owner = ordered(jnp.where(live, slot_owner[..., 0], plane))
     row = ordered(slot_row)
     own_chunks = own_requests // LANES
     own_owner = lax.dynamic_slice_in_dim(owner, part * own_chunks, own_chunks, 0)
     own_row = lax.dynamic_slice_in_dim(row, part * own_chunks, own_chunks, 0)
     per = capacity // LANES
-    lists, inverse, own_place = pl.pallas_call(
-        functools.partial(prep_kernel, plane, capacity),
+    small = capacity // 4
+    lists, inverse, own_place, own_small, extra = pl.pallas_call(
+        functools.partial(prep_kernel, plane, capacity, small, line),
         out_shape=[
             shape((plane, 2 * per, LANES), I32),
             shape((plane * per, LANES), I32),
             shape((own_chunks, LANES), I32),
+            shape((own_chunks, LANES), I32),
+            shape((8, LANES), I32),
         ],
-        in_specs=[VMEM] * 4,
-        out_specs=[VMEM] * 3,
-        compiler_params=params(32),
+        in_specs=[VMEM] * 5,
+        out_specs=[VMEM] * 5,
+        compiler_params=params(16),
         name="request_lists",
-    )(owner, row, own_owner, own_row)
-    lone = jnp.pad(positive[None, :], ((0, 7), (0, LANES - batch)))
-    embedded, got_lists, got_pos, wide_qkv, wide_out = pl.pallas_call(
-        functools.partial(fetch_kernel, plane, line, capacity),
+    )(owner, row, own_owner, own_row, positive.reshape(1, batch))
+
+    def row_scratch(count):
+        return [
+            pltpu.VMEM((plane, count, depth), BF16),
+            pltpu.VMEM((plane, count, depth), BF16),
+            pltpu.VMEM((plane * count, depth), F32),
+        ]
+
+    embedded, got_lists, got_extra, wide_qkv, wide_out = pl.pallas_call(
+        functools.partial(fetch_kernel, plane, line),
         out_shape=[
             shape((own_requests, depth), BF16),
             shape(lists.shape, I32),
@@ -888,9 +1032,7 @@
         out_specs=[VMEM] * 5,
         scratch_shapes=[
             pltpu.SMEM(lists.shape, I32),
-            pltpu.VMEM((plane, capacity, depth), BF16),
-            pltpu.VMEM((plane, capacity, depth), BF16),
-            pltpu.VMEM((plane * capacity, depth), F32),
+            *row_scratch(small),
             DMA((2, plane)),
             DMA((2, plane)),
             DMA((plane,)),
@@ -901,9 +1043,23 @@
             DMA((2, line)),
             DMA((3,)),
         ],
-        compiler_params=params(56, collective_id=2, has_side_effects=True),
+        compiler_params=params(16, collective_id=2, has_side_effects=True),
         name="fetch",
-    )(lists, lone, own_place, embedding, jnp.transpose(w_qkv, (0, 2, 1, 3)), w_out)
+    )(lists, extra, own_small, embedding, jnp.transpose(w_qkv, (0, 2, 1, 3)), w_out)
+    most = jnp.max(got_extra[:, 1:3, 0], 0)
+
+    def refetch(ids, place, table, _):
+        return pl.pallas_call(
+            functools.partial(refetch_kernel, plane),
+            out_shape=shape((own_requests, depth), BF16),
+            in_specs=[SMEM, SMEM, VMEM],
+            out_specs=VMEM,
+            scratch_shapes=[*row_scratch(capacity), DMA((plane,)), DMA((plane,))],
+            compiler_params=params(16, collective_id=7, has_side_effects=True),
+            name="refetch",
+        )(ids, place, table)
+
+    embedded = lax.cond(most[0] > small, refetch, lambda *given: given[3], got_lists, own_place, embedding, embedded)
     embedded = embedded.reshape(towers, tokens, depth)
 
     counts = jnp.transpose(slot_count).reshape(towers, line, own)
@@ -936,14 +1092,14 @@
             lead(groups, per_group * heads, LANES),
         ],
         scratch_shapes=[pltpu.VMEM((groups, per_group, line * LANES), F32)],
-        compiler_params=params(48),
+        compiler_params=params(20),
         name="attention_forward",
     )(counts, embedded, w_in, gains, wide_qkv, wide_out)
 
     prior = jnp.sum(
         jnp.where(item_qid[:, None] == jnp.arange(log_prior.shape[0])[None, :], log_prior[None, :], 0.0), 1
     )
-    positions = got_pos[:, 0, :batch].reshape(1, pairs)
+    positions = got_extra[:, 0, :batch].reshape(1, pairs)
     own_positions = lax.dynamic_slice_in_dim(positive, part * own, own, 0).reshape(own, 1)
     dpooled, d_one, d_two, d_three, loss = pl.pallas_call(
         functools.partial(upper_kernel, plane, line),
@@ -954,7 +1110,7 @@
             shape((towers, width // LANES, seconds, LANES), BF16),
             shape((8, LANES), F32),
         ],
-        in_specs=[VMEM] * 8,
+        in_specs=[VMEM] + [HBM] * 3 + [VMEM] * 4,
         out_specs=[VMEM] * 5,
         scratch_shapes=[
             pltpu.VMEM((towers, line, own, width), BF16),
@@ -969,8 +1125,12 @@
             DMA((5, line)),
             DMA((plane,)),
             DMA((plane,)),
+            pltpu.VMEM(w_one.shape, F32),
+            pltpu.VMEM(w_two.shape, F32),
+            pltpu.VMEM(w_three.shape, F32),
+            DMA((3,)),
         ],
-        compiler_params=params(56, collective_id=3, has_side_effects=True),
+        compiler_params=params(22 + 2 * (pairs * pairs >> 18), collective_id=3, has_side_effects=True),
         name="upper",
     )(pooled, w_one, w_two, w_three, prior.reshape(1, pairs), prior.reshape(pairs, 1), positions, own_positions)
 
@@ -1006,7 +1166,7 @@
             pl.BlockSpec((line, 1, width // LANES, LANES, LANES), lambda t: (0, t, 0, 0, 0)),
         ],
         scratch_shapes=[pltpu.VMEM((3 * line, tokens, LANES), BF16)],
-        compiler_params=params(56),
+        compiler_params=params(24),
         name="attention_backward",
     )(counts, embedded, w_in, gains, wide_qkv, wide_out, normed, qkv, prob, spread, pm, dpooled)
 
@@ -1043,7 +1203,7 @@
             DMA((plane,)),
             DMA,
         ],
-        compiler_params=params(48, collective_id=4, has_side_effects=True),
+        compiler_params=params(20, collective_id=4, has_side_effects=True),
         name="spread",
     )(demb.reshape(own_requests, depth), *grads, gain_rows)
     whole_at = line * (sizes[0] + sizes[1])
@@ -1055,40 +1215,53 @@
         (whole_at + whole_rows, last_rows),
     )
     line_rows = sizes[0] + sizes[1] + whole_rows
-    incoming, dense, dense_sq, gain_all = pl.pallas_call(
-        functools.partial(return_kernel, plane, line, capacity, cuts),
-        out_shape=[
-            shape((plane, capacity, depth), BF16),
-            shape((line_rows + last_rows, LANES), BF16),
-            shape((8, LANES), F32),
-            shape((8, LANES), F32),
-        ],
-        in_specs=[SMEM, VMEM, VMEM, VMEM],
-        out_specs=[VMEM] * 4,
-        scratch_shapes=[
-            pltpu.VMEM((requests, depth), F32),
-            pltpu.VMEM((plane, capacity, depth), BF16),
-            pltpu.VMEM((line, line_rows, LANES), BF16),
-            pltpu.VMEM((line, 8, LANES), F32),
-            DMA((plane,)),
-            DMA((plane,)),
-            DMA((3, line)),
-            DMA((3, line)),
-            DMA((line,)),
-            DMA((line,)),
-            DMA,
-        ],
-        compiler_params=params(48, collective_id=5, has_side_effects=True),
-        name="return_rows",
-    )(inverse.reshape(plane, per, LANES), every.reshape(requests, depth), summed, gain_sum)
+
+    def give_back(count, number):
+        return lambda *given: pl.pallas_call(
+            functools.partial(return_kernel, plane, line, count, cuts),
+            out_shape=[
+                shape((plane, capacity, depth), BF16),
+                shape((line_rows + last_rows, LANES), BF16),
+                shape((8, LANES), F32),
+                shape((8, LANES), F32),
+            ],
+            in_specs=[SMEM, VMEM, VMEM, VMEM],
+            out_specs=[VMEM] * 4,
+            scratch_shapes=[
+                pltpu.VMEM((requests, depth), F32),
+                pltpu.VMEM((plane, count, depth), BF16),
+                pltpu.VMEM((line, line_rows, LANES), BF16),
+                pltpu.VMEM((line, 8, LANES), F32),
+                DMA((plane,)),
+                DMA((plane,)),
+                DMA((3, line)),
+                DMA((3, line)),
+                DMA((line,)),
+                DMA((line,)),
+                DMA,
+            ],
+            compiler_params=params(16, collective_id=number, has_side_effects=True),
+            name="return_rows",
+        )(*given)
+
+    medium = capacity * 5 // 8
+    incoming, dense, dense_sq, gain_all = lax.cond(
+        most[1] > medium,
+        give_back(capacity, 8),
+        give_back(medium, 5),
+        inverse.reshape(plane, per, LANES),
+        every.reshape(requests, depth),
+        summed,
+        gain_sum,
+    )
     served = got_lists[:, :per, :].reshape(plane, capacity)
     table_grad, table_sq = pl.pallas_call(
-        functools.partial(scatter_kernel, capacity),
+        scatter_kernel,
         out_shape=[shape(embedding.shape, F32), shape((8, LANES), F32)],
         in_specs=[SMEM, SMEM, VMEM],
         out_specs=[VMEM, VMEM],
-        scratch_shapes=[pltpu.VMEM((capacity, depth), F32)],
-        compiler_params=params(48),
+        scratch_shapes=[pltpu.VMEM((capacity, depth), F32)] + [pltpu.VMEM(embedding.shape, F32)] * 3,
+        compiler_params=params(20),
         name="add_rows",
     )(jnp.maximum(served, 0), jnp.sum((served >= 0).astype(I32), 1), incoming)
 
@@ -1110,30 +1283,35 @@
             DMA((plane // 2,)),
             DMA,
         ],
-        compiler_params=params(32, collective_id=6, has_side_effects=True),
+        compiler_params=params(12, collective_id=6, has_side_effects=True),
         name="norm_parts",
     )(table_sq, dense_sq, dense, gain_all)
-    norm = jnp.sqrt(norm_sq[0, 0])
-    factor = jnp.minimum(1.0, CLIP_NORM / norm)
-    found, at = [], 0
-    for size in sizes:
-        found.append(dense_all[:, at : at + size].astype(F32))
-        at += size
-    d_qkv = jnp.transpose(found[0].reshape(towers, 3, width, LANES), (0, 2, 1, 3))
-    side = lambda grad, rows: jnp.transpose(grad.reshape(towers, -1, rows, LANES), (0, 2, 1, 3)).reshape(towers, rows, -1)
-    d_out, d_three, d_in = side(found[1], LANES), side(found[2], seconds), side(found[3], depth)
-    d_one, d_two = side(found[4], width), side(found[5], units)
-    d_gain = gain_all[: d_gain.size // LANES].reshape(towers, width)
-    done = []
-    done.extend(update(embedding, table_grad, embedding_mom, embedding_avg, factor, ROW_RATE))
-    done.extend(update(w_in, d_in, w_in_mom, w_in_avg, factor, MATRIX_RATE))
-    done.extend(update(norm_gain, d_gain, norm_gain_mom, norm_gain_avg, factor, GAIN_RATE))
-    done.extend(update(w_qkv, d_qkv, w_qkv_mom, w_qkv_avg, factor, MATRIX_RATE))
-    done.extend(update(w_out, d_out, w_out_mom, w_out_avg, factor, MATRIX_RATE))
-    done.extend(update(w_one, d_one, w_one_mom, w_one_avg, factor, MATRIX_RATE))
-    done.extend(update(w_two, d_two, w_two_mom, w_two_avg, factor, MATRIX_RATE))
-    done.extend(update(w_three, d_three, w_three_mom, w_three_avg, factor, MATRIX_RATE))
-    return (loss[0, 0], norm, *done)
+    flat = lambda w: w.reshape(-1, w.shape[-1])
+    turn = lambda w: flat(jnp.transpose(w, (0, 2, 1, 3)))
+    given = [embedding, embedding_mom, embedding_avg]
+    given += [turn(w) for w in (w_qkv, w_qkv_mom, w_qkv_avg)]
+    rest = (w_out, w_out_mom, w_out_avg, w_three, w_three_mom, w_three_avg, w_in, w_in_mom, w_in_avg)
+    rest += (w_one, w_one_mom, w_one_avg, w_two, w_two_mom, w_two_avg)
+    given += [flat(w) for w in rest]
+    given += [norm_gain, norm_gain_mom, norm_gain_avg]
+    heights = (towers * 3 * width, LANES, seconds, depth, width, units)
+    wides = (1, width // LANES, width // LANES, width // LANES, units // LANES, seconds // LANES)
+    blocks = tuple((k + 1, size, height, wide) for k, (size, height, wide) in enumerate(zip(sizes, heights, wides)))
+    *done, norm = pl.pallas_call(
+        functools.partial(update_kernel, blocks),
+        out_shape=[shape(w.shape, F32) for w in given] + [shape((8, LANES), F32)],
+        in_specs=[VMEM] * 4 + [HBM] * len(given),
+        out_specs=[HBM] * len(given) + [VMEM],
+        scratch_shapes=[pltpu.VMEM(w.shape, F32) for w in given] + [DMA((len(given),))] * 2,
+        compiler_params=params(57),
+        name="update",
+    )(norm_sq, table_grad, dense_all, gain_all, *given)
+    back = lambda k, w: [done[3 * k + j].reshape(w.shape) for j in range(3)]
+    unturned = [
+        jnp.transpose(w.reshape(towers, 3, width, LANES), (0, 2, 1, 3)) for w in done[3:6]
+    ]
+    new = done[:3] + back(4, w_in) + done[21:24] + unturned + back(2, w_out) + back(5, w_one) + back(6, w_two)
+    return (loss[0, 0], norm[0, 0], *new, *back(3, w_three))
 
 
 def solution(mesh):

time: 282 us -> 209 us (0.74)
  Pallas kernels: 232 us -> 190 us
  other arithmetic: 19.8 us -> 2.38 us
  local copies, waits for them, and re-layouts: 26.4 us -> 14.2 us
    pallas_call x1, Pallas kernels: 46.8 us -> 28.5 us  [shards(): pl.pallas_call(functools.partial(norm_kernel, plane, line), out_shape=[sh...]
    add x8 -> x0, other arithmetic: 16.9 us -> none  [update(): average_new = AVERAGE_DECAY * average + (1.0 - AVERAGE_DECAY) * weight_new]
    pallas_call x4 -> x5, Pallas kernels: 89.9 us -> 75.5 us  [the longest x1 30.7 us: shards(): pl.pallas_call(functools.partial(fetch_kernel, plane, line), out_shape=[s...]
    unnamed x95 -> x31, local copies, waits for them, and re-layouts: 18.6 us -> 7.68 us
    pallas_call x1, Pallas kernels: 44.7 us -> 38.4 us  [shards(): pl.pallas_call(functools.partial(upper_kernel, plane, line), out_shape=[s...]
where the time goes in v3:
time: 209 us; the launch traced here: 210 us
  Pallas kernels  190 us (91%)
  local copies, waits for them, and re-layouts  14.2 us (7%)
  other arithmetic  2.38 us (1%)
  between operations  2.24 us (1%)
    pallas_call x1, Pallas kernels, shards(): pl.pallas_call(functools.partial(upper_kernel, plane, line), out_shape=[s...  38.4 us
    pallas_call x1, Pallas kernels, shards(): pl.pallas_call(functools.partial(fetch_kernel, plane, line), out_shape=[s...  30.7 us
    pallas_call x1, Pallas kernels, shards(): pl.pallas_call(functools.partial(norm_kernel, plane, line), out_shape=[sh...  28.5 us
    pallas_call x1, Pallas kernels, shards(): pl.pallas_call(functools.partial(spread_kernel, plane, line), out_shape=[...  28 us
    pallas_call x1, Pallas kernels, give_back(): pl.pallas_call(functools.partial(return_kernel, plane, line, count, cuts)...  21.8 us
    pallas_call x1, Pallas kernels, shards(): pl.pallas_call(functools.partial(update_kernel, blocks), out_shape=[shape...  14.2 us
    pallas_call x1, Pallas kernels, shards(): pl.pallas_call(functools.partial(backward_kernel, slots), grid=(towers,),...  10.3 us
    pallas_call x1, Pallas kernels, shards(): pl.pallas_call(functools.partial(forward_kernel, slots), grid=(towers,),...  9.72 us

profile of v3, /device:TPU:0, one launch (start us, length us, event | category | flops | bytes accessed | tf_op | source)
XLA Modules:
  0.0 209.6 jit_solution(16419998820940674508)
XLA Ops:
  0.7 0.7 dynamic-slice_bitcast_fusion
  1.4 1.9 select_reduce_fusion
  3.3 0.7 reshape.250.gain
  4.0 0.8 reshape.244
  4.9 0.8 lt.29
  5.7 0.8 copy.66
  6.8 0.8 copy.68
  8.4 2.5 %request_lists.1 = (s32[8,16,128]{2,1,0:T(8,128)S(1)}, s32[64,128]{1,0:T(8,128)}, s32[8,128]{1,0:T(8,128)S(1)}, s32[8,128]{1,0:T(8,128)S(1)}, s32[8,128]{1,0:T(8,128)S(1)}) custom-call(s32[32,128]{1,0:T(8,128)S(1)} %reshape.246.owner, s32[32,128]{1,0:T(8,128)S(1)} %reshape.248.row, s32[8,128]{1,0:T(8,128)S(1)} %get-tuple-element.197.own_owner, ...), custom_call_target="tpu_custom_call" | custom-call | tf_op jit(solution)/shard_map/request_lists/pallas_call | solution.py:1000
  10.9 0.9 copy.70.prior_col
  11.8 1.1 copy-done.2
  12.9 0.9 copy-done.7
  13.8 30.7 %fetch.1 = (bf16[1024,128]{1,0:T(8,128)(2,1)}, s32[8,16,128]{2,1,0:T(8,128)S(1)}, s32[8,8,128]{2,1,0:T(8,128)S(1)}, bf16[4,2,3,256,128]{4,3,2,1,0:T(8,128)(2,1)S(1)}, bf16[4,2,128,256]{3,2,1,0:T(8,128)(2,1)S(1)}) custom-call(s32[8,16,128]{2,1,0:T(8,128)S(1)} %get-tuple-element.130.lists, s32[8,128]{1,0:T(8,128)S(1)} %get-tuple-element.131.extra, ...), custom_call_target="tpu_custom_call" | custom-call | tf_op jit(solution)/shard_map/fetch/pallas_call | solution.py:1022
  47.2 9.7 %attention_forward.1 = (bf16[2,16,256]{2,1,0:T(8,128)(2,1)S(1)}, bf16[2,16,512]{2,1,0:T(8,128)(2,1)S(1)}, bf16[2,512,256]{2,1,0:T(8,128)(2,1)S(1)}, bf16[2,12,51...) custom-call(s32[32]{0:T(128)S(1)} %reshape.245.cnt, ...), custom_call_target="tpu_custom_call" | custom-call | tf_op jit(solution)/shard_map/attention_forward/pallas_call | solution.py:1074
  57.0 38.4 %upper.1 = (bf16[2,16,256]{2,1,0:T(8,128)(2,1)S(1)}, bf16[2,2,256,128]{3,2,1,0:T(8,128)(2,1)S(1)}, bf16[2,4,256,128]{3,2,1,0:T(8,128)(2,1)S(1)}, bf16[2,2,512,128]{3,2,1,0:T(8,128)(2,1)S(1)}, f32[8,128]{1,0:T(8,128)S(1)}) custom-call(bf16[2,16,256]{2,1,0:T(8,128)(2,1)S(1)} %get-tuple-element.139.pooled, f32[2,256,256]{2,1,0:T(8,128)S(1)} %copy-done.5, ...), custom_call_target="tpu_custom_call" | custom-call | tf_op jit(solution)/shard_map/upper/pallas_call | solution.py:1104
  95.4 10.3 %attention_backward.1 = (bf16[2,512,128]{2,1,0:T(8,128)(2,1)S(1)}, bf16[2,2,128,128]{3,2,1,0:T(8,128)(2,1)S(1)}, f32[2,1,256]{2,1,0:T(1,128)S(1)}, bf16[4,2,3,25...) custom-call(s32[32]{0:T(128)S(1)} %reshape.245.cnt, bf16[2,512,128]{2,1,0:T(8,128)(2,1)S(1)} %copy-done.12, ...), custom_call_target="tpu_custom_call" | custom-call | tf_op jit(solution)/shard_map/attention_backward/pallas_call | solution.py:1137
  106.3 28.0 %spread.1 = (bf16[4,1024,128]{2,1,0:T(8,128)(2,1)S(1)}, bf16[1728,128]{1,0:T(8,128)(2,1)S(1)}, f32[8,128]{1,0:T(8,128)S(1)}) custom-call(bf16[1024,128]{1,0:T(8,128)(2,1)S(1)} %bitcast.99, bf16[4,4,2,192,128]{4,3,2,1,0:T(8,128)(2,1)S(1)} %bitcast.93, bf16[4,4,2,64,128]{4,3,2,1,0:T(8,128)(2,1)S(1)} %bitcast.97, bf16[4,2,256,128]{3,2,1,0:T(8,128)(2,1)S(1)} %bitcast.96, ...), custom_call_target="tpu_custom_call" | custom-call | tf_op jit(solution)/shard_map/spread/pallas_call | solution.py:1181
  134.3 22.1 %conditional.3 = ((bf16[8,1024,128]{2,1,0:T(8,128)(2,1)}, bf16[960,128]{1,0:T(8,128)(2,1)S(1)}, f32[8,128]{1,0:T(8,128)S(1)}, f32[8,128]{1,0:T(8,128)S(1)})) conditional(s32[]{:T(128)} %bitcast.14, (s32[8,8,128]{2,1,0:T(8,128)S(1)}, bf16[4096,128]{1,0:T(8,128)(2,1)S(1)}, bf16[1728,128]{1,0:T(8,128)(2,1)S(1)}, f32[8,128]{1,0:T(8,128)S(1)}) %tuple.41, ...), branch_computations={%region_5.6_spmd, %region_6.7_spmd} | conditional | bytes 8 | solution.py:1248
  134.3 21.8 %return_rows.2 = (bf16[8,1024,128]{2,1,0:T(8,128)(2,1)}, bf16[960,128]{1,0:T(8,128)(2,1)S(1)}, f32[8,128]{1,0:T(8,128)S(1)}, f32[8,128]{1,0:T(8,128)S(1)}) custom-call(s32[8,8,128]{2,1,0:T(8,128)S(1)} %get-tuple-element.34.tokens, bf16[4096,128]{1,0:T(8,128)(2,1)S(1)} %get-tuple-element.35.rows, bf16[1728,128]{1,0:T(8,128)(2,1)S(1)} %get-tuple-element.36.summed, ...), custom_call_target="tpu_custom_call" | custom-call | tf_op jit(solution)/shard_map/cond/branch_0_fun/return_rows/pallas_call | solution.py:1220
  156.3 6.3 %add_rows.1 = (f32[4096,128]{1,0:T(8,128)S(1)}, f32[8,128]{1,0:T(8,128)S(1)}) custom-call(s32[8,1024]{1,0:T(8,128)S(1)} %bitcast.100, s32[8]{0:T(128)S(1)} %get-tuple-element.192.counts, bf16[8,1024,128]{2,1,0:T(8,128)(2,1)} %get-tuple-element.159.rows), custom_call_target="tpu_custom_call" | custom-call | tf_op jit(solution)/shard_map/add_rows/pallas_call | solution.py:1258
  162.6 1.3 copy-done.4
  163.9 28.5 %norm_parts.1 = (f32[8,128]{1,0:T(8,128)S(1)}, bf16[8,960,128]{2,1,0:T(8,128)(2,1)S(1)}) custom-call(f32[8,128]{1,0:T(8,128)S(1)} %get-tuple-element.160.table_sq, f32[8,128]{1,0:T(8,128)S(1)} %get-tuple-element.161.dense_sq, bf16[960,128]{1,0:T(8,128)(2,1)S(1)} %get-tuple-element.162.dense, f32[8,128]{1,0:T(8,128)S(1)} %get-tuple-element.163.gain), custom_call_target="tpu_custom_call" | custom-call | tf_op jit(solution)/shard_map/norm_parts/pallas_call | solution.py:1268
  192.4 1.3 copy-done.6
  194.3 14.2 %update.1 = (f32[4096,128]{1,0:T(8,128)}, f32[4096,128]{1,0:T(8,128)}, f32[4096,128]{1,0:T(8,128)}, f32[1536,128]{1,0:T(8,128)}, f32[1536,128]{1,0:T(8,128)}, /*...) custom-call(f32[8,128]{1,0:T(8,128)} %copy-done.9, ...), custom_call_target="tpu_custom_call" | custom-call | tf_op jit(solution)/shard_map/update/pallas_call | solution.py:1300
  208.5 1.2 slice.27
  (42 shorter events, 3.5 us)
Async XLA Ops:
  7.7 0.7 copy-start.10
  11.8 1.1 copy-start.2
  12.9 0.9 copy-start.7
  44.6 2.6 %copy-start.3 = (f32[2,128,256]{2,1,0:T(8,128)S(1)}, f32[2,128,256]{2,1,0:T(8,128)}, u32[]{:S(2)}) copy-start(f32[2,128,256]{2,1,0:T(8,128)} %w_in.3) | copy-start | bytes 786436
  46.7 10.2 %copy-start = (f32[2,256,512]{2,1,0:T(8,128)S(1)}, f32[2,256,512]{2,1,0:T(8,128)}, u32[]{:S(2)}) copy-start(f32[2,256,512]{2,1,0:T(8,128)} %far_two.1) | copy-start | bytes 3145732
  46.9 10.0 %copy-start.1 = (f32[2,512,256]{2,1,0:T(8,128)S(1)}, f32[2,512,256]{2,1,0:T(8,128)}, u32[]{:S(2)}) copy-start(f32[2,512,256]{2,1,0:T(8,128)} %far_three.1) | copy-start | bytes 3145732
  46.9 10.0 %copy-start.5 = (f32[2,256,256]{2,1,0:T(8,128)S(1)}, f32[2,256,256]{2,1,0:T(8,128)}, u32[]{:S(2)}) copy-start(f32[2,256,256]{2,1,0:T(8,128)} %far_one.1) | copy-start | bytes 1572868
  46.9 10.0 %copy-start.8 = (f32[512,1]{1,0:T(8,128)S(1)}, f32[512,1]{1,0:T(8,128)}, u32[]{:S(2)}) copy-start(f32[512,1]{1,0:T(8,128)} %copy.70.prior_col) | copy-start | bytes 6148
  56.9 38.5 %copy-start.12 = (bf16[2,512,128]{2,1,0:T(8,128)(2,1)S(1)}, bf16[2,512,128]{2,1,0:T(8,128)(2,1)}, u32[]{:S(2)}) copy-start(bf16[2,512,128]{2,1,0:T(8,128)(2,1)} %get-tuple-element.206.x) | copy-start | bytes 786436
  105.8 28.5 %copy-start.13 = (s32[64,128]{1,0:T(8,128)S(1)}, s32[64,128]{1,0:T(8,128)}, u32[]{:S(2)}) copy-start(s32[64,128]{1,0:T(8,128)} %get-tuple-element.141) | copy-start | bytes 98308
  134.3 60.0 %copy-start.11 = (f32[4096,128]{1,0:T(8,128)S(1)}, f32[4096,128]{1,0:T(8,128)}, u32[]{:S(2)}) copy-start(f32[4096,128]{1,0:T(8,128)} %refs_0_.1) | copy-start | bytes 6291460
  162.6 1.3 copy-start.4
  192.4 1.3 copy-start.6
  193.7 0.6 copy-start.9

commit v4 on v3

--- a/solution.py
+++ b/solution.py
@@ -57,12 +57,13 @@
     return pltpu.CompilerParams(vmem_limit_bytes=limit << 20, **more)
 
 
-def lists_of(owner, row, owners, capacity):
+def lists_of(owner, values, owners, capacity):
     chunks = owner.shape[0]
     width = owners * capacity
     his = width // LANES
     sub = iota((owners, LANES), 0)
-    hots = jnp.concatenate([(owner[c : c + 1, :] == sub).astype(F32) for c in range(chunks)], 0).astype(BF16)
+    hot = [(owner[c : c + 1, :] == sub).astype(F32) for c in range(chunks)]
+    hots = jnp.concatenate(hot, 0).astype(BF16)
     before = (iota((LANES, LANES), 0) < iota((LANES, LANES), 1)).astype(BF16)
     earlier = nn(hots, before)
     totals = nn(hots, jnp.ones((LANES, LANES), BF16))
@@ -70,49 +71,67 @@
     places = []
     for c in range(chunks):
         cut = slice(c * owners, (c + 1) * owners)
-        at = hots[cut].astype(F32) * (earlier[cut] + base)
-        here = jnp.sum(at, 0, keepdims=True).astype(I32)
+        here = jnp.sum(hot[c] * (earlier[cut] + base), 0, keepdims=True).astype(I32)
         places.append(jnp.where(owner[c : c + 1, :] < owners, here, width))
         base = base + totals[cut]
-    acc = jnp.zeros((his, 4 * LANES), F32)
+    parts = 2 * len(values)
+    acc = jnp.zeros((his, parts * LANES), F32)
     for c in range(chunks):
         place = places[c]
-        value = row[c : c + 1, :]
-        token = iota((1, LANES), 1) + c * LANES
         left = (lax.shift_right_logical(place, 7) == iota((his, LANES), 0)).astype(BF16)
         low = (place & 127) == iota((LANES, LANES), 0)
-        parts = [lax.shift_right_logical(value, 6), value & 63, lax.shift_right_logical(token, 6), token & 63]
-        right = jnp.concatenate([jnp.where(low, part.astype(F32), 0.0) for part in parts], 0)
+        cuts = []
+        for value in values:
+            value = value[c : c + 1, :]
+            cuts += [lax.shift_right_logical(value, 6), value & 63]
+        right = jnp.concatenate([jnp.where(low, cut.astype(F32), 0.0) for cut in cuts], 0)
         acc = acc + nt(left, right.astype(BF16))
-    cuts = [acc[:, k * LANES : (k + 1) * LANES].astype(I32) for k in range(4)]
-    totals = [totals[c * owners : (c + 1) * owners] for c in range(chunks)]
-    return places, cuts[0] * 64 + cuts[1], cuts[2] * 64 + cuts[3], totals
-
-
-def prep_kernel(owners, capacity, small, line, owner, row, own_owner, own_row, positive, lists, inverse, own_place, own_small, extra):
+    cuts = [acc[:, k * LANES : (k + 1) * LANES].astype(I32) for k in range(parts)]
+    lists = [cuts[2 * k] * 64 + cuts[2 * k + 1] for k in range(len(values))]
+    return places, lists, hot
+
+
+def log2(value):
+    return value.bit_length() - 1
+
+
+def prep_kernel(
+    owners, capacity, small, line, owner_in, row_in, count, positive, lists, inverse, own_place, own_small, extra
+):
+    towers, slots, batch = owner_in.shape
+    own = batch // line
     per = capacity // LANES
-    _, rows, tokens, totals = lists_of(owner[...], row[...] + 1, owners, capacity)
-    places, own_rows, _, _ = lists_of(own_owner[...], own_row[...], owners, capacity)
+    side = lambda ref: jnp.concatenate([ref[t] for t in range(towers)], 1)
+    counts = jnp.concatenate([count[t : t + 1, :] for t in range(towers)], 1)
+    row = side(row_in)
+    slot, lane = iota((slots, LANES), 0), iota((slots, LANES), 1)
+    owner = jnp.where(slot < counts, side(owner_in), owners)
+    tower = lax.shift_right_logical(lane, log2(batch))
+    block = lax.shift_right_logical(lane & (batch - 1), log2(own))
+    token = ((block * towers + tower) * own + (lane & (own - 1))) * slots + slot
+    _, (rows, tokens), hot = lists_of(owner, (row + 1, token), owners, capacity)
+    own_owner = jnp.where(block == lax.axis_index("mp"), owner, owners)
+    places, (own_rows,), _ = lists_of(own_owner, (row,), owners, capacity)
     rows = rows - 1
     inverse[...] = tokens
     for d in range(owners):
         lists[d, 0:per, :] = rows[d * per : (d + 1) * per, :]
         lists[d, per : 2 * per, :] = own_rows[d * per : (d + 1) * per, :]
-    bits = capacity.bit_length() - 1
-    for c, place in enumerate(places):
-        place = jnp.where(place < owners * capacity, place, 0)
-        own_place[c : c + 1, :] = place
-        rank = jnp.minimum(place & (capacity - 1), small - 1)
-        own_small[c : c + 1, :] = lax.shift_right_logical(place, bits) * small + rank
-    cut = len(totals) // line
-    blocks = [sum(totals[m * cut + 1 : (m + 1) * cut], totals[m * cut]) for m in range(line)]
-    most = jnp.zeros((1, LANES), F32)
-    for block in blocks:
-        most = jnp.maximum(most, jnp.max(block, 0, keepdims=True))
-    every = jnp.max(sum(blocks[1:], blocks[0]), 0, keepdims=True)
+    place = jnp.concatenate(places, 0)
+    place = jnp.where(place < owners * capacity, place, 0)
+    own_place[...] = place
+    rank = jnp.minimum(place & (capacity - 1), small - 1)
+    own_small[...] = lax.shift_right_logical(place, log2(capacity)) * small + rank
+    asked = hot[0]
+    for more in hot[1:]:
+        asked = asked + more
+    near = lax.shift_right_logical(iota((LANES, LANES), 0) & (batch - 1), log2(own)) == iota((LANES, LANES), 1)
+    asked = asked.astype(BF16)
+    most = jnp.max(jnp.max(nn(asked, near.astype(BF16)), 0, keepdims=True), 1, keepdims=True)
+    every = jnp.max(nn(asked, jnp.ones((LANES, LANES), BF16)), 0, keepdims=True)
     extra[...] = jnp.zeros_like(extra)
-    extra[0:1, 0 : positive.shape[1]] = positive[...]
-    extra[1:2, :] = most.astype(I32)
+    extra[0:1, 0:batch] = positive[...]
+    extra[1:2, :] = jnp.broadcast_to(most, (1, LANES)).astype(I32)
     extra[2:3, :] = every.astype(I32)
 
 
@@ -136,17 +155,35 @@
 
 
 def gather_rows(ids, table, target):
-    per = LANES // 16
-
     def body(i, carry):
-        at = pl.multiple_of(i * 16, 16)
-        block = lax.shift_right_logical(i, 3)
-        first = (i & (per - 1)) * 16
-        rows = [table[pl.ds(ids(block, first + u), 1), :] for u in range(16)]
-        target[pl.ds(at, 16), :] = jnp.concatenate(rows, 0).astype(BF16)
+        at = ids(i)
+        rows = [table[pl.ds(at(u), 1), :] for u in range(16)]
+        target[pl.ds(pl.multiple_of(i * 16, 16), 16), :] = jnp.concatenate(rows, 0).astype(BF16)
         return carry
 
     lax.fori_loop(0, target.shape[0] // 16, body, 0)
+
+
+def listed(ids, first):
+    def at(i):
+        block = first + lax.shift_right_logical(i, 3)
+        start = (i & 7) * 16
+        return lambda u: ids[block, start + u]
+
+    return at
+
+
+def placed(place, part, towers, own, slots):
+    per = slots // 16
+
+    def at(i):
+        pair = lax.shift_right_logical(i, log2(per))
+        tower = lax.shift_right_logical(pair, log2(own))
+        lane = tower * (LANES // towers) + part * own + (pair & (own - 1))
+        start = (i & (per - 1)) * 16
+        return lambda u: place[start + u, lane]
+
+    return at
 
 
 def send_rows(plane, me, part, ids, table, sent, got, wide, out_sems, in_sems):
@@ -155,26 +192,26 @@
     copies = []
     for k in range(1, plane):
         peer = lax.rem(me + k, plane)
-        gather_rows(lambda b, j, peer=peer: ids[peer, half + b, j], table, sent.at[peer])
+        gather_rows(listed(ids.at[peer], half), table, sent.at[peer])
         copies.append(send(sent.at[peer], got.at[me], out_sems.at[k], in_sems.at[k], (peer, part)))
-    gather_rows(lambda b, j: ids[me, half + b, j], table, sent.at[me])
+    gather_rows(listed(ids.at[me], half), table, sent.at[me])
     wide[pl.ds(pl.multiple_of(me * capacity, capacity), capacity), :] = sent[me].astype(F32)
     return copies
 
 
-def take_rows(plane, me, copies, place, got, wide, out):
+def take_rows(plane, me, part, dims, copies, place, got, wide, out):
     capacity = got.shape[1]
     for k in range(1, plane):
         peer = lax.rem(me - k + plane, plane)
         copies[k - 1].wait_recv()
         wide[pl.ds(pl.multiple_of(peer * capacity, capacity), capacity), :] = got[peer].astype(F32)
-    gather_rows(lambda b, j: place[b, j], wide, out)
-
-
-def refetch_kernel(plane, ids, place, table, out, sent, got, wide, out_sems, in_sems):
+    gather_rows(placed(place, part, *dims), wide, out)
+
+
+def refetch_kernel(plane, dims, ids, place, table, out, sent, got, wide, out_sems, in_sems):
     me, part = enter(plane, 0)
     copies = send_rows(plane, me, part, ids, table, sent, got, wide, out_sems, in_sems)
-    take_rows(plane, me, copies, place, got, wide, out)
+    take_rows(plane, me, part, dims, copies, place, got, wide, out)
     for copy in copies:
         copy.wait_send()
 
@@ -182,6 +219,7 @@
 def fetch_kernel(
     plane,
     line,
+    dims,
     lists,
     extra,
     place,
@@ -242,7 +280,7 @@
             far[2 * (k - 1) + j].wait_recv()
             at = block.at[peer, core]
             near.append(send(at, at, near_out.at[j, k], near_in.at[j, k], (sibling, part)))
-    take_rows(plane, me, copies, place, got, wide, out)
+    take_rows(plane, me, part, dims, copies, place, got, wide, out)
     for copy in copies + far:
         copy.wait_send()
     for copy in near:
@@ -333,32 +371,74 @@
     gain_sum[...] = total
 
 
-def return_kernel(
+def add_rows(ids, count, blocks, grads, total, fresh):
+    height = total.shape[0]
+    rows = []
+    for block in blocks:
+        for r in range(-(-count // LANES)):
+            rows.append(ids[block, r : r + 1, 0 : min(LANES, count - r * LANES)])
+    numbers = jnp.concatenate(rows, 1)
+    values = jnp.concatenate([ref[...] for ref in grads], 0)
+    turned = jnp.transpose(jnp.broadcast_to(numbers.astype(F32), (8, numbers.shape[1])), (1, 0))[:, 0:1]
+    upper = turned >= height
+    none = jnp.zeros_like(values)
+    values = jnp.concatenate([jnp.where(upper, none, values), jnp.where(upper, values, none)], 1)
+    low = jnp.where(numbers >= 0, numbers & (height - 1), -1)
+    step = min(height, 1024)
+
+    def body(i, carry):
+        at = pl.multiple_of(i * step, step)
+        hot = jnp.where(low - at == iota((step, low.shape[1]), 0), 1.0, 0.0).astype(BF16)
+        part = nn(hot, values)
+        at = pl.ds(at, step)
+        total[at, :] = part if fresh else total[at, :] + part
+        return carry
+
+    lax.fori_loop(0, height // step, body, 0)
+
+
+def tail_kernel(
     plane,
     line,
     capacity,
     cuts,
     tokens,
+    ids,
     rows,
     summed,
     gain,
-    out,
-    dense,
-    dense_sq,
+    table,
+    dense_all,
+    norm_sq,
     gain_all,
     wide,
     sent,
+    back,
+    total,
     got,
     gains,
+    along,
+    across,
     out_sems,
     in_sems,
     far_out,
     far_in,
     gain_out,
     gain_in,
-    own_sem,
+    along_out,
+    along_in,
+    across_out,
+    across_in,
+    chip_out,
+    chip_in,
+    near_out,
+    near_in,
 ):
     me, part = enter(plane, line)
+    chips = plane // 2
+    core = lax.rem(me, 2)
+    chip = me // 2
+    sibling = me + 1 - 2 * core
     far = []
     split_cuts, (whole_at, whole_rows), (last_at, last_rows) = cuts
     for k in range(1, line):
@@ -379,12 +459,9 @@
     copies = []
     for k in range(1, plane):
         peer = lax.rem(me + k, plane)
-        gather_rows(lambda b, j, peer=peer: tokens[peer, b, j], wide, sent.at[peer])
-        target = out.at[me, 0:capacity]
-        copies.append(send(sent.at[peer], target, out_sems.at[k], in_sems.at[k], (peer, part)))
-    gather_rows(lambda b, j: tokens[me, b, j], wide, sent.at[me])
-    own = pltpu.make_async_copy(sent.at[me], out.at[me, 0:capacity], own_sem)
-    own.start()
+        gather_rows(listed(tokens.at[peer], 0), wide, sent.at[peer])
+        copies.append(send(sent.at[peer], back.at[me], out_sems.at[k], in_sems.at[k], (peer, part)))
+    gather_rows(listed(tokens.at[me], 0), wide, sent.at[me])
     to = 0
     for at, count in split_cuts:
         got[part, to : to + count] = summed[pl.ds(pl.multiple_of(at + part * count, 16), count), :]
@@ -392,137 +469,74 @@
     got[part, to : to + whole_rows] = summed[whole_at : whole_at + whole_rows, :]
     for copy in far:
         copy.wait()
-    total = got[0].astype(F32)
+    share = got[0].astype(F32)
     for m in range(1, line):
-        total = total + got[m].astype(F32)
-    dense[0 : to + whole_rows, :] = total.astype(BF16)
-    dense[to + whole_rows :, :] = summed[last_at : last_at + last_rows, :]
+        share = share + got[m].astype(F32)
+    dense_all[me, 0 : to + whole_rows, :] = share.astype(BF16)
+    dense_all[me, to + whole_rows :, :] = summed[last_at : last_at + last_rows, :]
+    dense = dense_all.at[me]
+    spread = []
+    for k in range(1, chips):
+        other = lax.rem(chip + k, chips)
+        spread.append(send(dense, dense, chip_out.at[k], chip_in.at[k], (2 * other + core, part)))
+    near = [send(dense, dense, near_out.at[0], near_in.at[0], (sibling, part))]
+
+    group = max(1, 1280 // capacity)
+    order = [me] + [lax.rem(me - k + plane, plane) for k in range(1, plane)]
+    for first in range(0, plane, group):
+        blocks = order[first : first + group]
+        grads = [sent.at[blocks[0]] if first == 0 else back.at[blocks[0]]] + [back.at[block] for block in blocks[1:]]
+        for k in range(max(first, 1), min(first + group, plane)):
+            copies[k - 1].wait_recv()
+        add_rows(ids, capacity, blocks, grads, total, first == 0)
+    for k in range(1, chips):
+        peer = 2 * lax.rem(chip - k + chips, chips) + core
+        spread[k - 1].wait_recv()
+        near.append(send(dense_all.at[peer], dense_all.at[peer], near_out.at[k], near_in.at[k], (sibling, part)))
+
     square = jnp.zeros((8, LANES), F32)
     for begin, count, weight in ((0, to, 1.0), (to, whole_rows, 1.0 / line), (to + whole_rows, last_rows, 1.0)):
-        block = dense[begin : begin + count, :].astype(F32)
+        block = dense_all[me, begin : begin + count, :].astype(F32)
         square = square + weight * jnp.sum((block * block).reshape(count // 8, 8, LANES), 0)
-    dense_sq[...] = square
-    total = gains[0]
-    for m in range(1, line):
-        total = total + gains[m]
-    gain_all[...] = total
-    own.wait()
-    for copy in copies:
-        copy.wait()
-
-
-def scatter_kernel(ids, counts, rows, out, square, wide, *others):
-    tables = (out, *others)
-    ways = len(tables)
-    for table in tables:
-        table[...] = jnp.zeros_like(table)
-    step = 4 * ways
-
-    for d in range(rows.shape[0]):
-        count = counts[d]
-
-        def widen(i, carry):
-            at = pl.ds(pl.multiple_of(i * 64, 64), 64)
-            wide[at, :] = rows[d, at, :].astype(F32)
-            return carry
-
-        lax.fori_loop(0, lax.shift_right_logical(count + 63, 6), widen, 0)
-
-        def body(i, carry):
-            for u in range(0, step, ways):
-                first = i * step + u
-                at = [ids[d, first + n] for n in range(ways)]
-                sums = [
-                    table[pl.ds(at[n], 1), :] + wide[pl.ds(first + n, 1), :] for n, table in enumerate(tables)
-                ]
-                for n, table in enumerate(tables):
-                    table[pl.ds(at[n], 1), :] = sums[n]
-            return carry
-
-        def rest(j, carry):
-            at = ids[d, j]
-            out[pl.ds(at, 1), :] = out[pl.ds(at, 1), :] + wide[pl.ds(j, 1), :]
-            return carry
-
-        full = lax.div(count, step)
-        lax.fori_loop(0, full, body, 0)
-        lax.fori_loop(full * step, count, rest, 0)
-
-    def add(i, total):
-        at = pl.ds(pl.multiple_of(i * 32, 32), 32)
-        block = out[at, :]
-        for table in others:
-            block = block + table[at, :]
-        out[at, :] = block
-        block = block * block
-        for r in range(4):
-            total = total + block[r * 8 : (r + 1) * 8, :]
-        return total
-
-    square[...] = lax.fori_loop(0, out.shape[0] // 32, add, jnp.zeros((8, LANES), F32))
-
-
-def norm_kernel(
-    plane,
-    line,
-    table_sq,
-    dense_sq,
-    dense,
-    gain,
-    norm_sq,
-    dense_all,
-    along,
-    across,
-    along_out,
-    along_in,
-    across_out,
-    across_in,
-    far_out,
-    far_in,
-    near_out,
-    near_in,
-    own_sem,
-):
-    me, part = enter(plane, line)
-    chips = plane // 2
-    core = lax.rem(me, 2)
-    chip = me // 2
-    sibling = me + 1 - 2 * core
-    across[me] = dense_sq[...] + table_sq[...] * (1.0 / line)
+    height = total.shape[0]
+
+    def settle(i, carry):
+        at = pl.multiple_of(i * 32, 32)
+        for half in range(2):
+            block = total[pl.ds(at, 32), half * LANES : (half + 1) * LANES]
+            table[pl.ds(at + half * height, 32), :] = block
+            block = block * block
+            for r in range(4):
+                carry = carry + block[r * 8 : (r + 1) * 8, :]
+        return carry
+
+    table_sq = lax.fori_loop(0, height // 32, settle, jnp.zeros((8, LANES), F32))
+    across[me] = square + table_sq * (1.0 / line)
     tiny = [
         send(across.at[me], across.at[me], across_out.at[k], across_in.at[k], (lax.rem(me + k, plane), part))
         for k in range(1, plane)
     ]
-    far = []
-    for k in range(1, chips):
-        to = lax.rem(chip + k, chips)
-        far.append(send(dense, dense_all.at[me], far_out.at[k], far_in.at[k], (2 * to + core, part)))
-    near = [send(dense, dense_all.at[me], near_out.at[0], near_in.at[0], (sibling, part))]
-    own = pltpu.make_async_copy(dense, dense_all.at[me], own_sem)
-    own.start()
     for copy in tiny:
         copy.wait()
-    total = across[0]
+    sums = across[0]
     for d in range(1, plane):
-        total = total + across[d]
-    along[part] = total
+        sums = sums + across[d]
+    along[part] = sums
     peers = [lax.rem(part + k, line) for k in range(1, line)]
     tiny = [
         send(along.at[part], along.at[part], along_out.at[k], along_in.at[k], (me, peer)) for k, peer in enumerate(peers)
     ]
-    for k in range(1, chips):
-        peer = 2 * lax.rem(chip - k + chips, chips) + core
-        far[k - 1].wait_recv()
-        near.append(send(dense_all.at[peer], dense_all.at[peer], near_out.at[k], near_in.at[k], (sibling, part)))
+    gain_sum = gains[0]
+    for m in range(1, line):
+        gain_sum = gain_sum + gains[m]
+    gain_all[...] = gain_sum
     for copy in tiny:
         copy.wait()
-    total = along[0]
+    sums = along[0]
     for m in range(1, line):
-        total = total + along[m]
-    gains = gain[...]
-    norm_sq[...] = jnp.broadcast_to(jnp.sum(total + gains * gains), norm_sq.shape)
-    own.wait()
-    for copy in far:
+        sums = sums + along[m]
+    norm_sq[...] = jnp.broadcast_to(jnp.sum(sums + gain_sum * gain_sum), norm_sq.shape)
+    for copy in copies + spread:
         copy.wait_send()
     for copy in near:
         copy.wait()
@@ -538,6 +552,7 @@
 def forward_kernel(slots, cnt, x, w_in, gain, w_qkv, w_out, pooled, pm_out, normed_out, qkv, prob, a_out, pm_acc):
     tower = pl.program_id(0)
     pairs = pooled.shape[1]
+    first = lax.axis_index("mp") * pairs
     parts = w_qkv.shape[0]
     per = LANES // slots
     groups = pairs // per
@@ -545,7 +560,7 @@
     xs = x[0]
     hidden = nn(xs, w_in[0].astype(BF16))
     inverse = lax.rsqrt(jnp.mean(hidden * hidden, -1, keepdims=True) + EPS)
-    normed = (hidden * inverse * gain[0]).astype(BF16)
+    normed = (hidden * inverse * gain[pl.ds(tower, 1), :]).astype(BF16)
     normed_out[0] = normed
     for c in range(3):
         for m in range(parts):
@@ -559,7 +574,7 @@
     own_head = iota((per * heads, LANES), 0) & (heads - 1)
 
     def group(g, carry):
-        counts = [cnt[tower * pairs + g * per + k] for k in range(per)]
+        counts = [cnt[tower, first + g * per + k] for k in range(per)]
         live_r = same & ((lane & (slots - 1)) < chain(pair_r, counts))
         live_s = (line & (slots - 1)) < chain(pair_s, counts)
         rows = pl.ds(pl.multiple_of(g * LANES, LANES), LANES)
@@ -589,7 +604,7 @@
     lax.fori_loop(0, groups, group, 0)
     pm = jnp.concatenate([pm_acc[g] for g in range(groups)], 0).astype(BF16)
     pm_out[0] = pm
-    every = [cnt[tower * pairs + k] for k in range(pairs)]
+    every = [cnt[tower, first + k] for k in range(pairs)]
     tokens = iota((pairs, pairs * slots), 1)
     mine = lax.shift_right_logical(tokens, shift) == iota(tokens.shape, 0)
     live = mine & ((tokens & (slots - 1)) < chain(iota(tokens.shape, 0), every))
@@ -613,7 +628,8 @@
     heads = 2 * parts
     shift = slots.bit_length() - 1
     tokens = pairs * slots
-    every = [cnt[tower * pairs + k] for k in range(pairs)]
+    first = lax.axis_index("mp") * pairs
+    every = [cnt[tower, first + k] for k in range(pairs)]
     count = chain(iota((pairs, width), 0), every).astype(F32)
     dsum = dpooled[0].astype(F32) / count
     branch = dsum.astype(BF16)
@@ -675,8 +691,15 @@
     hidden = nn(xs, w)
     inverse = lax.rsqrt(jnp.mean(hidden * hidden, -1, keepdims=True) + EPS)
     unit = hidden * inverse
-    d_gain[0] = jnp.sum(dnormed * unit, 0, keepdims=True)
-    scaled = dnormed * gain[0]
+    grad = jnp.sum(dnormed * unit, 0, keepdims=True)
+
+    @pl.when(tower == 0)
+    def _():
+        d_gain[...] = jnp.zeros_like(d_gain)
+
+    for j in range(width // LANES):
+        d_gain[pl.ds(tower * (width // LANES) + j, 1), :] = grad[:, j * LANES : (j + 1) * LANES]
+    scaled = dnormed * gain[pl.ds(tower, 1), :]
     dh = inverse * (scaled - unit * jnp.mean(scaled * unit, -1, keepdims=True))
     spread = jnp.broadcast_to(dsum[:, None, :], (pairs, slots, width))
     slot = iota((pairs, slots, width), 1)
@@ -704,10 +727,10 @@
     far_one,
     far_two,
     far_three,
-    prior_row,
-    prior_col,
-    pos_row,
-    pos_own,
+    log_prior,
+    item_qid,
+    extra,
+    positive,
     dpooled,
     d_one,
     d_two,
@@ -729,6 +752,9 @@
     w_two,
     w_three,
     load_sems,
+    second_mine,
+    dpool_mine,
+    prior_col,
 ):
     loads = [
         pltpu.make_async_copy(source, target, load_sems.at[j])
@@ -752,6 +778,16 @@
     one = [w_one[t].astype(BF16) for t in range(towers)]
     two = [w_two[t].astype(BF16) for t in range(towers)]
     three = [w_three[t].astype(BF16) for t in range(towers)]
+    qid = item_qid[...]
+    hot = (lax.shift_right_logical(qid, 7) == iota((log_prior.shape[0], pairs), 0)).astype(BF16)
+    high, rest = log_prior[...].astype(BF16), log_prior[...]
+    rest = rest - high.astype(F32)
+    middle, low = split(rest)
+    table = tn(high, hot) + tn(middle, hot) + tn(low, hot)
+    prior_row = jnp.sum(jnp.where((qid & 127) == iota((LANES, pairs), 0), table, 0.0), 0, keepdims=True)
+    prior_col[...] = jnp.transpose(jnp.broadcast_to(prior_row, (8, pairs)), (1, 0))
+    pos_row = jnp.concatenate([extra[d, 0:1, 0:rows] for d in range(plane)], 1)
+    pos_own = chain(iota((own, pairs), 0), [positive[part * own + k] for k in range(own)])
     for copy in first:
         copy.wait()
     act_one, slope_one, pools = [], [], []
@@ -760,7 +796,9 @@
         value, slope = gelu_parts(nn(pools[t], one[t]))
         act_one.append(value.astype(BF16))
         slope_one.append(slope)
-        second_send[t] = nn(act_one[t], two[t]).reshape(line, own, -1)
+        partial = nn(act_one[t], two[t]).reshape(line, own, -1)
+        second_mine[t] = partial
+        second_send[t] = partial.astype(BF16)
     second = [
         send(
             second_send.at[:, peers[k]], second_got.at[:, part], out_sems.at[1, k], in_sems.at[1, k], (me, peers[k])
@@ -771,9 +809,9 @@
         copy.wait()
     act_two, slope_two, third, length, vectors = [], [], [], [], []
     for t in range(towers):
-        total = second_send[t, part]
+        total = second_mine[t, part]
         for peer in peers:
-            total = total + second_got[t, peer]
+            total = total + second_got[t, peer].astype(F32)
         value, slope = gelu_parts(total)
         act_two.append(value.astype(BF16))
         slope_two.append(slope)
@@ -787,32 +825,44 @@
     ]
     for copy in along:
         copy.wait()
-    across = [
-        send(vec.at[:, me], vec.at[:, me], vec_out.at[k], vec_in.at[k], (lax.rem(me + k, plane), part))
-        for k in range(1, plane)
-    ]
+    chips = plane // 2
+    core = lax.rem(me, 2)
+    chip = me // 2
+    sibling = me + 1 - 2 * core
+    near = [send(vec.at[:, me], vec.at[:, me], vec_out.at[0], vec_in.at[0], (sibling, part))]
+    across = []
+    for k in range(1, chips):
+        other = 2 * lax.rem(chip + k, chips) + core
+        across.append(send(vec.at[:, me], vec.at[:, me], vec_out.at[k], vec_in.at[k], (other, part)))
+    for k in range(1, chips):
+        peer = 2 * lax.rem(chip - k + chips, chips) + core
+        across[k - 1].wait_recv()
+        sems = vec_out.at[chips + k], vec_in.at[chips + k]
+        near.append(send(vec.at[:, peer], vec.at[:, peer], *sems, (sibling, part)))
     for copy in across:
+        copy.wait_send()
+    for copy in near:
         copy.wait()
 
     queries = vec[0].reshape(pairs, width)
     items = vec[1].reshape(pairs, width)
-    logits = INV_TEMP * nt(items, queries) - prior_col[...]
+    logits = INV_TEMP * nt(items, queries) - prior_col[:, 0:1]
     peak = jnp.max(logits, 0, keepdims=True)
     log_total = peak + jnp.log(jnp.sum(jnp.exp(logits - peak), 0, keepdims=True))
-    picked = jnp.where(iota((pairs, pairs), 0) == pos_row[...], logits, 0.0)
+    picked = jnp.where(iota((pairs, pairs), 0) == pos_row, logits, 0.0)
     gap = log_total - jnp.sum(picked, 0, keepdims=True)
     loss[...] = jnp.broadcast_to(jnp.sum(gap, 1, keepdims=True), loss.shape)
     ahead = me * rows + part * own
-    mine = INV_TEMP * nt(vectors[0], items) - prior_row[...]
+    mine = INV_TEMP * nt(vectors[0], items) - prior_row
     top = jnp.max(mine, 1, keepdims=True)
     expo = jnp.exp(mine - top)
     chance = expo / jnp.sum(expo, 1, keepdims=True)
-    target = (iota(mine.shape, 1) == pos_own[...]).astype(F32)
+    target = (iota(mine.shape, 1) == pos_own).astype(F32)
     dlog = ((chance - target) / pairs).astype(BF16)
     dvec = [(INV_TEMP * nn(dlog, items)).astype(BF16)]
-    own_prior = prior_col[pl.ds(pl.multiple_of(ahead, own), own), :]
+    own_prior = prior_col[pl.ds(pl.multiple_of(ahead, own), own), 0:1]
     theirs = INV_TEMP * nt(vectors[1], queries) - own_prior
-    target = (iota(theirs.shape, 0) + ahead == pos_row[...]).astype(F32)
+    target = (iota(theirs.shape, 0) + ahead == pos_row).astype(F32)
     dlog = ((jnp.exp(theirs - log_total) - target) / pairs).astype(BF16)
     dvec.append((INV_TEMP * nn(dlog, queries)).astype(BF16))
 
@@ -839,7 +889,9 @@
         dsecond = dsec_all[t].reshape(rows, -1)
         dact = nt(dsecond, two[t]).astype(BF16).astype(F32)
         dfirst = (dact * slope_one[t]).astype(BF16)
-        dpool_send[t] = nt(dfirst, one[t]).reshape(line, own, width)
+        partial = nt(dfirst, one[t]).reshape(line, own, width)
+        dpool_mine[t] = partial
+        dpool_send[t] = partial.astype(BF16)
         dfirsts.append(dfirst)
     back = [
         send(dpool_send.at[:, peers[k]], dpool_got.at[:, part], out_sems.at[4, k], in_sems.at[4, k], (me, peers[k]))
@@ -854,9 +906,9 @@
     for copy in back:
         copy.wait()
     for t in range(towers):
-        total = dpool_send[t, part]
+        total = dpool_mine[t, part]
         for peer in peers:
-            total = total + dpool_got[t, peer]
+            total = total + dpool_got[t, peer].astype(F32)
         dpooled[t] = total.astype(BF16)
 
 
@@ -985,16 +1037,6 @@
     units = w_one.shape[2]
     seconds = w_two.shape[2]
 
-    def ordered(value):
-        value = value.reshape(line, own, towers, slots)
-        return jnp.transpose(value, (0, 2, 1, 3)).reshape(requests // LANES, LANES)
-
-    live = jnp.arange(slots)[None, None, :] < slot_count[:, :, None]
-    owner = ordered(jnp.where(live, slot_owner[..., 0], plane))
-    row = ordered(slot_row)
-    own_chunks = own_requests // LANES
-    own_owner = lax.dynamic_slice_in_dim(owner, part * own_chunks, own_chunks, 0)
-    own_row = lax.dynamic_slice_in_dim(row, part * own_chunks, own_chunks, 0)
     per = capacity // LANES
     small = capacity // 4
     lists, inverse, own_place, own_small, extra = pl.pallas_call(
@@ -1002,15 +1044,21 @@
         out_shape=[
             shape((plane, 2 * per, LANES), I32),
             shape((plane * per, LANES), I32),
-            shape((own_chunks, LANES), I32),
-            shape((own_chunks, LANES), I32),
+            shape((slots, LANES), I32),
+            shape((slots, LANES), I32),
             shape((8, LANES), I32),
         ],
-        in_specs=[VMEM] * 5,
+        in_specs=[VMEM] * 4,
         out_specs=[VMEM] * 5,
         compiler_params=params(16),
         name="request_lists",
-    )(owner, row, own_owner, own_row, positive.reshape(1, batch))
+    )(
+        jnp.transpose(slot_owner[..., 0], (1, 2, 0)),
+        jnp.transpose(slot_row, (1, 2, 0)),
+        jnp.transpose(slot_count),
+        positive.reshape(1, batch),
+    )
+    dims = (towers, own, slots)
 
     def row_scratch(count):
         return [
@@ -1020,7 +1068,7 @@
         ]
 
     embedded, got_lists, got_extra, wide_qkv, wide_out = pl.pallas_call(
-        functools.partial(fetch_kernel, plane, line),
+        functools.partial(fetch_kernel, plane, line, dims),
         out_shape=[
             shape((own_requests, depth), BF16),
             shape(lists.shape, I32),
@@ -1050,7 +1098,7 @@
 
     def refetch(ids, place, table, _):
         return pl.pallas_call(
-            functools.partial(refetch_kernel, plane),
+            functools.partial(refetch_kernel, plane, dims),
             out_shape=shape((own_requests, depth), BF16),
             in_specs=[SMEM, SMEM, VMEM],
             out_specs=VMEM,
@@ -1062,10 +1110,8 @@
     embedded = lax.cond(most[0] > small, refetch, lambda *given: given[3], got_lists, own_place, embedding, embedded)
     embedded = embedded.reshape(towers, tokens, depth)
 
-    counts = jnp.transpose(slot_count).reshape(towers, line, own)
-    counts = lax.dynamic_index_in_dim(counts, part, 1, keepdims=False).reshape(towers * own)
+    counts = jnp.transpose(slot_count)
     heads = 2 * line
-    gains = norm_gain.reshape(towers, 1, width)
     groups = tokens // LANES
     per_group = LANES // slots
     lead = lambda *dims: pl.BlockSpec((1,) + dims, lambda t: (t,) + (0,) * len(dims))
@@ -1082,7 +1128,7 @@
             shape((towers, groups, heads, LANES, LANES), BF16),
             shape((towers, groups, per_group * heads, LANES), BF16),
         ],
-        in_specs=[SMEM, lead(tokens, depth), lead(depth, width), lead(1, width), qkv_spec, out_spec],
+        in_specs=[SMEM, lead(tokens, depth), lead(depth, width), VMEM, qkv_spec, out_spec],
         out_specs=[
             lead(own, width),
             lead(own, line * LANES),
@@ -1094,13 +1140,8 @@
         scratch_shapes=[pltpu.VMEM((groups, per_group, line * LANES), F32)],
         compiler_params=params(20),
         name="attention_forward",
-    )(counts, embedded, w_in, gains, wide_qkv, wide_out)
-
-    prior = jnp.sum(
-        jnp.where(item_qid[:, None] == jnp.arange(log_prior.shape[0])[None, :], log_prior[None, :], 0.0), 1
-    )
-    positions = got_extra[:, 0, :batch].reshape(1, pairs)
-    own_positions = lax.dynamic_slice_in_dim(positive, part * own, own, 0).reshape(own, 1)
+    )(counts, embedded, w_in, norm_gain, wide_qkv, wide_out)
+
     dpooled, d_one, d_two, d_three, loss = pl.pallas_call(
         functools.partial(upper_kernel, plane, line),
         out_shape=[
@@ -1110,17 +1151,17 @@
             shape((towers, width // LANES, seconds, LANES), BF16),
             shape((8, LANES), F32),
         ],
-        in_specs=[VMEM] + [HBM] * 3 + [VMEM] * 4,
+        in_specs=[VMEM] + [HBM] * 3 + [VMEM] * 3 + [SMEM],
         out_specs=[VMEM] * 5,
         scratch_shapes=[
             pltpu.VMEM((towers, line, own, width), BF16),
-            pltpu.VMEM((towers, line, own, seconds), F32),
-            pltpu.VMEM((towers, line, own, seconds), F32),
+            pltpu.VMEM((towers, line, own, seconds), BF16),
+            pltpu.VMEM((towers, line, own, seconds), BF16),
             pltpu.VMEM((towers, plane, line, own, width), BF16),
             pltpu.VMEM((towers, line, own, seconds), BF16),
             pltpu.VMEM((towers, line, own, seconds), BF16),
-            pltpu.VMEM((towers, line, own, width), F32),
-            pltpu.VMEM((towers, line, own, width), F32),
+            pltpu.VMEM((towers, line, own, width), BF16),
+            pltpu.VMEM((towers, line, own, width), BF16),
             DMA((5, line)),
             DMA((5, line)),
             DMA((plane,)),
@@ -1129,10 +1170,22 @@
             pltpu.VMEM(w_two.shape, F32),
             pltpu.VMEM(w_three.shape, F32),
             DMA((3,)),
+            pltpu.VMEM((towers, line, own, seconds), F32),
+            pltpu.VMEM((towers, line, own, width), F32),
+            pltpu.VMEM((pairs, 8), F32),
         ],
         compiler_params=params(22 + 2 * (pairs * pairs >> 18), collective_id=3, has_side_effects=True),
         name="upper",
-    )(pooled, w_one, w_two, w_three, prior.reshape(1, pairs), prior.reshape(pairs, 1), positions, own_positions)
+    )(
+        pooled,
+        w_one,
+        w_two,
+        w_three,
+        log_prior.reshape(-1, LANES),
+        item_qid.reshape(1, pairs),
+        got_extra,
+        positive,
+    )
 
     demb, d_in, d_gain, d_qkv, d_out = pl.pallas_call(
         functools.partial(backward_kernel, slots),
@@ -1140,7 +1193,7 @@
         out_shape=[
             shape((towers, tokens, depth), BF16),
             shape((towers, width // LANES, depth, LANES), BF16),
-            shape((towers, 1, width), F32),
+            shape((8, LANES), F32),
             shape((line, towers, 3, width, LANES), BF16),
             shape((line, towers, width // LANES, LANES, LANES), BF16),
         ],
@@ -1148,7 +1201,7 @@
             SMEM,
             lead(tokens, depth),
             lead(depth, width),
-            lead(1, width),
+            VMEM,
             qkv_spec,
             out_spec,
             lead(tokens, width),
@@ -1161,14 +1214,14 @@
         out_specs=[
             lead(tokens, depth),
             lead(width // LANES, depth, LANES),
-            lead(1, width),
+            pl.BlockSpec((8, LANES), lambda t: (0, 0)),
             qkv_spec,
             pl.BlockSpec((line, 1, width // LANES, LANES, LANES), lambda t: (0, t, 0, 0, 0)),
         ],
         scratch_shapes=[pltpu.VMEM((3 * line, tokens, LANES), BF16)],
         compiler_params=params(24),
         name="attention_backward",
-    )(counts, embedded, w_in, gains, wide_qkv, wide_out, normed, qkv, prob, spread, pm, dpooled)
+    )(counts, embedded, w_in, norm_gain, wide_qkv, wide_out, normed, qkv, prob, spread, pm, dpooled)
 
     def shares(grad, lead=()):
         rows = grad.size // (LANES * plane * (lead[0] if lead else 1))
@@ -1177,7 +1230,6 @@
     grads = [shares(d_qkv, (line,)), shares(d_out, (line,))] + [shares(g) for g in (d_three, d_in, d_one, d_two)]
     sizes = [g.shape[-2] for g in grads]
     share = line * (sizes[0] + sizes[1]) + sum(sizes[2:])
-    gain_rows = jnp.pad(d_gain.reshape(-1, LANES), ((0, 8 - d_gain.size // LANES), (0, 0)))
     every, summed, gain_sum = pl.pallas_call(
         functools.partial(spread_kernel, plane, line),
         out_shape=[
@@ -1205,7 +1257,7 @@
         ],
         compiler_params=params(20, collective_id=4, has_side_effects=True),
         name="spread",
-    )(demb.reshape(own_requests, depth), *grads, gain_rows)
+    )(demb.reshape(own_requests, depth), *grads, d_gain)
     whole_at = line * (sizes[0] + sizes[1])
     whole_rows = sizes[2] + sizes[3]
     last_rows = sizes[4] + sizes[5]
@@ -1216,76 +1268,56 @@
     )
     line_rows = sizes[0] + sizes[1] + whole_rows
 
-    def give_back(count, number):
+    def tail(count, number):
         return lambda *given: pl.pallas_call(
-            functools.partial(return_kernel, plane, line, count, cuts),
+            functools.partial(tail_kernel, plane, line, count, cuts),
             out_shape=[
-                shape((plane, capacity, depth), BF16),
-                shape((line_rows + last_rows, LANES), BF16),
+                shape(embedding.shape, F32),
+                shape((plane, line_rows + last_rows, LANES), BF16),
                 shape((8, LANES), F32),
                 shape((8, LANES), F32),
             ],
-            in_specs=[SMEM, VMEM, VMEM, VMEM],
+            in_specs=[SMEM] + [VMEM] * 4,
             out_specs=[VMEM] * 4,
             scratch_shapes=[
                 pltpu.VMEM((requests, depth), F32),
                 pltpu.VMEM((plane, count, depth), BF16),
+                pltpu.VMEM((plane, count, depth), BF16),
+                pltpu.VMEM((embedding.shape[0] // 2, 2 * depth), F32),
                 pltpu.VMEM((line, line_rows, LANES), BF16),
                 pltpu.VMEM((line, 8, LANES), F32),
+                pltpu.VMEM((line, 8, LANES), F32),
+                pltpu.VMEM((plane, 8, LANES), F32),
                 DMA((plane,)),
                 DMA((plane,)),
                 DMA((3, line)),
                 DMA((3, line)),
                 DMA((line,)),
                 DMA((line,)),
-                DMA,
+                DMA((line,)),
+                DMA((line,)),
+                DMA((plane,)),
+                DMA((plane,)),
+                DMA((plane // 2,)),
+                DMA((plane // 2,)),
+                DMA((plane // 2,)),
+                DMA((plane // 2,)),
             ],
-            compiler_params=params(16, collective_id=number, has_side_effects=True),
-            name="return_rows",
+            compiler_params=params(36, collective_id=number, has_side_effects=True),
+            name="tail",
         )(*given)
 
     medium = capacity * 5 // 8
-    incoming, dense, dense_sq, gain_all = lax.cond(
+    table_grad, dense_all, norm_sq, gain_all = lax.cond(
         most[1] > medium,
-        give_back(capacity, 8),
-        give_back(medium, 5),
+        tail(capacity, 8),
+        tail(medium, 5),
         inverse.reshape(plane, per, LANES),
+        got_lists,
         every.reshape(requests, depth),
         summed,
         gain_sum,
     )
-    served = got_lists[:, :per, :].reshape(plane, capacity)
-    table_grad, table_sq = pl.pallas_call(
-        scatter_kernel,
-        out_shape=[shape(embedding.shape, F32), shape((8, LANES), F32)],
-        in_specs=[SMEM, SMEM, VMEM],
-        out_specs=[VMEM, VMEM],
-        scratch_shapes=[pltpu.VMEM((capacity, depth), F32)] + [pltpu.VMEM(embedding.shape, F32)] * 3,
-        compiler_params=params(20),
-        name="add_rows",
-    )(jnp.maximum(served, 0), jnp.sum((served >= 0).astype(I32), 1), incoming)
-
-    norm_sq, dense_all = pl.pallas_call(
-        functools.partial(norm_kernel, plane, line),
-        out_shape=[shape((8, LANES), F32), shape((plane, *dense.shape), BF16)],
-        in_specs=[VMEM] * 4,
-        out_specs=[VMEM] * 2,
-        scratch_shapes=[
-            pltpu.VMEM((line, 8, LANES), F32),
-            pltpu.VMEM((plane, 8, LANES), F32),
-            DMA((line,)),
-            DMA((line,)),
-            DMA((plane,)),
-            DMA((plane,)),
-            DMA((plane // 2,)),
-            DMA((plane // 2,)),
-            DMA((plane // 2,)),
-            DMA((plane // 2,)),
-            DMA,
-        ],
-        compiler_params=params(12, collective_id=6, has_side_effects=True),
-        name="norm_parts",
-    )(table_sq, dense_sq, dense, gain_all)
     flat = lambda w: w.reshape(-1, w.shape[-1])
     turn = lambda w: flat(jnp.transpose(w, (0, 2, 1, 3)))
     given = [embedding, embedding_mom, embedding_avg]

time: 209 us -> 191 us (0.914)
  Pallas kernels: 190 us -> 178 us
  local copies, waits for them, and re-layouts: 14.2 us -> 9.26 us
  other arithmetic: 2.38 us -> 0.13 us
    pallas_call x4 -> x2, Pallas kernels: 87.3 us -> 76.4 us  [the longest x1 46 us: tail(): pl.pallas_call(functools.partial(tail_kernel, plane, line, count, cuts),...]
    reshape x8 -> x0, local copies, waits for them, and re-layouts: 3.36 us -> none  [the longest x1 0.86 us: shards(): prior.reshape(pairs, 1)]
    pallas_call x1, Pallas kernels: 38.4 us -> 35.9 us  [shards(): pl.pallas_call(functools.partial(upper_kernel, plane, line), out_shape=[s...]
    reduce_sum x2 -> x0, other arithmetic: 2.17 us -> none  [the longest x1 1.94 us: shards(): jnp.sum(jnp.where(item_qid[:, None] == jnp.arange(log_prior.shape[0])[Non...]
    unnamed x31 -> x40, local copies, waits for them, and re-layouts: 7.68 us -> 6.97 us
where the time goes in v4:
time: 191 us; the launch traced here: 190 us
  Pallas kernels  178 us (93%)
  local copies, waits for them, and re-layouts  9.26 us (5%)
  between operations  2.2 us (1%)
    pallas_call x1, Pallas kernels, tail(): pl.pallas_call(functools.partial(tail_kernel, plane, line, count, cuts),...  46 us
    pallas_call x1, Pallas kernels, shards(): pl.pallas_call(functools.partial(upper_kernel, plane, line), out_shape=[s...  35.9 us
    pallas_call x1, Pallas kernels, shards(): pl.pallas_call(functools.partial(fetch_kernel, plane, line, dims), out_sh...  30.4 us
    pallas_call x1, Pallas kernels, shards(): pl.pallas_call(functools.partial(spread_kernel, plane, line), out_shape=[...  27.8 us
    pallas_call x1, Pallas kernels, shards(): pl.pallas_call(functools.partial(update_kernel, blocks), out_shape=[shape...  14.3 us
    pallas_call x1, Pallas kernels, shards(): pl.pallas_call(functools.partial(backward_kernel, slots), grid=(towers,),...  10.7 us
    pallas_call x1, Pallas kernels, shards(): pl.pallas_call(functools.partial(forward_kernel, slots), grid=(towers,),...  9.6 us
    unnamed x40, local copies, waits for them, and re-layouts  6.97 us

profile of v4, /device:TPU:0, one launch (start us, length us, event | category | flops | bytes accessed | tf_op | source)
XLA Modules:
  0.0 190.3 jit_solution(11833131873813619424)
XLA Ops:
  0.7 0.7 copy-done.9
  1.4 0.8 copy-done.10
  2.2 0.7 copy-done.13
  2.9 0.7 copy-done.16
  3.5 3.3 %request_lists.1 = (s32[8,16,128]{2,1,0:T(8,128)S(1)}, s32[64,128]{1,0:T(8,128)}, s32[32,128]{1,0:T(8,128)S(1)}, s32[32,128]{1,0:T(8,128)S(1)}, s32[8,128]{1,0:T(8,128)S(1)}) custom-call(s32[2,32,64]{2,1,0:T(8,128)S(1)} %bitcast.85, s32[2,32,64]{2,1,0:T(8,128)S(1)} %bitcast.86, s32[2,64]{1,0:T(2,128)S(1)} %bitcast.88, s32[1,64]{1,0:T(1,128)S(1)} %bitcast.92), custom_call_target="tpu_custom_call" | custom-call | tf_op jit(solution)/shard_map/request_lists/pallas_call | solution.py:1042
  6.8 1.1 copy-done.2
  7.9 0.9 copy-done.8
  8.9 30.4 %fetch.1 = (bf16[1024,128]{1,0:T(8,128)(2,1)}, s32[8,16,128]{2,1,0:T(8,128)S(1)}, s32[8,8,128]{2,1,0:T(8,128)S(1)}, bf16[4,2,3,256,128]{4,3,2,1,0:T(8,128)(2,1)S(1)}, bf16[4,2,128,256]{3,2,1,0:T(8,128)(2,1)S(1)}) custom-call(s32[8,16,128]{2,1,0:T(8,128)S(1)} %get-tuple-element.132.lists, s32[8,128]{1,0:T(8,128)S(1)} %get-tuple-element.133.extra, ...), custom_call_target="tpu_custom_call" | custom-call | tf_op jit(solution)/shard_map/fetch/pallas_call | solution.py:1070
  39.3 0.0 copy-start.5
  39.3 0.8 copy-done.5
  40.1 0.1 slice_reduce_fusion
  40.3 0.6 fusion
  42.2 0.2 conditional.2
  42.4 1.2 copy-done.6
  43.6 9.6 %attention_forward.1 = (bf16[2,16,256]{2,1,0:T(8,128)(2,1)S(1)}, bf16[2,16,512]{2,1,0:T(8,128)(2,1)S(1)}, bf16[2,512,256]{2,1,0:T(8,128)(2,1)S(1)}, bf16[2,12,51...) custom-call(s32[2,64]{1,0:T(2,128)S(1)} %bitcast.89, ...), custom_call_target="tpu_custom_call" | custom-call | tf_op jit(solution)/shard_map/attention_forward/pallas_call | solution.py:1120
  53.2 0.0 copy-done.4
  53.3 35.9 %upper.1 = (bf16[2,16,256]{2,1,0:T(8,128)(2,1)S(1)}, bf16[2,2,256,128]{3,2,1,0:T(8,128)(2,1)S(1)}, bf16[2,4,256,128]{3,2,1,0:T(8,128)(2,1)S(1)}, bf16[2,2,512,128]{3,2,1,0:T(8,128)(2,1)S(1)}, f32[8,128]{1,0:T(8,128)S(1)}) custom-call(bf16[2,16,256]{2,1,0:T(8,128)(2,1)S(1)} %get-tuple-element.141.pooled, f32[2,256,256]{2,1,0:T(8,128)S(1)} %copy-done.4, ...), custom_call_target="tpu_custom_call" | custom-call | tf_op jit(solution)/shard_map/upper/pallas_call | solution.py:1145
  89.2 10.7 %attention_backward.1 = (bf16[2,512,128]{2,1,0:T(8,128)(2,1)S(1)}, bf16[2,2,128,128]{3,2,1,0:T(8,128)(2,1)S(1)}, f32[8,128]{1,0:T(8,128)S(1)}, bf16[4,2,3,256,12...) custom-call(s32[2,64]{1,0:T(2,128)S(1)} %bitcast.90, bf16[2,512,128]{2,1,0:T(8,128)(2,1)} %get-tuple-element.200.x, ...), custom_call_target="tpu_custom_call" | custom-call | tf_op jit(solution)/shard_map/attention_backward/pallas_call | solution.py:1190
  99.9 0.5 slice.17
  100.5 27.8 %spread.1 = (bf16[4,1024,128]{2,1,0:T(8,128)(2,1)S(1)}, bf16[1728,128]{1,0:T(8,128)(2,1)S(1)}, f32[8,128]{1,0:T(8,128)S(1)}) custom-call(bf16[1024,128]{1,0:T(8,128)(2,1)S(1)} %bitcast.83, bf16[4,4,2,192,128]{4,3,2,1,0:T(8,128)(2,1)S(1)} %bitcast.77, bf16[4,4,2,64,128]{4,3,2,1,0:T(8,128)(2,1)S(1)} %bitcast.81, bf16[4,2,256,128]{3,2,1,0:T(8,128)(2,1)S(1)} %bitcast.80, ...), custom_call_target="tpu_custom_call" | custom-call | tf_op jit(solution)/shard_map/spread/pallas_call | solution.py:1233
  128.3 46.5 %conditional.3 = ((f32[4096,128]{1,0:T(8,128)}, bf16[8,960,128]{2,1,0:T(8,128)(2,1)}, f32[8,128]{1,0:T(8,128)S(1)}, f32[8,128]{1,0:T(8,128)S(1)})) conditional(s32[]{:T(128)} %bitcast.12, (s32[8,8,128]{2,1,0:T(8,128)S(1)}, s32[8,16,128]{2,1,0:T(8,128)S(1)}, bf16[4096,128]{1,0:T(8,128)(2,1)S(1)}, bf16[1728,128]{1,0:T(8,128)(2,1)S(1)}, ...), branch_computations={%region_3.0_spmd, %region_4.0_spmd} | conditional | bytes 8 | solution.py:1311
  128.5 46.0 %tail.2 = (f32[4096,128]{1,0:T(8,128)}, bf16[8,960,128]{2,1,0:T(8,128)(2,1)}, f32[8,128]{1,0:T(8,128)S(1)}, f32[8,128]{1,0:T(8,128)S(1)}) custom-call(s32[8,8,128]{2,1,0:T(8,128)S(1)} %get-tuple-element.38.tokens, s32[8,16,128]{2,1,0:T(8,128)S(1)} %get-tuple-element.39.ids, bf16[4096,128]{1,0:T(8,128)(2,1)S(1)} %get-tuple-element.40.rows, ...), custom_call_target="tpu_custom_call" | custom-call | tf_op jit(solution)/shard_map/cond/branch_0_fun/tail/pallas_call | solution.py:1272
  174.8 14.3 %update.1 = (f32[4096,128]{1,0:T(8,128)}, f32[4096,128]{1,0:T(8,128)}, f32[4096,128]{1,0:T(8,128)}, f32[1536,128]{1,0:T(8,128)}, f32[1536,128]{1,0:T(8,128)}, /*...) custom-call(f32[8,128]{1,0:T(8,128)S(1)} %get-tuple-element.161.norm, ...), custom_call_target="tpu_custom_call" | custom-call | tf_op jit(solution)/shard_map/update/pallas_call | solution.py:1332
  189.1 1.2 slice.19
  (30 shorter events, 0.1 us)
Async XLA Ops:
  0.7 0.8 copy-start.9
  1.4 0.8 copy-start.10
  2.2 0.7 copy-start.13
  2.9 0.7 copy-start.16
  6.8 1.1 copy-start.2
  7.9 0.9 copy-start.8
  8.9 33.5 %copy-start.3 = (f32[2,128,256]{2,1,0:T(8,128)S(1)}, f32[2,128,256]{2,1,0:T(8,128)}, u32[]{:S(2)}) copy-start(f32[2,128,256]{2,1,0:T(8,128)} %w_in.3) | copy-start | bytes 786436
  8.9 33.5 %copy-start.11 = (f32[2,256]{1,0:T(2,128)S(1)}, f32[2,256]{1,0:T(2,128)}, u32[]{:S(2)}) copy-start(f32[2,256]{1,0:T(2,128)} %refs_21_.1) | copy-start | bytes 6148
  8.9 33.5 %copy-start.14 = (s32[64,2]{0,1:T(2,128)S(1)}, s32[64,2]{0,1:T(2,128)}, u32[]{:S(2)}) copy-start(s32[64,2]{0,1:T(2,128)} %param.36) | copy-start | bytes 1540
  39.3 0.8 copy-start.5
  42.1 11.1 %copy-start = (f32[2,256,512]{2,1,0:T(8,128)S(1)}, f32[2,256,512]{2,1,0:T(8,128)}, u32[]{:S(2)}) copy-start(f32[2,256,512]{2,1,0:T(8,128)} %far_two.1) | copy-start | bytes 3145732
  42.2 11.1 %copy-start.4 = (f32[2,256,256]{2,1,0:T(8,128)S(1)}, f32[2,256,256]{2,1,0:T(8,128)}, u32[]{:S(2)}) copy-start(f32[2,256,256]{2,1,0:T(8,128)} %far_one.1) | copy-start | bytes 1572868
  42.2 11.1 %copy-start.12 = (f32[4096]{0:T(1024)S(1)}, f32[4096]{0:T(1024)}, u32[]{:S(2)}) copy-start(f32[4096]{0:T(1024)} %param.39) | copy-start | bytes 49156
  42.2 11.1 %copy-start.15 = (s32[512]{0:T(512)S(1)}, s32[512]{0:T(512)}, u32[]{:S(2)}) copy-start(s32[512]{0:T(512)} %param.37) | copy-start | bytes 6148
  42.2 11.1 %copy-start.17 = (s32[64]{0:T(128)S(1)}, s32[64]{0:T(128)}, u32[]{:S(2)}) copy-start(s32[64]{0:T(128)} %positive.1) | copy-start | bytes 772
  42.4 1.2 copy-start.6
  43.6 9.7 %copy-start.1 = (f32[2,512,256]{2,1,0:T(8,128)S(1)}, f32[2,512,256]{2,1,0:T(8,128)}, u32[]{:S(2)}) copy-start(f32[2,512,256]{2,1,0:T(8,128)} %far_three.1) | copy-start | bytes 3145732
  43.6 45.6 %copy-start.7 = (bf16[4,2,128,256]{3,2,1,0:T(8,128)(2,1)S(1)}, bf16[4,2,128,256]{3,2,1,0:T(8,128)(2,1)}, u32[]{:S(2)}) copy-start(bf16[4,2,128,256]{3,2,1,0:T(8,128)(2,1)} %copy-done.5) | copy-start | bytes 1572868
  99.9 28.4 %copy-start.19 = (s32[64,128]{1,0:T(8,128)S(1)}, s32[64,128]{1,0:T(8,128)}, u32[]{:S(2)}) copy-start(s32[64,128]{1,0:T(8,128)} %get-tuple-element.143) | copy-start | bytes 98308
  128.3 46.5 %copy-start.18 = (f32[4096,128]{1,0:T(8,128)S(1)}, f32[4096,128]{1,0:T(8,128)}, u32[]{:S(2)}) copy-start(f32[4096,128]{1,0:T(8,128)} %refs_0_.1) | copy-start | bytes 6291460

commit v5 on v4

--- a/solution.py
+++ b/solution.py
@@ -55,6 +55,10 @@
 
 def params(limit, **more):
     return pltpu.CompilerParams(vmem_limit_bytes=limit << 20, **more)
+
+
+def log2(value):
+    return value.bit_length() - 1
 
 
 def lists_of(owner, values, owners, capacity):
@@ -91,59 +95,79 @@
     return places, lists, hot
 
 
-def log2(value):
-    return value.bit_length() - 1
-
-
-def prep_kernel(
-    owners, capacity, small, line, owner_in, row_in, count, positive, lists, inverse, own_place, own_small, extra
-):
-    towers, slots, batch = owner_in.shape
-    own = batch // line
+class Slots:
+    def __init__(self, owners, line, owner, row, count):
+        towers, slots, batch = owner.shape
+        own = batch // line
+        side = lambda ref: jnp.concatenate([ref[t] for t in range(towers)], 1)
+        counts = jnp.concatenate([count[t : t + 1, :] for t in range(towers)], 1)
+        slot, lane = iota((slots, LANES), 0), iota((slots, LANES), 1)
+        tower = lax.shift_right_logical(lane, log2(batch))
+        self.row = side(row)
+        self.owner = jnp.where(slot < counts, side(owner), owners)
+        self.block = lax.shift_right_logical(lane & (batch - 1), log2(own))
+        self.token = ((self.block * towers + tower) * own + (lane & (own - 1))) * slots + slot
+
+
+def make_own_lists(slots, owners, capacity, small, height, own_lists, own_place, own_small):
     per = capacity // LANES
-    side = lambda ref: jnp.concatenate([ref[t] for t in range(towers)], 1)
-    counts = jnp.concatenate([count[t : t + 1, :] for t in range(towers)], 1)
-    row = side(row_in)
-    slot, lane = iota((slots, LANES), 0), iota((slots, LANES), 1)
-    owner = jnp.where(slot < counts, side(owner_in), owners)
-    tower = lax.shift_right_logical(lane, log2(batch))
-    block = lax.shift_right_logical(lane & (batch - 1), log2(own))
-    token = ((block * towers + tower) * own + (lane & (own - 1))) * slots + slot
-    _, (rows, tokens), hot = lists_of(owner, (row + 1, token), owners, capacity)
-    own_owner = jnp.where(block == lax.axis_index("mp"), owner, owners)
-    places, (own_rows,), _ = lists_of(own_owner, (row,), owners, capacity)
-    rows = rows - 1
-    inverse[...] = tokens
+    owner = jnp.where(slots.block == lax.axis_index("mp"), slots.owner, owners)
+    places, (rows,), _ = lists_of(owner, (slots.row,), owners, capacity)
+    rows = jnp.minimum(jnp.maximum(rows, 0), height - 1)
     for d in range(owners):
-        lists[d, 0:per, :] = rows[d * per : (d + 1) * per, :]
-        lists[d, per : 2 * per, :] = own_rows[d * per : (d + 1) * per, :]
+        own_lists[d] = rows[d * per : (d + 1) * per, :]
     place = jnp.concatenate(places, 0)
-    place = jnp.where(place < owners * capacity, place, 0)
+    place = jnp.maximum(jnp.where(place < owners * capacity, place, 0), 0)
     own_place[...] = place
     rank = jnp.minimum(place & (capacity - 1), small - 1)
     own_small[...] = lax.shift_right_logical(place, log2(capacity)) * small + rank
+
+
+def make_lists(slots, owners, capacity, batch, line, positive, lists, inverse):
+    per = capacity // LANES
+    _, (rows, tokens), hot = lists_of(slots.owner, (slots.row + 1, slots.token), owners, capacity)
+    rows = rows - 1
+    inverse[...] = tokens
     asked = hot[0]
     for more in hot[1:]:
         asked = asked + more
+    own = batch // line
     near = lax.shift_right_logical(iota((LANES, LANES), 0) & (batch - 1), log2(own)) == iota((LANES, LANES), 1)
     asked = asked.astype(BF16)
     most = jnp.max(jnp.max(nn(asked, near.astype(BF16)), 0, keepdims=True), 1, keepdims=True)
     every = jnp.max(nn(asked, jnp.ones((LANES, LANES), BF16)), 0, keepdims=True)
-    extra[...] = jnp.zeros_like(extra)
-    extra[0:1, 0:batch] = positive[...]
-    extra[1:2, :] = jnp.broadcast_to(most, (1, LANES)).astype(I32)
-    extra[2:3, :] = every.astype(I32)
-
-
-def enter(plane, line):
+    most = jnp.broadcast_to(most, (1, LANES))
+    for d in range(owners):
+        lists[d, 0:per, :] = rows[d * per : (d + 1) * per, :]
+        lists[d, per : per + 1, 0:batch] = positive[...]
+        lists[d, per + 1 : per + 2, :] = most.astype(I32)
+        lists[d, per + 2 : per + 3, :] = every.astype(I32)
+
+
+def announce(plane, line):
     me, part = lax.axis_index("dp"), lax.axis_index("mp")
     barrier = pltpu.get_barrier_semaphore()
     for k in range(1, plane):
         pl.semaphore_signal(barrier, inc=1, device_id=(lax.rem(me + k, plane), part), device_id_type=MESH)
     for k in range(1, line):
         pl.semaphore_signal(barrier, inc=1, device_id=(me, lax.rem(part + k, line)), device_id_type=MESH)
-    pl.semaphore_wait(barrier, max(plane - 1, 0) + max(line - 1, 0))
     return me, part
+
+
+def await_others(plane, line):
+    pl.semaphore_wait(pltpu.get_barrier_semaphore(), max(plane - 1, 0) + max(line - 1, 0))
+
+
+def enter(plane, line):
+    me, part = announce(plane, line)
+    await_others(plane, line)
+    return me, part
+
+
+def partners(me, count):
+    order = sorted(range(1, count), key=lambda k: (-bin(k >> 1).count("1"), k & 1, k))
+    bits = [lax.rem(me // (1 << b), 2) for b in range(log2(count))]
+    return [sum((1 << b) * (1 - bit if k >> b & 1 else bit) for b, bit in enumerate(bits)) for k in order]
 
 
 def send(source, target, out_sem, in_sem, device):
@@ -188,22 +212,19 @@
 
 def send_rows(plane, me, part, ids, table, sent, got, wide, out_sems, in_sems):
     capacity = sent.shape[1]
-    half = ids.shape[1] // 2
     copies = []
-    for k in range(1, plane):
-        peer = lax.rem(me + k, plane)
-        gather_rows(listed(ids.at[peer], half), table, sent.at[peer])
+    for k, peer in enumerate(partners(me, plane)):
+        gather_rows(listed(ids.at[peer], 0), table, sent.at[peer])
         copies.append(send(sent.at[peer], got.at[me], out_sems.at[k], in_sems.at[k], (peer, part)))
-    gather_rows(listed(ids.at[me], half), table, sent.at[me])
+    gather_rows(listed(ids.at[me], 0), table, sent.at[me])
     wide[pl.ds(pl.multiple_of(me * capacity, capacity), capacity), :] = sent[me].astype(F32)
     return copies
 
 
 def take_rows(plane, me, part, dims, copies, place, got, wide, out):
     capacity = got.shape[1]
-    for k in range(1, plane):
-        peer = lax.rem(me - k + plane, plane)
-        copies[k - 1].wait_recv()
+    for copy, peer in zip(copies, partners(me, plane)):
+        copy.wait_recv()
         wide[pl.ds(pl.multiple_of(peer * capacity, capacity), capacity), :] = got[peer].astype(F32)
     gather_rows(placed(place, part, *dims), wide, out)
 
@@ -220,17 +241,27 @@
     plane,
     line,
     dims,
+    capacity,
+    owner_in,
+    row_in,
+    count,
+    positive,
+    far_table,
+    far_qkv,
+    far_wout,
+    out,
+    got_own,
+    got_lists,
+    weights,
+    inverse,
+    own_place,
+    own_lists,
+    own_small,
     lists,
-    extra,
-    place,
     table,
     w_qkv,
     w_out,
-    out,
-    got_lists,
-    got_extra,
-    wide_qkv,
-    wide_out,
+    place,
     ids,
     sent,
     got,
@@ -241,49 +272,80 @@
     in_sems,
     far_out,
     far_in,
+    side_out,
+    side_in,
     near_out,
     near_in,
     own_sems,
+    load_sems,
 ):
-    me, part = enter(plane, line)
+    loads = [
+        pltpu.make_async_copy(source, target, load_sems.at[j])
+        for j, (source, target) in enumerate(((far_qkv, w_qkv), (far_wout, w_out), (far_table, table)))
+    ]
+    for copy in loads:
+        copy.start()
+    me, part = announce(plane, line)
     core = lax.rem(me, 2)
+    half = lax.rem(me // 2, 2)
     sibling = me + 1 - 2 * core
-    wide_qkv[part] = w_qkv[...].astype(BF16)
-    wide_out[part] = w_out[...].astype(BF16)
-    far = []
+    partner = me + 2 - 4 * half
+    batch = positive.shape[1]
+    slots = Slots(plane, line, owner_in, row_in, count)
+    make_own_lists(slots, plane, capacity, sent.shape[1], table.shape[0], own_lists, own_place, own_small)
+    places = pltpu.make_async_copy(own_small, place, own_sems.at[0])
+    places.start()
+    for copy in loads[:2]:
+        copy.wait()
+    rows = weights.shape[3] // 2
+    for c in range(3):
+        weights[part, :, c] = w_qkv[:, c].astype(BF16)
+    for j in range(2):
+        weights[part, :, 3, j * LANES : (j + 1) * LANES, :] = w_out[:, :, j * LANES : (j + 1) * LANES].astype(BF16)
+    quarter = lambda m, h: weights.at[m, core, :, pl.ds(pl.multiple_of(h * rows, rows), rows), :]
+    await_others(plane, line)
+    far, asked, told = [], [], []
     for k in range(1, line):
         peer = lax.rem(part + k, line)
-        for j, block in enumerate((wide_qkv, wide_out)):
-            at = block.at[part, core]
-            far.append(send(at, at, far_out.at[j, k], far_in.at[j, k], (me, peer)))
-    asked = []
+        far.append(send(quarter(part, half), quarter(part, half), far_out.at[k], far_in.at[k], (me, peer)))
     for k in range(1, plane):
         peer = lax.rem(me + k, plane)
-        asked.append(send(lists.at[peer], got_lists.at[me], list_out.at[0, k], list_in.at[0, k], (peer, part)))
-        asked.append(send(extra, got_extra.at[me], list_out.at[1, k], list_in.at[1, k], (peer, part)))
+        asked.append(send(own_lists.at[peer], got_own.at[me], list_out.at[0, k], list_in.at[0, k], (peer, part)))
+    make_lists(slots, plane, capacity, batch, line, positive, lists, inverse)
+    for k in range(1, plane):
+        peer = lax.rem(me + k, plane)
+        told.append(send(lists.at[peer], got_lists.at[me], list_out.at[1, k], list_in.at[1, k], (peer, part)))
     mine = [
-        pltpu.make_async_copy(lists.at[me], got_lists.at[me], own_sems.at[0]),
-        pltpu.make_async_copy(extra, got_extra.at[me], own_sems.at[1]),
+        pltpu.make_async_copy(own_lists.at[me], got_own.at[me], own_sems.at[1]),
+        pltpu.make_async_copy(lists.at[me], got_lists.at[me], own_sems.at[2]),
     ]
     for copy in mine:
         copy.start()
-    for copy in mine + asked:
-        copy.wait()
-    numbers = pltpu.make_async_copy(got_lists, ids, own_sems.at[2])
+    for copy in asked:
+        copy.wait()
+    mine[0].wait()
+    numbers = pltpu.make_async_copy(got_own.at[:, 0 : ids.shape[1]], ids, own_sems.at[3])
     numbers.start()
-    numbers.wait()
+    for copy in (numbers, places, loads[2]):
+        copy.wait()
     copies = send_rows(plane, me, part, ids, table, sent, got, wide, out_sems, in_sems)
-    near = []
+    sides, near = [], []
     for k in range(1, line):
         peer = lax.rem(part - k + line, line)
-        for j, block in enumerate((wide_qkv, wide_out)):
-            far[2 * (k - 1) + j].wait_recv()
-            at = block.at[peer, core]
-            near.append(send(at, at, near_out.at[j, k], near_in.at[j, k], (sibling, part)))
+        far[k - 1].wait_recv()
+        at = quarter(peer, half)
+        sides.append(send(at, at, side_out.at[k], side_in.at[k], (partner, part)))
+        near.append(send(at, at, near_out.at[0, k], near_in.at[0, k], (sibling, part)))
     take_rows(plane, me, part, dims, copies, place, got, wide, out)
-    for copy in copies + far:
+    for k in range(1, line):
+        peer = lax.rem(part - k + line, line)
+        sides[k - 1].wait_recv()
+        at = quarter(peer, 1 - half)
+        near.append(send(at, at, near_out.at[1, k], near_in.at[1, k], (sibling, part)))
+    mine[1].wait()
+    for copy in copies + far + sides:
         copy.wait_send()
-    for copy in near:
+    for copy in told + near:
         copy.wait()
 
 
@@ -457,8 +519,8 @@
     gains[part] = gain[...]
     wide[...] = rows[...].astype(F32)
     copies = []
-    for k in range(1, plane):
-        peer = lax.rem(me + k, plane)
+    others = partners(me, plane)
+    for k, peer in enumerate(others):
         gather_rows(listed(tokens.at[peer], 0), wide, sent.at[peer])
         copies.append(send(sent.at[peer], back.at[me], out_sems.at[k], in_sems.at[k], (peer, part)))
     gather_rows(listed(tokens.at[me], 0), wide, sent.at[me])
@@ -475,25 +537,20 @@
     dense_all[me, 0 : to + whole_rows, :] = share.astype(BF16)
     dense_all[me, to + whole_rows :, :] = summed[last_at : last_at + last_rows, :]
     dense = dense_all.at[me]
-    spread = []
-    for k in range(1, chips):
-        other = lax.rem(chip + k, chips)
-        spread.append(send(dense, dense, chip_out.at[k], chip_in.at[k], (2 * other + core, part)))
-    near = [send(dense, dense, near_out.at[0], near_in.at[0], (sibling, part))]
-
+    spread, near = [], []
     group = max(1, 1280 // capacity)
-    order = [me] + [lax.rem(me - k + plane, plane) for k in range(1, plane)]
+    order = [me] + others
     for first in range(0, plane, group):
         blocks = order[first : first + group]
         grads = [sent.at[blocks[0]] if first == 0 else back.at[blocks[0]]] + [back.at[block] for block in blocks[1:]]
         for k in range(max(first, 1), min(first + group, plane)):
             copies[k - 1].wait_recv()
+        if first + group >= plane:
+            for k in range(1, chips):
+                other = lax.rem(chip + k, chips)
+                spread.append(send(dense, dense, chip_out.at[k], chip_in.at[k], (2 * other + core, part)))
+            near.append(send(dense, dense, near_out.at[0], near_in.at[0], (sibling, part)))
         add_rows(ids, capacity, blocks, grads, total, first == 0)
-    for k in range(1, chips):
-        peer = 2 * lax.rem(chip - k + chips, chips) + core
-        spread[k - 1].wait_recv()
-        near.append(send(dense_all.at[peer], dense_all.at[peer], near_out.at[k], near_in.at[k], (sibling, part)))
-
     square = jnp.zeros((8, LANES), F32)
     for begin, count, weight in ((0, to, 1.0), (to, whole_rows, 1.0 / line), (to + whole_rows, last_rows, 1.0)):
         block = dense_all[me, begin : begin + count, :].astype(F32)
@@ -526,6 +583,10 @@
     tiny = [
         send(along.at[part], along.at[part], along_out.at[k], along_in.at[k], (me, peer)) for k, peer in enumerate(peers)
     ]
+    for k in range(1, chips):
+        peer = 2 * lax.rem(chip - k + chips, chips) + core
+        spread[k - 1].wait_recv()
+        near.append(send(dense_all.at[peer], dense_all.at[peer], near_out.at[k], near_in.at[k], (sibling, part)))
     gain_sum = gains[0]
     for m in range(1, line):
         gain_sum = gain_sum + gains[m]
@@ -549,11 +610,11 @@
     return out
 
 
-def forward_kernel(slots, cnt, x, w_in, gain, w_qkv, w_out, pooled, pm_out, normed_out, qkv, prob, a_out, pm_acc):
+def forward_kernel(slots, cnt, x, w_in, gain, w_all, pooled, pm_out, normed_out, qkv, prob, a_out, pm_acc):
     tower = pl.program_id(0)
     pairs = pooled.shape[1]
     first = lax.axis_index("mp") * pairs
-    parts = w_qkv.shape[0]
+    parts = w_all.shape[0]
     per = LANES // slots
     groups = pairs // per
     heads = 2 * parts
@@ -564,7 +625,7 @@
     normed_out[0] = normed
     for c in range(3):
         for m in range(parts):
-            qkv[0, c * parts + m] = nn(normed, w_qkv[m, 0, c]).astype(BF16)
+            qkv[0, c * parts + m] = nn(normed, w_all[m, 0, c]).astype(BF16)
     lane = iota((LANES, LANES), 1)
     line = iota((LANES, LANES), 0)
     shift = slots.bit_length() - 1
@@ -611,18 +672,23 @@
     high, low = split(nn(live.astype(BF16), xs))
     w = w_in[0].astype(BF16)
     total = nn(high, w) + nn(low, w)
-    for m in range(parts):
-        total = total + nn(pm[:, m * LANES : (m + 1) * LANES], w_out[m, 0])
+    sides = []
+    for j in range(2):
+        side = total[:, j * LANES : (j + 1) * LANES]
+        for m in range(parts):
+            side = side + nn(pm[:, m * LANES : (m + 1) * LANES], w_all[m, 0, 3, j * LANES : (j + 1) * LANES, :])
+        sides.append(side)
+    total = jnp.concatenate(sides, 1)
     count = chain(iota(total.shape, 0), every).astype(F32)
     pooled[0] = (total / count).astype(BF16)
 
 
 def backward_kernel(
-    slots, cnt, x, w_in, gain, w_qkv, w_out, normed_in, qkv, prob, a_in, pm_in, dpooled, demb, d_in, d_gain, d_qkv, d_out, dqkv
+    slots, cnt, x, w_in, gain, w_all, normed_in, qkv, prob, a_in, pm_in, dpooled, demb, d_in, d_gain, d_qkv, d_out, dqkv
 ):
     tower = pl.program_id(0)
     pairs, width = dpooled.shape[1:]
-    parts = w_qkv.shape[0]
+    parts = w_all.shape[0]
     per = LANES // slots
     groups = pairs // per
     heads = 2 * parts
@@ -638,7 +704,11 @@
         grad = tn(pm_in[0, :, m * LANES : (m + 1) * LANES], branch).astype(BF16)
         for j in range(width // LANES):
             d_out[m, 0, j] = grad[:, j * LANES : (j + 1) * LANES]
-        dmix.append(nt(branch, w_out[m, 0]))
+        mix = 0.0
+        for j in range(2):
+            cut = slice(j * LANES, (j + 1) * LANES)
+            mix = mix + nt(branch[:, cut], w_all[m, 0, 3, cut, :])
+        dmix.append(mix)
     lane = iota((LANES, LANES), 1)
     line = iota((LANES, LANES), 0)
     pair_s = lax.shift_right_logical(line, shift)
@@ -683,7 +753,7 @@
     for m in range(parts):
         for c in range(3):
             grad = dqkv[c * parts + m]
-            dnormed = dnormed + nt(grad, w_qkv[m, 0, c])
+            dnormed = dnormed + nt(grad, w_all[m, 0, c])
             d_qkv[m, 0, c] = tn(normed, grad).astype(BF16)
     dnormed = dnormed.astype(BF16).astype(F32)
     xs = x[0]
@@ -729,7 +799,7 @@
     far_three,
     log_prior,
     item_qid,
-    extra,
+    lists,
     positive,
     dpooled,
     d_one,
@@ -764,6 +834,7 @@
         copy.start()
     me, part = enter(plane, line)
     towers, own, width = pooled.shape
+    per = lists.shape[1] - 8
     rows = own * line
     pairs = rows * plane
     peers = [lax.rem(part + k, line) for k in range(1, line)]
@@ -786,7 +857,7 @@
     table = tn(high, hot) + tn(middle, hot) + tn(low, hot)
     prior_row = jnp.sum(jnp.where((qid & 127) == iota((LANES, pairs), 0), table, 0.0), 0, keepdims=True)
     prior_col[...] = jnp.transpose(jnp.broadcast_to(prior_row, (8, pairs)), (1, 0))
-    pos_row = jnp.concatenate([extra[d, 0:1, 0:rows] for d in range(plane)], 1)
+    pos_row = jnp.concatenate([lists[d, per : per + 1, 0:rows] for d in range(plane)], 1)
     pos_own = chain(iota((own, pairs), 0), [positive[part * own + k] for k in range(own)])
     for copy in first:
         copy.wait()
@@ -851,7 +922,7 @@
     log_total = peak + jnp.log(jnp.sum(jnp.exp(logits - peak), 0, keepdims=True))
     picked = jnp.where(iota((pairs, pairs), 0) == pos_row, logits, 0.0)
     gap = log_total - jnp.sum(picked, 0, keepdims=True)
-    loss[...] = jnp.broadcast_to(jnp.sum(gap, 1, keepdims=True), loss.shape)
+    loss[0, 0] = jnp.sum(gap)
     ahead = me * rows + part * own
     mine = INV_TEMP * nt(vectors[0], items) - prior_row
     top = jnp.max(mine, 1, keepdims=True)
@@ -925,10 +996,18 @@
     sources, targets, norm = refs[:arrays], refs[arrays : 2 * arrays], refs[2 * arrays]
     held, in_sems, out_sems = refs[2 * arrays + 1 : 3 * arrays + 1], refs[-2], refs[-1]
     loads = [pltpu.make_async_copy(sources[k], held[k], in_sems.at[k]) for k in range(arrays)]
-    for copy in loads:
-        copy.start()
-    norm[...] = jnp.sqrt(norm_sq[...])
-    factor = jnp.minimum(1.0, CLIP_NORM / norm[0:1, :])
+    ahead = 8
+
+    def load(k):
+        if k < arrays // 3:
+            for copy in loads[3 * k : 3 * k + 3]:
+                copy.start()
+
+    for k in range(ahead):
+        load(k)
+    root = jnp.sqrt(norm_sq[...])
+    norm[0, 0] = jnp.max(root)
+    factor = jnp.minimum(1.0, CLIP_NORM / root[0:1, :])
     stores = []
 
     def finish(k):
@@ -946,6 +1025,7 @@
     def wait(k):
         for copy in loads[3 * k : 3 * k + 3]:
             copy.wait()
+        load(k + ahead)
 
     wait(0)
 
@@ -1039,25 +1119,6 @@
 
     per = capacity // LANES
     small = capacity // 4
-    lists, inverse, own_place, own_small, extra = pl.pallas_call(
-        functools.partial(prep_kernel, plane, capacity, small, line),
-        out_shape=[
-            shape((plane, 2 * per, LANES), I32),
-            shape((plane * per, LANES), I32),
-            shape((slots, LANES), I32),
-            shape((slots, LANES), I32),
-            shape((8, LANES), I32),
-        ],
-        in_specs=[VMEM] * 4,
-        out_specs=[VMEM] * 5,
-        compiler_params=params(16),
-        name="request_lists",
-    )(
-        jnp.transpose(slot_owner[..., 0], (1, 2, 0)),
-        jnp.transpose(slot_row, (1, 2, 0)),
-        jnp.transpose(slot_count),
-        positive.reshape(1, batch),
-    )
     dims = (towers, own, slots)
 
     def row_scratch(count):
@@ -1067,34 +1128,54 @@
             pltpu.VMEM((plane * count, depth), F32),
         ]
 
-    embedded, got_lists, got_extra, wide_qkv, wide_out = pl.pallas_call(
-        functools.partial(fetch_kernel, plane, line, dims),
+    turned = jnp.transpose(w_qkv, (0, 2, 1, 3))
+    embedded, got_own, got_lists, weights, inverse, own_place = pl.pallas_call(
+        functools.partial(fetch_kernel, plane, line, dims, capacity),
         out_shape=[
             shape((own_requests, depth), BF16),
-            shape(lists.shape, I32),
-            shape((plane, 8, LANES), I32),
-            shape((line, towers, 3, width, LANES), BF16),
-            shape((line, towers, LANES, width), BF16),
+            shape((plane, per, LANES), I32),
+            shape((plane, per + 8, LANES), I32),
+            shape((line, towers, 4, width, LANES), BF16),
+            shape((plane * per, LANES), I32),
+            shape((slots, LANES), I32),
         ],
-        in_specs=[VMEM, VMEM, SMEM, VMEM, VMEM, VMEM],
-        out_specs=[VMEM] * 5,
+        in_specs=[VMEM] * 4 + [HBM] * 3,
+        out_specs=[VMEM] * 6,
         scratch_shapes=[
-            pltpu.SMEM(lists.shape, I32),
+            pltpu.VMEM((plane, per, LANES), I32),
+            pltpu.VMEM((slots, LANES), I32),
+            pltpu.VMEM((plane, per + 8, LANES), I32),
+            pltpu.VMEM(embedding.shape, F32),
+            pltpu.VMEM(turned.shape, F32),
+            pltpu.VMEM(w_out.shape, F32),
+            pltpu.SMEM((slots, LANES), I32),
+            pltpu.SMEM((plane, -(-small // LANES), LANES), I32),
             *row_scratch(small),
             DMA((2, plane)),
             DMA((2, plane)),
             DMA((plane,)),
             DMA((plane,)),
+            DMA((line,)),
+            DMA((line,)),
+            DMA((line,)),
+            DMA((line,)),
             DMA((2, line)),
             DMA((2, line)),
-            DMA((2, line)),
-            DMA((2, line)),
+            DMA((4,)),
             DMA((3,)),
         ],
-        compiler_params=params(16, collective_id=2, has_side_effects=True),
+        compiler_params=params(60, collective_id=2, has_side_effects=True),
         name="fetch",
-    )(lists, extra, own_small, embedding, jnp.transpose(w_qkv, (0, 2, 1, 3)), w_out)
-    most = jnp.max(got_extra[:, 1:3, 0], 0)
+    )(
+        jnp.transpose(slot_owner[..., 0], (1, 2, 0)),
+        jnp.transpose(slot_row, (1, 2, 0)),
+        jnp.transpose(slot_count),
+        positive.reshape(1, batch),
+        embedding,
+        turned,
+        w_out,
+    )
+    most = jnp.max(got_lists[:, per + 1 : per + 3, 0], 0)
 
     def refetch(ids, place, table, _):
         return pl.pallas_call(
@@ -1107,7 +1188,7 @@
             name="refetch",
         )(ids, place, table)
 
-    embedded = lax.cond(most[0] > small, refetch, lambda *given: given[3], got_lists, own_place, embedding, embedded)
+    embedded = lax.cond(most[0] > small, refetch, lambda *given: given[3], got_own, own_place, embedding, embedded)
     embedded = embedded.reshape(towers, tokens, depth)
 
     counts = jnp.transpose(slot_count)
@@ -1116,7 +1197,7 @@
     per_group = LANES // slots
     lead = lambda *dims: pl.BlockSpec((1,) + dims, lambda t: (t,) + (0,) * len(dims))
     qkv_spec = pl.BlockSpec((line, 1, 3, width, LANES), lambda t: (0, t, 0, 0, 0))
-    out_spec = pl.BlockSpec((line, 1, LANES, width), lambda t: (0, t, 0, 0))
+    all_spec = pl.BlockSpec((line, 1, 4, width, LANES), lambda t: (0, t, 0, 0, 0))
     pooled, pm, normed, qkv, prob, spread = pl.pallas_call(
         functools.partial(forward_kernel, slots),
         grid=(towers,),
@@ -1128,7 +1209,7 @@
             shape((towers, groups, heads, LANES, LANES), BF16),
             shape((towers, groups, per_group * heads, LANES), BF16),
         ],
-        in_specs=[SMEM, lead(tokens, depth), lead(depth, width), VMEM, qkv_spec, out_spec],
+        in_specs=[SMEM, lead(tokens, depth), lead(depth, width), VMEM, all_spec],
         out_specs=[
             lead(own, width),
             lead(own, line * LANES),
@@ -1140,7 +1221,7 @@
         scratch_shapes=[pltpu.VMEM((groups, per_group, line * LANES), F32)],
         compiler_params=params(20),
         name="attention_forward",
-    )(counts, embedded, w_in, norm_gain, wide_qkv, wide_out)
+    )(counts, embedded, w_in, norm_gain, weights)
 
     dpooled, d_one, d_two, d_three, loss = pl.pallas_call(
         functools.partial(upper_kernel, plane, line),
@@ -1149,10 +1230,10 @@
             shape((towers, units // LANES, width, LANES), BF16),
             shape((towers, seconds // LANES, units, LANES), BF16),
             shape((towers, width // LANES, seconds, LANES), BF16),
-            shape((8, LANES), F32),
+            shape((1, 1), F32),
         ],
         in_specs=[VMEM] + [HBM] * 3 + [VMEM] * 3 + [SMEM],
-        out_specs=[VMEM] * 5,
+        out_specs=[VMEM] * 4 + [SMEM],
         scratch_shapes=[
             pltpu.VMEM((towers, line, own, width), BF16),
             pltpu.VMEM((towers, line, own, seconds), BF16),
@@ -1183,7 +1264,7 @@
         w_three,
         log_prior.reshape(-1, LANES),
         item_qid.reshape(1, pairs),
-        got_extra,
+        got_lists,
         positive,
     )
 
@@ -1202,8 +1283,7 @@
             lead(tokens, depth),
             lead(depth, width),
             VMEM,
-            qkv_spec,
-            out_spec,
+            all_spec,
             lead(tokens, width),
             lead(3 * line, tokens, LANES),
             lead(groups, heads, LANES, LANES),
@@ -1221,7 +1301,7 @@
         scratch_shapes=[pltpu.VMEM((3 * line, tokens, LANES), BF16)],
         compiler_params=params(24),
         name="attention_backward",
-    )(counts, embedded, w_in, norm_gain, wide_qkv, wide_out, normed, qkv, prob, spread, pm, dpooled)
+    )(counts, embedded, w_in, norm_gain, weights, normed, qkv, prob, spread, pm, dpooled)
 
     def shares(grad, lead=()):
         rows = grad.size // (LANES * plane * (lead[0] if lead else 1))
@@ -1305,7 +1385,7 @@
             ],
             compiler_params=params(36, collective_id=number, has_side_effects=True),
             name="tail",
-        )(*given)
+        )(given[0][:, : -(-count // LANES)], *given[1:])
 
     medium = capacity * 5 // 8
     table_grad, dense_all, norm_sq, gain_all = lax.cond(
@@ -1331,9 +1411,9 @@
     blocks = tuple((k + 1, size, height, wide) for k, (size, height, wide) in enumerate(zip(sizes, heights, wides)))
     *done, norm = pl.pallas_call(
         functools.partial(update_kernel, blocks),
-        out_shape=[shape(w.shape, F32) for w in given] + [shape((8, LANES), F32)],
+        out_shape=[shape(w.shape, F32) for w in given] + [shape((1, 1), F32)],
         in_specs=[VMEM] * 4 + [HBM] * len(given),
-        out_specs=[HBM] * len(given) + [VMEM],
+        out_specs=[HBM] * len(given) + [SMEM],
         scratch_shapes=[pltpu.VMEM(w.shape, F32) for w in given] + [DMA((len(given),))] * 2,
         compiler_params=params(57),
         name="update",
@@ -1343,7 +1423,7 @@
         jnp.transpose(w.reshape(towers, 3, width, LANES), (0, 2, 1, 3)) for w in done[3:6]
     ]
     new = done[:3] + back(4, w_in) + done[21:24] + unturned + back(2, w_out) + back(5, w_one) + back(6, w_two)
-    return (loss[0, 0], norm[0, 0], *new, *back(3, w_three))
+    return (loss.reshape(()), norm.reshape(()), *new, *back(3, w_three))
 
 
 def solution(mesh):

time: 191 us -> 176 us (0.921)
  local copies, waits for them, and re-layouts: 9.26 us -> 0.66 us
  Pallas kernels: 178 us -> 170 us
    unnamed x40 -> x22, local copies, waits for them, and re-layouts: 6.97 us -> 0.07 us
    pallas_call x1, Pallas kernels: 35.9 us -> 32.4 us  [shards(): pl.pallas_call(functools.partial(upper_kernel, plane, line), out_shape=[s...]
    pallas_call x1, Pallas kernels: 46 us -> 43.4 us  [tail(): pl.pallas_call(functools.partial(tail_kernel, plane, line, count, cuts),...]
    pallas_call x2 -> x1, Pallas kernels: 33.7 us -> 32 us  [shards(): pl.pallas_call(functools.partial(fetch_kernel, plane, line, dims, capacit...]
where the time goes in v5:
time: 176 us; the launch traced here: 175 us
  Pallas kernels  170 us (97%)
  between operations  4 us (2%)
    pallas_call x1, Pallas kernels, tail(): pl.pallas_call(functools.partial(tail_kernel, plane, line, count, cuts),...  43.4 us
    pallas_call x1, Pallas kernels, shards(): pl.pallas_call(functools.partial(upper_kernel, plane, line), out_shape=[s...  32.4 us
    pallas_call x1, Pallas kernels, shards(): pl.pallas_call(functools.partial(fetch_kernel, plane, line, dims, capacit...  32 us
    pallas_call x1, Pallas kernels, shards(): pl.pallas_call(functools.partial(spread_kernel, plane, line), out_shape=[...  27.2 us
    pallas_call x1, Pallas kernels, shards(): pl.pallas_call(functools.partial(update_kernel, blocks), out_shape=[shape...  14.3 us
    pallas_call x1, Pallas kernels, shards(): pl.pallas_call(functools.partial(backward_kernel, slots), grid=(towers,),...  10.9 us
    pallas_call x1, Pallas kernels, shards(): pl.pallas_call(functools.partial(forward_kernel, slots), grid=(towers,),...  9.69 us

profile of v5, /device:TPU:0, one launch (start us, length us, event | category | flops | bytes accessed | tf_op | source)
XLA Modules:
  0.0 175.4 jit_solution(13474281854733592575)
XLA Ops:
  0.7 0.0 copy-start.3
  0.7 0.0 copy-start.5
  0.7 0.0 copy-start.7
  0.7 32.0 %fetch.1 = (bf16[1024,128]{1,0:T(8,128)(2,1)}, s32[8,8,128]{2,1,0:T(8,128)}, s32[8,16,128]{2,1,0:T(8,128)S(1)}, bf16[4,2,4,256,128]{4,3,2,1,0:T(8,128)(2,1)}, s3...) custom-call(s32[2,32,64]{2,1,0:T(8,128)} %bitcast.109, s32[2,32,64]{2,1,0:T(8,128)} %bitcast.110, s32[2,64]{1,0:T(2,128)} %bitcast.84, ...), custom_call_target="tpu_custom_call" | custom-call | tf_op jit(solution)/shard_map/fetch/pallas_call | solution.py:1132
  32.8 0.0 copy-start
  32.8 0.1 slice_reduce_fusion
  32.9 0.6 fusion
  34.8 0.0 copy-start.1
  34.8 0.0 copy-start.6
  34.8 0.0 copy-start.8
  34.8 0.0 copy-start.9
  34.8 0.2 conditional.2
  35.0 0.0 copy-done.3
  35.1 0.0 copy-start.2
  35.1 0.0 copy-start.4
  35.1 9.7 %attention_forward.1 = (bf16[2,16,256]{2,1,0:T(8,128)(2,1)S(1)}, bf16[2,16,512]{2,1,0:T(8,128)(2,1)S(1)}, bf16[2,512,256]{2,1,0:T(8,128)(2,1)S(1)}, bf16[2,12,51...) custom-call(s32[2,64]{1,0:T(2,128)S(1)} %bitcast.85, ...), custom_call_target="tpu_custom_call" | custom-call | tf_op jit(solution)/shard_map/attention_forward/pallas_call | solution.py:1201
  44.8 0.0 copy-done.6
  44.8 32.4 %upper.1 = (bf16[2,16,256]{2,1,0:T(8,128)(2,1)S(1)}, bf16[2,2,256,128]{3,2,1,0:T(8,128)(2,1)S(1)}, bf16[2,4,256,128]{3,2,1,0:T(8,128)(2,1)S(1)}, bf16[2,2,512,128]{3,2,1,0:T(8,128)(2,1)S(1)}, f32[1,1]{1,0:T(1,128)}) custom-call(bf16[2,16,256]{2,1,0:T(8,128)(2,1)S(1)} %get-tuple-element.133.pooled, f32[2,256,256]{2,1,0:T(8,128)S(1)} %copy-done.4, ...), custom_call_target="tpu_custom_call" | custom-call | tf_op jit(solution)/shard_map/upper/pallas_call | solution.py:1226
  77.3 10.9 %attention_backward.1 = (bf16[2,512,128]{2,1,0:T(8,128)(2,1)S(1)}, bf16[2,2,128,128]{3,2,1,0:T(8,128)(2,1)S(1)}, f32[8,128]{1,0:T(8,128)S(1)}, bf16[4,2,3,256,12...) custom-call(s32[2,64]{1,0:T(2,128)S(1)} %bitcast.86, bf16[2,512,128]{2,1,0:T(8,128)(2,1)} %get-tuple-element.244.x, ...), custom_call_target="tpu_custom_call" | custom-call | tf_op jit(solution)/shard_map/attention_backward/pallas_call | solution.py:1271
  88.2 27.2 %spread.1 = (bf16[4,1024,128]{2,1,0:T(8,128)(2,1)S(1)}, bf16[1728,128]{1,0:T(8,128)(2,1)S(1)}, f32[8,128]{1,0:T(8,128)S(1)}) custom-call(bf16[1024,128]{1,0:T(8,128)(2,1)S(1)} %bitcast.81, bf16[4,4,2,192,128]{4,3,2,1,0:T(8,128)(2,1)S(1)} %bitcast.76, bf16[4,4,2,64,128]{4,3,2,1,0:T(8,128)(2,1)S(1)} %bitcast.79, bf16[4,2,256,128]{3,2,1,0:T(8,128)(2,1)S(1)} %bitcast.78, ...), custom_call_target="tpu_custom_call" | custom-call | tf_op jit(solution)/shard_map/spread/pallas_call | solution.py:1313
  115.4 0.0 copy-start.10
  115.4 43.9 %conditional.3 = ((f32[4096,128]{1,0:T(8,128)}, bf16[8,960,128]{2,1,0:T(8,128)(2,1)}, f32[8,128]{1,0:T(8,128)S(1)}, f32[8,128]{1,0:T(8,128)S(1)})) conditional(s32[]{:T(128)} %bitcast.12, (s32[8,8,128]{2,1,0:T(8,128)S(1)}, s32[8,16,128]{2,1,0:T(8,128)S(1)}, bf16[4096,128]{1,0:T(8,128)(2,1)S(1)}, bf16[1728,128]{1,0:T(8,128)(2,1)S(1)}, ...), branch_computations={%region_3.0_spmd, %region_4.0_spmd} | conditional | bytes 8 | solution.py:1391
  115.6 43.4 %tail.2 = (f32[4096,128]{1,0:T(8,128)}, bf16[8,960,128]{2,1,0:T(8,128)(2,1)}, f32[8,128]{1,0:T(8,128)S(1)}, f32[8,128]{1,0:T(8,128)S(1)}) custom-call(s32[8,5,128]{2,1,0:T(8,128)S(1)} %bitcast.108, s32[8,16,128]{2,1,0:T(8,128)S(1)} %get-tuple-element.39.ids, bf16[4096,128]{1,0:T(8,128)(2,1)S(1)} %get-tuple-element.40.rows, ...), custom_call_target="tpu_custom_call" | custom-call | tf_op jit(solution)/shard_map/cond/branch_0_fun/tail/pallas_call | solution.py:1352
  159.3 14.3 %update.1 = (f32[4096,128]{1,0:T(8,128)}, f32[4096,128]{1,0:T(8,128)}, f32[4096,128]{1,0:T(8,128)}, f32[1536,128]{1,0:T(8,128)}, f32[1536,128]{1,0:T(8,128)}, /*...) custom-call(f32[8,128]{1,0:T(8,128)S(1)} %get-tuple-element.153.norm, ...), custom_call_target="tpu_custom_call" | custom-call | tf_op jit(solution)/shard_map/update/pallas_call | solution.py:1412
  (9 shorter events, 0.0 us)
Async XLA Ops:
  0.7 34.4 %copy-start.3 = (f32[2,128,256]{2,1,0:T(8,128)S(1)}, f32[2,128,256]{2,1,0:T(8,128)}, u32[]{:S(2)}) copy-start(f32[2,128,256]{2,1,0:T(8,128)} %w_in.3) | copy-start | bytes 786436
  0.7 34.4 %copy-start.5 = (f32[2,256]{1,0:T(2,128)S(1)}, f32[2,256]{1,0:T(2,128)}, u32[]{:S(2)}) copy-start(f32[2,256]{1,0:T(2,128)} %refs_21_.1) | copy-start | bytes 6148
  0.7 34.3 %copy-start.7 = (s32[64,2]{0,1:T(2,128)S(1)}, s32[64,2]{0,1:T(2,128)}, u32[]{:S(2)}) copy-start(s32[64,2]{0,1:T(2,128)} %param.36) | copy-start | bytes 1540
  32.8 2.3 %copy-start = (bf16[4,2,4,256,128]{4,3,2,1,0:T(8,128)(2,1)S(1)}, bf16[4,2,4,256,128]{4,3,2,1,0:T(8,128)(2,1)}, u32[]{:S(2)}) copy-start(bf16[4,2,4,256,128]{4,3,2,1,0:T(8,128)(2,1)} %get-tuple-element.132.w_all) | copy-start | bytes 6291460
  34.8 10.0 %copy-start.1 = (f32[2,256,512]{2,1,0:T(8,128)S(1)}, f32[2,256,512]{2,1,0:T(8,128)}, u32[]{:S(2)}) copy-start(f32[2,256,512]{2,1,0:T(8,128)} %far_two.1) | copy-start | bytes 3145732
  34.8 10.0 %copy-start.6 = (f32[4096]{0:T(1024)S(1)}, f32[4096]{0:T(1024)}, u32[]{:S(2)}) copy-start(f32[4096]{0:T(1024)} %param.39) | copy-start | bytes 49156
  34.8 10.0 %copy-start.8 = (s32[512]{0:T(512)S(1)}, s32[512]{0:T(512)}, u32[]{:S(2)}) copy-start(s32[512]{0:T(512)} %param.37) | copy-start | bytes 6148
  34.8 10.0 %copy-start.9 = (s32[64]{0:T(128)S(1)}, s32[64]{0:T(128)}, u32[]{:S(2)}) copy-start(s32[64]{0:T(128)} %positive.1) | copy-start | bytes 772
  35.1 9.8 %copy-start.2 = (f32[2,512,256]{2,1,0:T(8,128)S(1)}, f32[2,512,256]{2,1,0:T(8,128)}, u32[]{:S(2)}) copy-start(f32[2,512,256]{2,1,0:T(8,128)} %far_three.1) | copy-start | bytes 3145732
  35.1 9.8 %copy-start.4 = (f32[2,256,256]{2,1,0:T(8,128)S(1)}, f32[2,256,256]{2,1,0:T(8,128)}, u32[]{:S(2)}) copy-start(f32[2,256,256]{2,1,0:T(8,128)} %far_one.1) | copy-start | bytes 1572868
  115.4 43.9 %copy-start.10 = (f32[4096,128]{1,0:T(8,128)S(1)}, f32[4096,128]{1,0:T(8,128)}, u32[]{:S(2)}) copy-start(f32[4096,128]{1,0:T(8,128)} %refs_0_.1) | copy-start | bytes 6291460

commit v6 on v5

--- a/solution.py
+++ b/solution.py
@@ -347,90 +347,6 @@
         copy.wait_send()
     for copy in told + near:
         copy.wait()
-
-
-def spread_kernel(
-    plane,
-    line,
-    mine,
-    d_qkv,
-    d_out,
-    d_three,
-    d_in,
-    d_one,
-    d_two,
-    gain,
-    out,
-    summed,
-    gain_sum,
-    near_split,
-    near_whole,
-    half,
-    got,
-    gains,
-    far_out,
-    far_in,
-    near_out,
-    near_in,
-    sum_out,
-    sum_in,
-    gain_out,
-    gain_in,
-    own_sem,
-):
-    me, part = enter(plane, line)
-    chips = plane // 2
-    core = lax.rem(me, 2)
-    chip = me // 2
-    sibling = me + 1 - 2 * core
-    copies = []
-    for k in range(1, line):
-        peer = lax.rem(part + k, line)
-        copies.append(send(mine, out.at[part], far_out.at[k], far_in.at[k], (me, peer)))
-    split_grads, whole_grads = (d_qkv, d_out), (d_three, d_in, d_one, d_two)
-    first = []
-    for j, grad in enumerate(split_grads):
-        first.append(send(grad.at[:, :, 1 - core], near_split[j], near_out.at[j], near_in.at[j], (sibling, part)))
-    for j, grad in enumerate(whole_grads, len(split_grads)):
-        first.append(send(grad.at[:, 1 - core], near_whole[j - 2], near_out.at[j], near_in.at[j], (sibling, part)))
-    for k in range(1, plane):
-        peer = lax.rem(me + k, plane)
-        copies.append(send(gain, gains.at[me], gain_out.at[k], gain_in.at[k], (peer, part)))
-    own = pltpu.make_async_copy(mine, out.at[part], own_sem)
-    own.start()
-    gains[me] = gain[...]
-    for copy in first:
-        copy.wait()
-    for c in range(chips):
-        at = 0
-        for j, grad in enumerate(split_grads):
-            rows = grad.shape[3]
-            for m in range(line):
-                total = grad[m, c, core].astype(F32) + near_split[j][m, c].astype(F32)
-                half[c, at : at + rows, :] = total.astype(BF16)
-                at += rows
-        for j, grad in enumerate(whole_grads):
-            rows = grad.shape[2]
-            total = grad[c, core].astype(F32) + near_whole[j][c].astype(F32)
-            half[c, at : at + rows, :] = total.astype(BF16)
-            at += rows
-    sums = []
-    for k in range(1, chips):
-        to = lax.rem(chip + k, chips)
-        sums.append(send(half.at[to], got.at[k - 1], sum_out.at[k], sum_in.at[k], (2 * to + core, part)))
-    for copy in sums:
-        copy.wait()
-    total = half[chip].astype(F32)
-    for k in range(chips - 1):
-        total = total + got[k].astype(F32)
-    summed[...] = total.astype(BF16)
-    own.wait()
-    for copy in copies:
-        copy.wait()
-    total = gains[0]
-    for d in range(1, plane):
-        total = total + gains[d]
-    gain_sum[...] = total
 
 
 def add_rows(ids, count, blocks, grads, total, fresh):
@@ -683,10 +599,18 @@
     pooled[0] = (total / count).astype(BF16)
 
 
-def backward_kernel(
-    slots, cnt, x, w_in, gain, w_all, normed_in, qkv, prob, a_in, pm_in, dpooled, demb, d_in, d_gain, d_qkv, d_out, dqkv
+def put(target, size, first, value):
+    done = 0
+    while done < value.shape[0]:
+        share, inside = divmod(first + done, size)
+        count = min(size - inside, value.shape[0] - done)
+        target[share // 2, share % 2, inside : inside + count, :] = value[done : done + count]
+        done += count
+
+
+def backward_tower(
+    tower, slots, cnt, x, w_in, gain, w_all, normed_in, qkv, prob, a_in, pm_in, dpooled, demb, d_in, d_gain, d_qkv, d_out, dqkv
 ):
-    tower = pl.program_id(0)
     pairs, width = dpooled.shape[1:]
     parts = w_all.shape[0]
     per = LANES // slots
@@ -697,17 +621,18 @@
     first = lax.axis_index("mp") * pairs
     every = [cnt[tower, first + k] for k in range(pairs)]
     count = chain(iota((pairs, width), 0), every).astype(F32)
-    dsum = dpooled[0].astype(F32) / count
+    dsum = dpooled[tower].astype(F32) / count
     branch = dsum.astype(BF16)
     dmix = []
     for m in range(parts):
-        grad = tn(pm_in[0, :, m * LANES : (m + 1) * LANES], branch).astype(BF16)
+        grad = tn(pm_in[tower, :, m * LANES : (m + 1) * LANES], branch).astype(BF16)
         for j in range(width // LANES):
-            d_out[m, 0, j] = grad[:, j * LANES : (j + 1) * LANES]
+            begin = (tower * (width // LANES) + j) * LANES
+            put(d_out.at[m], d_out.shape[3], begin, grad[:, j * LANES : (j + 1) * LANES])
         mix = 0.0
         for j in range(2):
             cut = slice(j * LANES, (j + 1) * LANES)
-            mix = mix + nt(branch[:, cut], w_all[m, 0, 3, cut, :])
+            mix = mix + nt(branch[:, cut], w_all[m, tower, 3, cut, :])
         dmix.append(mix)
     lane = iota((LANES, LANES), 1)
     line = iota((LANES, LANES), 0)
@@ -728,48 +653,44 @@
             head = iota((per * heads, LANES), 1) // DH + 2 * m
             stack = jnp.where(own_head == head, spread, 0.0).astype(BF16)
             stacks.append(stack)
-            dots = dots + nt(stack, qkv[0, 2 * parts + m, rows, :])
+            dots = dots + nt(stack, qkv[tower, 2 * parts + m, rows, :])
         dots = jnp.where(own_pair == token_pair, dots, 0.0)
         pull = dots[0:heads]
         for k in range(1, per):
             pull = pull + dots[k * heads : (k + 1) * heads]
         for m in range(parts):
-            query, key = qkv[0, m, rows, :], qkv[0, parts + m, rows, :]
+            query, key = qkv[tower, m, rows, :], qkv[tower, parts + m, rows, :]
             none = jnp.zeros_like(query)
             dq = jnp.zeros((LANES, LANES), F32)
             dk = jnp.zeros((LANES, LANES), F32)
             for half in range(2):
                 h = 2 * m + half
-                p = prob[0, g, h].astype(F32)
+                p = prob[tower, g, h].astype(F32)
                 t = p * pull[h : h + 1, :]
                 ds = ((t - p * jnp.sum(t, 1, keepdims=True)) * scale).astype(BF16)
                 dq = dq + nn(ds, jnp.where(halves[half], key, none))
                 dk = dk + tn(ds, jnp.where(halves[half], query, none))
             dqkv[m, rows, :] = dq.astype(BF16)
             dqkv[parts + m, rows, :] = dk.astype(BF16)
-            dqkv[2 * parts + m, rows, :] = tn(a_in[0, g], stacks[m]).astype(BF16)
-    normed = normed_in[0]
+            dqkv[2 * parts + m, rows, :] = tn(a_in[tower, g], stacks[m]).astype(BF16)
+    normed = normed_in[tower]
     dnormed = jnp.zeros((tokens, width), F32)
     for m in range(parts):
         for c in range(3):
             grad = dqkv[c * parts + m]
-            dnormed = dnormed + nt(grad, w_all[m, 0, c])
-            d_qkv[m, 0, c] = tn(normed, grad).astype(BF16)
+            dnormed = dnormed + nt(grad, w_all[m, tower, c])
+            put(d_qkv.at[m], d_qkv.shape[3], (tower * 3 + c) * width, tn(normed, grad).astype(BF16))
     dnormed = dnormed.astype(BF16).astype(F32)
-    xs = x[0]
-    w = w_in[0].astype(BF16)
+    xs = x[tower]
+    w = w_in[tower].astype(BF16)
     hidden = nn(xs, w)
     inverse = lax.rsqrt(jnp.mean(hidden * hidden, -1, keepdims=True) + EPS)
     unit = hidden * inverse
     grad = jnp.sum(dnormed * unit, 0, keepdims=True)
-
-    @pl.when(tower == 0)
-    def _():
-        d_gain[...] = jnp.zeros_like(d_gain)
-
     for j in range(width // LANES):
-        d_gain[pl.ds(tower * (width // LANES) + j, 1), :] = grad[:, j * LANES : (j + 1) * LANES]
-    scaled = dnormed * gain[pl.ds(tower, 1), :]
+        r = tower * (width // LANES) + j
+        d_gain[r : r + 1, :] = grad[:, j * LANES : (j + 1) * LANES]
+    scaled = dnormed * gain[tower : tower + 1, :]
     dh = inverse * (scaled - unit * jnp.mean(scaled * unit, -1, keepdims=True))
     spread = jnp.broadcast_to(dsum[:, None, :], (pairs, slots, width))
     slot = iota((pairs, slots, width), 1)
@@ -778,8 +699,133 @@
     dhidden = (spread + dh).astype(BF16)
     grad = tn(xs, dhidden).astype(BF16)
     for j in range(width // LANES):
-        d_in[0, j] = grad[:, j * LANES : (j + 1) * LANES]
-    demb[0] = nt(dhidden, w).astype(BF16)
+        begin = (tower * (width // LANES) + j) * xs.shape[1]
+        put(d_in, d_in.shape[2], begin, grad[:, j * LANES : (j + 1) * LANES])
+    demb[...] = nt(dhidden, w).astype(BF16)
+
+
+def backward_kernel(
+    plane,
+    line,
+    slots,
+    cnt,
+    x,
+    w_in,
+    gain,
+    w_all,
+    normed,
+    qkv,
+    prob,
+    a_in,
+    pm,
+    dpooled,
+    d_three,
+    d_one,
+    d_two,
+    out,
+    summed,
+    gain_sum,
+    d_qkv,
+    d_out,
+    d_in,
+    d_gain,
+    dqkv,
+    near_split,
+    near_whole,
+    half,
+    got,
+    got_late,
+    gains,
+    far_out,
+    far_in,
+    near_out,
+    near_in,
+    sum_out,
+    sum_in,
+    gain_out,
+    gain_in,
+):
+    me, part = enter(plane, line)
+    chips = plane // 2
+    core = lax.rem(me, 2)
+    chip = me // 2
+    sibling = me + 1 - 2 * core
+    towers, tokens = x.shape[:2]
+    late, early = (d_in,), (d_three, d_one, d_two)
+    nears = [send(grad.at[:, 1 - core], near_whole[1 + j], near_out.at[j], near_in.at[j], (sibling, part)) for j, grad in enumerate(early)]
+    copies = []
+
+    def tower(t):
+        demb = out.at[part, t * tokens : (t + 1) * tokens]
+        backward_tower(
+            t, slots, cnt, x, w_in, gain, w_all, normed, qkv, prob, a_in, pm, dpooled, demb, d_in, d_gain, d_qkv, d_out, dqkv
+        )
+        for k in range(1, line):
+            peer = lax.rem(part + k, line)
+            copies.append(send(demb, demb, far_out.at[t, k], far_in.at[t, k], (me, peer)))
+
+    def whole(c, at, grad, near):
+        rows = grad.shape[2]
+        half[c, at : at + rows, :] = (grad[c, core].astype(F32) + near[c].astype(F32)).astype(BF16)
+        return at + rows
+
+    def exchange(begin, end, target, sems):
+        sums = []
+        for k in range(1, chips):
+            to = lax.rem(chip + k, chips)
+            source = half.at[to, begin:end]
+            sums.append(send(source, target.at[k - 1], sum_out.at[sems, k], sum_in.at[sems, k], (2 * to + core, part)))
+        return sums
+
+    def collect(begin, end, target, sums):
+        for copy in sums:
+            copy.wait()
+        total = half[chip, begin:end, :].astype(F32)
+        for k in range(chips - 1):
+            total = total + target[k].astype(F32)
+        summed[begin:end, :] = total.astype(BF16)
+
+    first = line * (d_qkv.shape[3] + d_out.shape[3]) + d_in.shape[2]
+    d_gain[...] = jnp.zeros_like(d_gain)
+    tower(0)
+    for copy in nears:
+        copy.wait()
+    for c in range(chips):
+        at = first
+        for j, grad in enumerate(early):
+            at = whole(c, at, grad, near_whole[1 + j])
+    last = at
+    sums = exchange(first, last, got, 0)
+    for t in range(1, towers):
+        tower(t)
+    nears = []
+    for j, grad in enumerate((d_qkv, d_out)):
+        nears.append(send(grad.at[:, :, 1 - core], near_split[j], near_out.at[3 + j], near_in.at[3 + j], (sibling, part)))
+    nears.append(send(d_in.at[:, 1 - core], near_whole[0], near_out.at[5], near_in.at[5], (sibling, part)))
+    for k in range(1, plane):
+        peer = lax.rem(me + k, plane)
+        copies.append(send(d_gain, gains.at[me], gain_out.at[k], gain_in.at[k], (peer, part)))
+    gains[me] = d_gain[...]
+    for copy in nears:
+        copy.wait()
+    for c in range(chips):
+        at = 0
+        for grad, near in zip((d_qkv, d_out), near_split):
+            rows = grad.shape[3]
+            for m in range(line):
+                total = grad[m, c, core].astype(F32) + near[m, c].astype(F32)
+                half[c, at : at + rows, :] = total.astype(BF16)
+                at += rows
+        whole(c, at, d_in, near_whole[0])
+    late_sums = exchange(0, first, got_late, 1)
+    collect(first, last, got, sums)
+    collect(0, first, got_late, late_sums)
+    for copy in copies:
+        copy.wait()
+    total = gains[0]
+    for d in range(1, plane):
+        total = total + gains[d]
+    gain_sum[...] = total
 
 
 def gelu_parts(v):
@@ -1196,7 +1242,6 @@
     groups = tokens // LANES
     per_group = LANES // slots
     lead = lambda *dims: pl.BlockSpec((1,) + dims, lambda t: (t,) + (0,) * len(dims))
-    qkv_spec = pl.BlockSpec((line, 1, 3, width, LANES), lambda t: (0, t, 0, 0, 0))
     all_spec = pl.BlockSpec((line, 1, 4, width, LANES), lambda t: (0, t, 0, 0, 0))
     pooled, pm, normed, qkv, prob, spread = pl.pallas_call(
         functools.partial(forward_kernel, slots),
@@ -1268,76 +1313,60 @@
         positive,
     )
 
-    demb, d_in, d_gain, d_qkv, d_out = pl.pallas_call(
-        functools.partial(backward_kernel, slots),
-        grid=(towers,),
-        out_shape=[
-            shape((towers, tokens, depth), BF16),
-            shape((towers, width // LANES, depth, LANES), BF16),
-            shape((8, LANES), F32),
-            shape((line, towers, 3, width, LANES), BF16),
-            shape((line, towers, width // LANES, LANES, LANES), BF16),
-        ],
-        in_specs=[
-            SMEM,
-            lead(tokens, depth),
-            lead(depth, width),
-            VMEM,
-            all_spec,
-            lead(tokens, width),
-            lead(3 * line, tokens, LANES),
-            lead(groups, heads, LANES, LANES),
-            lead(groups, per_group * heads, LANES),
-            lead(own, line * LANES),
-            lead(own, width),
-        ],
-        out_specs=[
-            lead(tokens, depth),
-            lead(width // LANES, depth, LANES),
-            pl.BlockSpec((8, LANES), lambda t: (0, 0)),
-            qkv_spec,
-            pl.BlockSpec((line, 1, width // LANES, LANES, LANES), lambda t: (0, t, 0, 0, 0)),
-        ],
-        scratch_shapes=[pltpu.VMEM((3 * line, tokens, LANES), BF16)],
-        compiler_params=params(24),
-        name="attention_backward",
-    )(counts, embedded, w_in, norm_gain, weights, normed, qkv, prob, spread, pm, dpooled)
-
-    def shares(grad, lead=()):
-        rows = grad.size // (LANES * plane * (lead[0] if lead else 1))
-        return grad.reshape(*lead, plane // 2, 2, rows, LANES)
-
-    grads = [shares(d_qkv, (line,)), shares(d_out, (line,))] + [shares(g) for g in (d_three, d_in, d_one, d_two)]
-    sizes = [g.shape[-2] for g in grads]
+    totals = (towers * 3 * width, towers * width, towers * depth * width // LANES)
+    totals += tuple(grad.size // LANES for grad in (d_three, d_one, d_two))
+    sizes = [total // plane for total in totals]
+    shares = lambda grad: grad.reshape(plane // 2, 2, -1, LANES)
     share = line * (sizes[0] + sizes[1]) + sum(sizes[2:])
+    early = sum(sizes[3:])
     every, summed, gain_sum = pl.pallas_call(
-        functools.partial(spread_kernel, plane, line),
+        functools.partial(backward_kernel, plane, line, slots),
         out_shape=[
             shape((line, own_requests, depth), BF16),
             shape((share, LANES), BF16),
             shape((8, LANES), F32),
         ],
-        in_specs=[VMEM] * 8,
+        in_specs=[SMEM] + [VMEM] * 13,
         out_specs=[VMEM] * 3,
         scratch_shapes=[
+            pltpu.VMEM((line, plane // 2, 2, sizes[0], LANES), BF16),
+            pltpu.VMEM((line, plane // 2, 2, sizes[1], LANES), BF16),
+            pltpu.VMEM((plane // 2, 2, sizes[2], LANES), BF16),
+            pltpu.VMEM((8, LANES), F32),
+            pltpu.VMEM((3 * line, tokens, LANES), BF16),
             [pltpu.VMEM((line, plane // 2, size, LANES), BF16) for size in sizes[:2]],
             [pltpu.VMEM((plane // 2, size, LANES), BF16) for size in sizes[2:]],
             pltpu.VMEM((plane // 2, share, LANES), BF16),
-            pltpu.VMEM((plane // 2 - 1, share, LANES), BF16),
+            pltpu.VMEM((plane // 2 - 1, early, LANES), BF16),
+            pltpu.VMEM((plane // 2 - 1, share - early, LANES), BF16),
             pltpu.VMEM((plane, 8, LANES), F32),
-            DMA((line,)),
-            DMA((line,)),
+            DMA((towers, line)),
+            DMA((towers, line)),
             DMA((6,)),
             DMA((6,)),
-            DMA((plane // 2,)),
-            DMA((plane // 2,)),
+            DMA((2, plane // 2)),
+            DMA((2, plane // 2)),
             DMA((plane,)),
             DMA((plane,)),
-            DMA,
         ],
-        compiler_params=params(20, collective_id=4, has_side_effects=True),
-        name="spread",
-    )(demb.reshape(own_requests, depth), *grads, d_gain)
+        compiler_params=params(40, collective_id=4, has_side_effects=True),
+        name="attention_backward",
+    )(
+        counts,
+        embedded,
+        w_in,
+        norm_gain,
+        weights,
+        normed,
+        qkv,
+        prob,
+        spread,
+        pm,
+        dpooled,
+        shares(d_three),
+        shares(d_one),
+        shares(d_two),
+    )
     whole_at = line * (sizes[0] + sizes[1])
     whole_rows = sizes[2] + sizes[3]
     last_rows = sizes[4] + sizes[5]
@@ -1402,11 +1431,11 @@
     turn = lambda w: flat(jnp.transpose(w, (0, 2, 1, 3)))
     given = [embedding, embedding_mom, embedding_avg]
     given += [turn(w) for w in (w_qkv, w_qkv_mom, w_qkv_avg)]
-    rest = (w_out, w_out_mom, w_out_avg, w_three, w_three_mom, w_three_avg, w_in, w_in_mom, w_in_avg)
+    rest = (w_out, w_out_mom, w_out_avg, w_in, w_in_mom, w_in_avg, w_three, w_three_mom, w_three_avg)
     rest += (w_one, w_one_mom, w_one_avg, w_two, w_two_mom, w_two_avg)
     given += [flat(w) for w in rest]
     given += [norm_gain, norm_gain_mom, norm_gain_avg]
-    heights = (towers * 3 * width, LANES, seconds, depth, width, units)
+    heights = (towers * 3 * width, LANES, depth, seconds, width, units)
     wides = (1, width // LANES, width // LANES, width // LANES, units // LANES, seconds // LANES)
     blocks = tuple((k + 1, size, height, wide) for k, (size, height, wide) in enumerate(zip(sizes, heights, wides)))
     *done, norm = pl.pallas_call(
@@ -1422,8 +1451,8 @@
     unturned = [
         jnp.transpose(w.reshape(towers, 3, width, LANES), (0, 2, 1, 3)) for w in done[3:6]
     ]
-    new = done[:3] + back(4, w_in) + done[21:24] + unturned + back(2, w_out) + back(5, w_one) + back(6, w_two)
-    return (loss.reshape(()), norm.reshape(()), *new, *back(3, w_three))
+    new = done[:3] + back(3, w_in) + done[21:24] + unturned + back(2, w_out) + back(5, w_one) + back(6, w_two)
+    return (loss.reshape(()), norm.reshape(()), *new, *back(4, w_three))
 
 
 def solution(mesh):

time: 176 us -> 169 us (0.960)
  Pallas kernels: 170 us -> 164 us
    pallas_call x2 -> x1, Pallas kernels: 38.1 us -> 30.3 us  [shards(): pl.pallas_call(functools.partial(backward_kernel, plane, line, slots), ou...]
where the time goes in v6:
time: 169 us
  Pallas kernels  164 us (97%)
  between operations  4.01 us (2%)
    pallas_call x1, Pallas kernels, tail(): pl.pallas_call(functools.partial(tail_kernel, plane, line, count, cuts),...  44.9 us
    pallas_call x1, Pallas kernels, shards(): pl.pallas_call(functools.partial(upper_kernel, plane, line), out_shape=[s...  32.6 us
    pallas_call x1, Pallas kernels, shards(): pl.pallas_call(functools.partial(fetch_kernel, plane, line, dims, capacit...  32 us
    pallas_call x1, Pallas kernels, shards(): pl.pallas_call(functools.partial(backward_kernel, plane, line, slots), ou...  30.3 us
    pallas_call x1, Pallas kernels, shards(): pl.pallas_call(functools.partial(update_kernel, blocks), out_shape=[shape...  14.3 us
    pallas_call x1, Pallas kernels, shards(): pl.pallas_call(functools.partial(forward_kernel, slots), grid=(towers,),...  9.72 us

profile of v6, /device:TPU:0, one launch (start us, length us, event | category | flops | bytes accessed | tf_op | source)
XLA Modules:
  0.0 168.7 jit_solution(8069343142805682229)
XLA Ops:
  0.7 0.0 copy-start.3
  0.7 0.0 copy-start.5
  0.7 0.0 copy-start.7
  0.7 32.0 %fetch.1 = (bf16[1024,128]{1,0:T(8,128)(2,1)}, s32[8,8,128]{2,1,0:T(8,128)}, s32[8,16,128]{2,1,0:T(8,128)S(1)}, bf16[4,2,4,256,128]{4,3,2,1,0:T(8,128)(2,1)}, s3...) custom-call(s32[2,32,64]{2,1,0:T(8,128)} %bitcast.101, s32[2,32,64]{2,1,0:T(8,128)} %bitcast.102, s32[2,64]{1,0:T(2,128)} %bitcast.76, ...), custom_call_target="tpu_custom_call" | custom-call | tf_op jit(solution)/shard_map/fetch/pallas_call | solution.py:1178
  32.8 0.1 slice_reduce_fusion
  32.9 0.6 fusion
  34.8 0.0 copy-start.1
  34.8 0.0 copy-start.6
  34.8 0.0 copy-start.8
  34.8 0.0 copy-start.9
  34.8 0.0 copy-done.3
  34.9 0.0 copy-done.5
  34.9 0.0 copy-done.7
  34.9 0.0 copy-done
  34.9 0.0 copy-start.2
  34.9 0.0 copy-start.4
  34.9 9.7 %attention_forward.1 = (bf16[2,16,256]{2,1,0:T(8,128)(2,1)S(1)}, bf16[2,16,512]{2,1,0:T(8,128)(2,1)S(1)}, bf16[2,512,256]{2,1,0:T(8,128)(2,1)S(1)}, bf16[2,12,51...) custom-call(s32[2,64]{1,0:T(2,128)S(1)} %bitcast.77, ...), custom_call_target="tpu_custom_call" | custom-call | tf_op jit(solution)/shard_map/attention_forward/pallas_call | solution.py:1246
  44.6 0.0 copy-done.6
  44.7 32.6 %upper.1 = (bf16[2,16,256]{2,1,0:T(8,128)(2,1)S(1)}, bf16[2,2,256,128]{3,2,1,0:T(8,128)(2,1)S(1)}, bf16[2,4,256,128]{3,2,1,0:T(8,128)(2,1)S(1)}, bf16[2,2,512,128]{3,2,1,0:T(8,128)(2,1)S(1)}, f32[1,1]{1,0:T(1,128)}) custom-call(bf16[2,16,256]{2,1,0:T(8,128)(2,1)S(1)} %get-tuple-element.128.pooled, f32[2,256,256]{2,1,0:T(8,128)S(1)} %copy-done.4, ...), custom_call_target="tpu_custom_call" | custom-call | tf_op jit(solution)/shard_map/upper/pallas_call | solution.py:1271
  77.3 30.3 %attention_backward.1 = (bf16[4,1024,128]{2,1,0:T(8,128)(2,1)S(1)}, bf16[1728,128]{1,0:T(8,128)(2,1)S(1)}, f32[8,128]{1,0:T(8,128)S(1)}) custom-call(s32[2,64]{1,0:T(2,128)S(1)} %bitcast.78, bf16[2,512,128]{2,1,0:T(8,128)(2,1)} %get-tuple-element.234.x, f32[2,128,256]{2,1,0:T(8,128)S(1)} %copy-done.3, f32[2,256]{1,0:T(2,128)S(1)} %copy-done.5, ...), custom_call_target="tpu_custom_call" | custom-call | tf_op jit(solution)/shard_map/attention_backward/pallas_call | solution.py:1322
  107.7 0.0 copy-start.10
  107.7 45.0 %conditional.3 = ((f32[4096,128]{1,0:T(8,128)}, bf16[8,960,128]{2,1,0:T(8,128)(2,1)}, f32[8,128]{1,0:T(8,128)S(1)}, f32[8,128]{1,0:T(8,128)S(1)})) conditional(s32[]{:T(128)} %bitcast.12, (s32[8,8,128]{2,1,0:T(8,128)S(1)}, s32[8,16,128]{2,1,0:T(8,128)S(1)}, bf16[4096,128]{1,0:T(8,128)(2,1)S(1)}, bf16[1728,128]{1,0:T(8,128)(2,1)S(1)}, ...), branch_computations={%region_3.0_spmd, %region_4.0_spmd} | conditional | bytes 8 | solution.py:1420
  107.7 44.9 %tail.2 = (f32[4096,128]{1,0:T(8,128)}, bf16[8,960,128]{2,1,0:T(8,128)(2,1)}, f32[8,128]{1,0:T(8,128)S(1)}, f32[8,128]{1,0:T(8,128)S(1)}) custom-call(s32[8,5,128]{2,1,0:T(8,128)S(1)} %bitcast.100, s32[8,16,128]{2,1,0:T(8,128)S(1)} %get-tuple-element.39.ids, bf16[4096,128]{1,0:T(8,128)(2,1)S(1)} %get-tuple-element.40.rows, ...), custom_call_target="tpu_custom_call" | custom-call | tf_op jit(solution)/shard_map/cond/branch_0_fun/tail/pallas_call | solution.py:1381
  152.7 14.3 %update.1 = (f32[4096,128]{1,0:T(8,128)}, f32[4096,128]{1,0:T(8,128)}, f32[4096,128]{1,0:T(8,128)}, f32[1536,128]{1,0:T(8,128)}, f32[1536,128]{1,0:T(8,128)}, /*...) custom-call(f32[8,128]{1,0:T(8,128)S(1)} %get-tuple-element.143.norm, ...), custom_call_target="tpu_custom_call" | custom-call | tf_op jit(solution)/shard_map/update/pallas_call | solution.py:1441
  (8 shorter events, 0.0 us)
Async XLA Ops:
  0.7 34.2 %copy-start.3 = (f32[2,128,256]{2,1,0:T(8,128)S(1)}, f32[2,128,256]{2,1,0:T(8,128)}, u32[]{:S(2)}) copy-start(f32[2,128,256]{2,1,0:T(8,128)} %w_in.3) | copy-start | bytes 786436
  0.7 34.2 %copy-start.5 = (f32[2,256]{1,0:T(2,128)S(1)}, f32[2,256]{1,0:T(2,128)}, u32[]{:S(2)}) copy-start(f32[2,256]{1,0:T(2,128)} %refs_21_.1) | copy-start | bytes 6148
  0.7 34.2 %copy-start.7 = (s32[64,2]{0,1:T(2,128)S(1)}, s32[64,2]{0,1:T(2,128)}, u32[]{:S(2)}) copy-start(s32[64,2]{0,1:T(2,128)} %param.36) | copy-start | bytes 1540
  32.8 2.1 %copy-start = (bf16[4,2,4,256,128]{4,3,2,1,0:T(8,128)(2,1)S(1)}, bf16[4,2,4,256,128]{4,3,2,1,0:T(8,128)(2,1)}, u32[]{:S(2)}) copy-start(bf16[4,2,4,256,128]{4,3,2,1,0:T(8,128)(2,1)} %get-tuple-element.127.w_all) | copy-start | bytes 6291460
  34.8 9.8 %copy-start.1 = (f32[2,256,512]{2,1,0:T(8,128)S(1)}, f32[2,256,512]{2,1,0:T(8,128)}, u32[]{:S(2)}) copy-start(f32[2,256,512]{2,1,0:T(8,128)} %far_two.1) | copy-start | bytes 3145732
  34.8 9.8 %copy-start.6 = (f32[4096]{0:T(1024)S(1)}, f32[4096]{0:T(1024)}, u32[]{:S(2)}) copy-start(f32[4096]{0:T(1024)} %param.39) | copy-start | bytes 49156
  34.8 9.8 %copy-start.8 = (s32[512]{0:T(512)S(1)}, s32[512]{0:T(512)}, u32[]{:S(2)}) copy-start(s32[512]{0:T(512)} %param.37) | copy-start | bytes 6148
  34.8 9.8 %copy-start.9 = (s32[64]{0:T(128)S(1)}, s32[64]{0:T(128)}, u32[]{:S(2)}) copy-start(s32[64]{0:T(128)} %positive.1) | copy-start | bytes 772
  34.9 9.8 %copy-start.2 = (f32[2,512,256]{2,1,0:T(8,128)S(1)}, f32[2,512,256]{2,1,0:T(8,128)}, u32[]{:S(2)}) copy-start(f32[2,512,256]{2,1,0:T(8,128)} %far_three.1) | copy-start | bytes 3145732
  34.9 9.8 %copy-start.4 = (f32[2,256,256]{2,1,0:T(8,128)S(1)}, f32[2,256,256]{2,1,0:T(8,128)}, u32[]{:S(2)}) copy-start(f32[2,256,256]{2,1,0:T(8,128)} %far_one.1) | copy-start | bytes 1572868
  107.7 45.0 %copy-start.10 = (f32[4096,128]{1,0:T(8,128)S(1)}, f32[4096,128]{1,0:T(8,128)}, u32[]{:S(2)}) copy-start(f32[4096,128]{1,0:T(8,128)} %refs_0_.1) | copy-start | bytes 6291460

commit v7 on v6

--- a/solution.py
+++ b/solution.py
@@ -526,22 +526,21 @@
     return out
 
 
-def forward_kernel(slots, cnt, x, w_in, gain, w_all, pooled, pm_out, normed_out, qkv, prob, a_out, pm_acc):
-    tower = pl.program_id(0)
+def forward_tower(tower, slots, cnt, x, w_in, gain, w_all, pooled, pm_out, normed_out, qkv, prob, a_out, pm_acc):
     pairs = pooled.shape[1]
     first = lax.axis_index("mp") * pairs
     parts = w_all.shape[0]
     per = LANES // slots
     groups = pairs // per
     heads = 2 * parts
-    xs = x[0]
-    hidden = nn(xs, w_in[0].astype(BF16))
+    xs = x[tower]
+    hidden = nn(xs, w_in[tower].astype(BF16))
     inverse = lax.rsqrt(jnp.mean(hidden * hidden, -1, keepdims=True) + EPS)
-    normed = (hidden * inverse * gain[pl.ds(tower, 1), :]).astype(BF16)
-    normed_out[0] = normed
+    normed = (hidden * inverse * gain[tower : tower + 1, :]).astype(BF16)
+    normed_out[tower] = normed
     for c in range(3):
         for m in range(parts):
-            qkv[0, c * parts + m] = nn(normed, w_all[m, 0, c]).astype(BF16)
+            qkv[tower, c * parts + m] = nn(normed, w_all[m, tower, c]).astype(BF16)
     lane = iota((LANES, LANES), 1)
     line = iota((LANES, LANES), 0)
     shift = slots.bit_length() - 1
@@ -557,20 +556,20 @@
         rows = pl.ds(pl.multiple_of(g * LANES, LANES), LANES)
         sums = []
         for m in range(parts):
-            query, key = qkv[0, m, rows, :], qkv[0, parts + m, rows, :]
+            query, key = qkv[tower, m, rows, :], qkv[tower, parts + m, rows, :]
             for half in range(2):
                 scores = nt(jnp.where(halves[half], query, jnp.zeros_like(query)), key) * 0.125
                 scores = jnp.where(live_r, scores, -1000000000.0)
                 expo = jnp.exp(scores - jnp.max(scores, 1, keepdims=True))
                 p = (expo * (1.0 / jnp.sum(expo, 1, keepdims=True))).astype(BF16)
-                prob[0, g, 2 * m + half] = p
+                prob[tower, g, 2 * m + half] = p
                 sums.append(jnp.sum(jnp.where(live_s, p.astype(F32), 0.0), 0, keepdims=True))
         sums = jnp.concatenate(sums, 0)
         pair_l = lax.shift_right_logical(iota((heads, LANES), 1), shift)
         stack = jnp.concatenate([jnp.where(pair_l == k, sums, 0.0) for k in range(per)], 0).astype(BF16)
-        a_out[0, g] = stack
+        a_out[tower, g] = stack
         for m in range(parts):
-            mix = nn(stack, qkv[0, 2 * parts + m, rows, :])
+            mix = nn(stack, qkv[tower, 2 * parts + m, rows, :])
             head = iota((per * heads, LANES), 1) // DH + 2 * m
             mix = jnp.where(own_head == head, mix, 0.0)
             pm_acc[g, :, m * LANES : (m + 1) * LANES] = jnp.concatenate(
@@ -580,23 +579,23 @@
 
     lax.fori_loop(0, groups, group, 0)
     pm = jnp.concatenate([pm_acc[g] for g in range(groups)], 0).astype(BF16)
-    pm_out[0] = pm
+    pm_out[tower] = pm
     every = [cnt[tower, first + k] for k in range(pairs)]
     tokens = iota((pairs, pairs * slots), 1)
     mine = lax.shift_right_logical(tokens, shift) == iota(tokens.shape, 0)
     live = mine & ((tokens & (slots - 1)) < chain(iota(tokens.shape, 0), every))
     high, low = split(nn(live.astype(BF16), xs))
-    w = w_in[0].astype(BF16)
+    w = w_in[tower].astype(BF16)
     total = nn(high, w) + nn(low, w)
     sides = []
     for j in range(2):
         side = total[:, j * LANES : (j + 1) * LANES]
         for m in range(parts):
-            side = side + nn(pm[:, m * LANES : (m + 1) * LANES], w_all[m, 0, 3, j * LANES : (j + 1) * LANES, :])
+            side = side + nn(pm[:, m * LANES : (m + 1) * LANES], w_all[m, tower, 3, j * LANES : (j + 1) * LANES, :])
         sides.append(side)
     total = jnp.concatenate(sides, 1)
     count = chain(iota(total.shape, 0), every).astype(F32)
-    pooled[0] = (total / count).astype(BF16)
+    pooled[tower] = (total / count).astype(BF16)
 
 
 def put(target, size, first, value):
@@ -704,130 +703,6 @@
     demb[...] = nt(dhidden, w).astype(BF16)
 
 
-def backward_kernel(
-    plane,
-    line,
-    slots,
-    cnt,
-    x,
-    w_in,
-    gain,
-    w_all,
-    normed,
-    qkv,
-    prob,
-    a_in,
-    pm,
-    dpooled,
-    d_three,
-    d_one,
-    d_two,
-    out,
-    summed,
-    gain_sum,
-    d_qkv,
-    d_out,
-    d_in,
-    d_gain,
-    dqkv,
-    near_split,
-    near_whole,
-    half,
-    got,
-    got_late,
-    gains,
-    far_out,
-    far_in,
-    near_out,
-    near_in,
-    sum_out,
-    sum_in,
-    gain_out,
-    gain_in,
-):
-    me, part = enter(plane, line)
-    chips = plane // 2
-    core = lax.rem(me, 2)
-    chip = me // 2
-    sibling = me + 1 - 2 * core
-    towers, tokens = x.shape[:2]
-    late, early = (d_in,), (d_three, d_one, d_two)
-    nears = [send(grad.at[:, 1 - core], near_whole[1 + j], near_out.at[j], near_in.at[j], (sibling, part)) for j, grad in enumerate(early)]
-    copies = []
-
-    def tower(t):
-        demb = out.at[part, t * tokens : (t + 1) * tokens]
-        backward_tower(
-            t, slots, cnt, x, w_in, gain, w_all, normed, qkv, prob, a_in, pm, dpooled, demb, d_in, d_gain, d_qkv, d_out, dqkv
-        )
-        for k in range(1, line):
-            peer = lax.rem(part + k, line)
-            copies.append(send(demb, demb, far_out.at[t, k], far_in.at[t, k], (me, peer)))
-
-    def whole(c, at, grad, near):
-        rows = grad.shape[2]
-        half[c, at : at + rows, :] = (grad[c, core].astype(F32) + near[c].astype(F32)).astype(BF16)
-        return at + rows
-
-    def exchange(begin, end, target, sems):
-        sums = []
-        for k in range(1, chips):
-            to = lax.rem(chip + k, chips)
-            source = half.at[to, begin:end]
-            sums.append(send(source, target.at[k - 1], sum_out.at[sems, k], sum_in.at[sems, k], (2 * to + core, part)))
-        return sums
-
-    def collect(begin, end, target, sums):
-        for copy in sums:
-            copy.wait()
-        total = half[chip, begin:end, :].astype(F32)
-        for k in range(chips - 1):
-            total = total + target[k].astype(F32)
-        summed[begin:end, :] = total.astype(BF16)
-
-    first = line * (d_qkv.shape[3] + d_out.shape[3]) + d_in.shape[2]
-    d_gain[...] = jnp.zeros_like(d_gain)
-    tower(0)
-    for copy in nears:
-        copy.wait()
-    for c in range(chips):
-        at = first
-        for j, grad in enumerate(early):
-            at = whole(c, at, grad, near_whole[1 + j])
-    last = at
-    sums = exchange(first, last, got, 0)
-    for t in range(1, towers):
-        tower(t)
-    nears = []
-    for j, grad in enumerate((d_qkv, d_out)):
-        nears.append(send(grad.at[:, :, 1 - core], near_split[j], near_out.at[3 + j], near_in.at[3 + j], (sibling, part)))
-    nears.append(send(d_in.at[:, 1 - core], near_whole[0], near_out.at[5], near_in.at[5], (sibling, part)))
-    for k in range(1, plane):
-        peer = lax.rem(me + k, plane)
-        copies.append(send(d_gain, gains.at[me], gain_out.at[k], gain_in.at[k], (peer, part)))
-    gains[me] = d_gain[...]
-    for copy in nears:
-        copy.wait()
-    for c in range(chips):
-        at = 0
-        for grad, near in zip((d_qkv, d_out), near_split):
-            rows = grad.shape[3]
-            for m in range(line):
-                total = grad[m, c, core].astype(F32) + near[m, c].astype(F32)
-                half[c, at : at + rows, :] = total.astype(BF16)
-                at += rows
-        whole(c, at, d_in, near_whole[0])
-    late_sums = exchange(0, first, got_late, 1)
-    collect(first, last, got, sums)
-    collect(0, first, got_late, late_sums)
-    for copy in copies:
-        copy.wait()
-    total = gains[0]
-    for d in range(1, plane):
-        total = total + gains[d]
-    gain_sum[...] = total
-
-
 def gelu_parts(v):
     c = 0.7978845608028654
     inner = jnp.tanh(c * (v + 0.044715 * (v * v * v)))
@@ -836,13 +711,12 @@
     return value, slope
 
 
-def upper_kernel(
+def upper_layers(
+    me,
+    part,
     plane,
     line,
     pooled,
-    far_one,
-    far_two,
-    far_three,
     log_prior,
     item_qid,
     lists,
@@ -867,18 +741,11 @@
     w_one,
     w_two,
     w_three,
-    load_sems,
+    loads,
     second_mine,
     dpool_mine,
     prior_col,
 ):
-    loads = [
-        pltpu.make_async_copy(source, target, load_sems.at[j])
-        for j, (source, target) in enumerate(((far_one, w_one), (far_two, w_two), (far_three, w_three)))
-    ]
-    for copy in loads:
-        copy.start()
-    me, part = enter(plane, line)
     towers, own, width = pooled.shape
     per = lists.shape[1] - 8
     rows = own * line
@@ -998,7 +865,7 @@
     for t in range(towers):
         grad = tn(act_two[t], dthirds[t]).astype(BF16)
         for j in range(width // LANES):
-            d_three[t, j] = grad[:, j * LANES : (j + 1) * LANES]
+            put(d_three, d_three.shape[2], (t * (width // LANES) + j) * grad.shape[0], grad[:, j * LANES : (j + 1) * LANES])
     for copy in spread:
         copy.wait()
     dfirsts = []
@@ -1018,8 +885,10 @@
         dsecond = dsec_all[t].reshape(rows, -1)
         for grads, grad in ((d_two, tn(act_one[t], dsecond)), (d_one, tn(pools[t], dfirsts[t]))):
             grad = grad.astype(BF16)
-            for j in range(grad.shape[1] // LANES):
-                grads[t, j] = grad[:, j * LANES : (j + 1) * LANES]
+            wide = grad.shape[1] // LANES
+            for j in range(wide):
+                begin = (t * wide + j) * grad.shape[0]
+                put(grads, grads.shape[2], begin, grad[:, j * LANES : (j + 1) * LANES])
     for copy in back:
         copy.wait()
     for t in range(towers):
@@ -1027,6 +896,176 @@
         for peer in peers:
             total = total + dpool_got[t, peer].astype(F32)
         dpooled[t] = total.astype(BF16)
+
+
+def towers_kernel(
+    plane,
+    line,
+    slots,
+    cnt,
+    x,
+    w_in,
+    gain,
+    w_all,
+    far_one,
+    far_two,
+    far_three,
+    log_prior,
+    item_qid,
+    lists,
+    positive,
+    out,
+    summed,
+    gain_sum,
+    loss,
+    pooled,
+    pm,
+    normed,
+    qkv,
+    prob,
+    a_in,
+    pm_acc,
+    upper_scratch,
+    w_one,
+    w_two,
+    w_three,
+    load_sems,
+    dpooled,
+    d_three,
+    d_one,
+    d_two,
+    d_qkv,
+    d_out,
+    d_in,
+    d_gain,
+    dqkv,
+    near_split,
+    near_whole,
+    half,
+    got,
+    got_late,
+    gains,
+    far_out,
+    far_in,
+    near_out,
+    near_in,
+    sum_out,
+    sum_in,
+    gain_out,
+    gain_in,
+):
+    loads = [
+        pltpu.make_async_copy(source, target, load_sems.at[j])
+        for j, (source, target) in enumerate(((far_one, w_one), (far_two, w_two), (far_three, w_three)))
+    ]
+    for copy in loads:
+        copy.start()
+    me, part = announce(plane, line)
+    for t in range(x.shape[0]):
+        forward_tower(t, slots, cnt, x, w_in, gain, w_all, pooled, pm, normed, qkv, prob, a_in, pm_acc)
+    await_others(plane, line)
+    upper_layers(
+        me,
+        part,
+        plane,
+        line,
+        pooled,
+        log_prior,
+        item_qid,
+        lists,
+        positive,
+        dpooled,
+        d_one,
+        d_two,
+        d_three,
+        loss,
+        *upper_scratch[:-3],
+        w_one,
+        w_two,
+        w_three,
+        loads,
+        *upper_scratch[-3:],
+    )
+    chips = plane // 2
+    core = lax.rem(me, 2)
+    chip = me // 2
+    sibling = me + 1 - 2 * core
+    towers, tokens = x.shape[:2]
+    late, early = (d_in,), (d_three, d_one, d_two)
+    nears = [send(grad.at[:, 1 - core], near_whole[1 + j], near_out.at[j], near_in.at[j], (sibling, part)) for j, grad in enumerate(early)]
+    copies = []
+
+    def tower(t):
+        demb = out.at[part, t * tokens : (t + 1) * tokens]
+        backward_tower(
+            t, slots, cnt, x, w_in, gain, w_all, normed, qkv, prob, a_in, pm, dpooled, demb, d_in, d_gain, d_qkv, d_out, dqkv
+        )
+        for k in range(1, line):
+            peer = lax.rem(part + k, line)
+            copies.append(send(demb, demb, far_out.at[t, k], far_in.at[t, k], (me, peer)))
+
+    def whole(c, at, grad, near):
+        rows = grad.shape[2]
+        half[c, at : at + rows, :] = (grad[c, core].astype(F32) + near[c].astype(F32)).astype(BF16)
+        return at + rows
+
+    def exchange(begin, end, target, sems):
+        sums = []
+        for k in range(1, chips):
+            to = lax.rem(chip + k, chips)
+            source = half.at[to, begin:end]
+            sums.append(send(source, target.at[k - 1], sum_out.at[sems, k], sum_in.at[sems, k], (2 * to + core, part)))
+        return sums
+
+    def collect(begin, end, target, sums):
+        for copy in sums:
+            copy.wait()
+        total = half[chip, begin:end, :].astype(F32)
+        for k in range(chips - 1):
+            total = total + target[k].astype(F32)
+        summed[begin:end, :] = total.astype(BF16)
+
+    first = line * (d_qkv.shape[3] + d_out.shape[3]) + d_in.shape[2]
+    d_gain[...] = jnp.zeros_like(d_gain)
+    tower(0)
+    for copy in nears:
+        copy.wait()
+    for c in range(chips):
+        at = first
+        for j, grad in enumerate(early):
+            at = whole(c, at, grad, near_whole[1 + j])
+    last = at
+    sums = exchange(first, last, got, 0)
+    for t in range(1, towers):
+        tower(t)
+    nears = []
+    for j, grad in enumerate((d_qkv, d_out)):
+        nears.append(send(grad.at[:, :, 1 - core], near_split[j], near_out.at[3 + j], near_in.at[3 + j], (sibling, part)))
+    nears.append(send(d_in.at[:, 1 - core], near_whole[0], near_out.at[5], near_in.at[5], (sibling, part)))
+    for k in range(1, plane):
+        peer = lax.rem(me + k, plane)
+        copies.append(send(d_gain, gains.at[me], gain_out.at[k], gain_in.at[k], (peer, part)))
+    gains[me] = d_gain[...]
+    for copy in nears:
+        copy.wait()
+    for c in range(chips):
+        at = 0
+        for grad, near in zip((d_qkv, d_out), near_split):
+            rows = grad.shape[3]
+            for m in range(line):
+                total = grad[m, c, core].astype(F32) + near[m, c].astype(F32)
+                half[c, at : at + rows, :] = total.astype(BF16)
+                at += rows
+        whole(c, at, d_in, near_whole[0])
+    late_sums = exchange(0, first, got_late, 1)
+    collect(first, last, got, sums)
+    collect(0, first, got_late, late_sums)
+    for copy in copies:
+        copy.wait()
+    total = gains[0]
+    for d in range(1, plane):
+        total = total + gains[d]
+    gain_sum[...] = total
 
 
 def update(weight, grad, moment, average, factor, rate):
@@ -1241,97 +1280,58 @@
     heads = 2 * line
     groups = tokens // LANES
     per_group = LANES // slots
-    lead = lambda *dims: pl.BlockSpec((1,) + dims, lambda t: (t,) + (0,) * len(dims))
-    all_spec = pl.BlockSpec((line, 1, 4, width, LANES), lambda t: (0, t, 0, 0, 0))
-    pooled, pm, normed, qkv, prob, spread = pl.pallas_call(
-        functools.partial(forward_kernel, slots),
-        grid=(towers,),
+    totals = (towers * 3 * width, towers * width, towers * depth * width // LANES)
+    totals += tuple(towers * size // LANES for size in (seconds * width, width * units, units * seconds))
+    sizes = [total // plane for total in totals]
+    held = lambda size: pltpu.VMEM((plane // 2, 2, size, LANES), BF16)
+    share = line * (sizes[0] + sizes[1]) + sum(sizes[2:])
+    early = sum(sizes[3:])
+    every, summed, gain_sum, loss = pl.pallas_call(
+        functools.partial(towers_kernel, plane, line, slots),
         out_shape=[
-            shape((towers, own, width), BF16),
-            shape((towers, own, line * LANES), BF16),
-            shape((towers, tokens, width), BF16),
-            shape((towers, 3 * line, tokens, LANES), BF16),
-            shape((towers, groups, heads, LANES, LANES), BF16),
-            shape((towers, groups, per_group * heads, LANES), BF16),
-        ],
-        in_specs=[SMEM, lead(tokens, depth), lead(depth, width), VMEM, all_spec],
-        out_specs=[
-            lead(own, width),
-            lead(own, line * LANES),
-            lead(tokens, width),
-            lead(3 * line, tokens, LANES),
-            lead(groups, heads, LANES, LANES),
-            lead(groups, per_group * heads, LANES),
-        ],
-        scratch_shapes=[pltpu.VMEM((groups, per_group, line * LANES), F32)],
-        compiler_params=params(20),
-        name="attention_forward",
-    )(counts, embedded, w_in, norm_gain, weights)
-
-    dpooled, d_one, d_two, d_three, loss = pl.pallas_call(
-        functools.partial(upper_kernel, plane, line),
-        out_shape=[
-            shape((towers, own, width), BF16),
-            shape((towers, units // LANES, width, LANES), BF16),
-            shape((towers, seconds // LANES, units, LANES), BF16),
-            shape((towers, width // LANES, seconds, LANES), BF16),
+            shape((line, own_requests, depth), BF16),
+            shape((share, LANES), BF16),
+            shape((8, LANES), F32),
             shape((1, 1), F32),
         ],
-        in_specs=[VMEM] + [HBM] * 3 + [VMEM] * 3 + [SMEM],
-        out_specs=[VMEM] * 4 + [SMEM],
+        in_specs=[SMEM] + [VMEM] * 4 + [HBM] * 3 + [VMEM] * 3 + [SMEM],
+        out_specs=[VMEM] * 3 + [SMEM],
         scratch_shapes=[
-            pltpu.VMEM((towers, line, own, width), BF16),
-            pltpu.VMEM((towers, line, own, seconds), BF16),
-            pltpu.VMEM((towers, line, own, seconds), BF16),
-            pltpu.VMEM((towers, plane, line, own, width), BF16),
-            pltpu.VMEM((towers, line, own, seconds), BF16),
-            pltpu.VMEM((towers, line, own, seconds), BF16),
-            pltpu.VMEM((towers, line, own, width), BF16),
-            pltpu.VMEM((towers, line, own, width), BF16),
-            DMA((5, line)),
-            DMA((5, line)),
-            DMA((plane,)),
-            DMA((plane,)),
+            pltpu.VMEM((towers, own, width), BF16),
+            pltpu.VMEM((towers, own, line * LANES), BF16),
+            pltpu.VMEM((towers, tokens, width), BF16),
+            pltpu.VMEM((towers, 3 * line, tokens, LANES), BF16),
+            pltpu.VMEM((towers, groups, heads, LANES, LANES), BF16),
+            pltpu.VMEM((towers, groups, per_group * heads, LANES), BF16),
+            pltpu.VMEM((groups, per_group, line * LANES), F32),
+            [
+                pltpu.VMEM((towers, line, own, width), BF16),
+                pltpu.VMEM((towers, line, own, seconds), BF16),
+                pltpu.VMEM((towers, line, own, seconds), BF16),
+                pltpu.VMEM((towers, plane, line, own, width), BF16),
+                pltpu.VMEM((towers, line, own, seconds), BF16),
+                pltpu.VMEM((towers, line, own, seconds), BF16),
+                pltpu.VMEM((towers, line, own, width), BF16),
+                pltpu.VMEM((towers, line, own, width), BF16),
+                DMA((5, line)),
+                DMA((5, line)),
+                DMA((plane,)),
+                DMA((plane,)),
+                pltpu.VMEM((towers, line, own, seconds), F32),
+                pltpu.VMEM((towers, line, own, width), F32),
+                pltpu.VMEM((pairs, 8), F32),
+            ],
             pltpu.VMEM(w_one.shape, F32),
             pltpu.VMEM(w_two.shape, F32),
             pltpu.VMEM(w_three.shape, F32),
             DMA((3,)),
-            pltpu.VMEM((towers, line, own, seconds), F32),
-            pltpu.VMEM((towers, line, own, width), F32),
-            pltpu.VMEM((pairs, 8), F32),
-        ],
-        compiler_params=params(22 + 2 * (pairs * pairs >> 18), collective_id=3, has_side_effects=True),
-        name="upper",
-    )(
-        pooled,
-        w_one,
-        w_two,
-        w_three,
-        log_prior.reshape(-1, LANES),
-        item_qid.reshape(1, pairs),
-        got_lists,
-        positive,
-    )
-
-    totals = (towers * 3 * width, towers * width, towers * depth * width // LANES)
-    totals += tuple(grad.size // LANES for grad in (d_three, d_one, d_two))
-    sizes = [total // plane for total in totals]
-    shares = lambda grad: grad.reshape(plane // 2, 2, -1, LANES)
-    share = line * (sizes[0] + sizes[1]) + sum(sizes[2:])
-    early = sum(sizes[3:])
-    every, summed, gain_sum = pl.pallas_call(
-        functools.partial(backward_kernel, plane, line, slots),
-        out_shape=[
-            shape((line, own_requests, depth), BF16),
-            shape((share, LANES), BF16),
-            shape((8, LANES), F32),
-        ],
-        in_specs=[SMEM] + [VMEM] * 13,
-        out_specs=[VMEM] * 3,
-        scratch_shapes=[
+            pltpu.VMEM((towers, own, width), BF16),
+            held(sizes[3]),
+            held(sizes[4]),
+            held(sizes[5]),
             pltpu.VMEM((line, plane // 2, 2, sizes[0], LANES), BF16),
             pltpu.VMEM((line, plane // 2, 2, sizes[1], LANES), BF16),
-            pltpu.VMEM((plane // 2, 2, sizes[2], LANES), BF16),
+            held(sizes[2]),
             pltpu.VMEM((8, LANES), F32),
             pltpu.VMEM((3 * line, tokens, LANES), BF16),
             [pltpu.VMEM((line, plane // 2, size, LANES), BF16) for size in sizes[:2]],
@@ -1349,23 +1349,21 @@
             DMA((plane,)),
             DMA((plane,)),
         ],
-        compiler_params=params(40, collective_id=4, has_side_effects=True),
-        name="attention_backward",
+        compiler_params=params(60, collective_id=4, has_side_effects=True),
+        name="towers",
     )(
         counts,
         embedded,
         w_in,
         norm_gain,
         weights,
-        normed,
-        qkv,
-        prob,
-        spread,
-        pm,
-        dpooled,
-        shares(d_three),
-        shares(d_one),
-        shares(d_two),
+        w_one,
+        w_two,
+        w_three,
+        log_prior.reshape(-1, LANES),
+        item_qid.reshape(1, pairs),
+        got_lists,
+        positive,
     )
     whole_at = line * (sizes[0] + sizes[1])
     whole_rows = sizes[2] + sizes[3]

time: 169 us -> 163 us (0.964)
  Pallas kernels: 164 us -> 158 us
    pallas_call x3 -> x1, Pallas kernels: 72.7 us -> 68.3 us  [shards(): pl.pallas_call(functools.partial(towers_kernel, plane, line, slots), out_...]
where the time goes in v7:
time: 163 us
  Pallas kernels  158 us (97%)
  between operations  3.76 us (2%)
    pallas_call x1, Pallas kernels, shards(): pl.pallas_call(functools.partial(towers_kernel, plane, line, slots), out_...  68.3 us
    pallas_call x1, Pallas kernels, tail(): pl.pallas_call(functools.partial(tail_kernel, plane, line, count, cuts),...  43.7 us
    pallas_call x1, Pallas kernels, shards(): pl.pallas_call(functools.partial(fetch_kernel, plane, line, dims, capacit...  32.1 us
    pallas_call x1, Pallas kernels, shards(): pl.pallas_call(functools.partial(update_kernel, blocks), out_shape=[shape...  14.3 us

profile of v7, /device:TPU:0, one launch (start us, length us, event | category | flops | bytes accessed | tf_op | source)
XLA Modules:
  0.0 162.8 jit_solution(7988891638182185894)
XLA Ops:
  0.7 0.0 copy-start
  0.7 32.1 %fetch.1 = (bf16[1024,128]{1,0:T(8,128)(2,1)S(1)}, s32[8,8,128]{2,1,0:T(8,128)S(1)}, s32[8,16,128]{2,1,0:T(8,128)S(1)}, bf16[4,2,4,256,128]{4,3,2,1,0:T(8,128)(2...) custom-call(s32[2,32,64]{2,1,0:T(8,128)} %bitcast.91, s32[2,32,64]{2,1,0:T(8,128)} %bitcast.92, s32[2,64]{1,0:T(2,128)} %bitcast.94, ...), custom_call_target="tpu_custom_call" | custom-call | tf_op jit(solution)/shard_map/fetch/pallas_call | solution.py:1217
  32.7 0.1 slice_reduce_fusion
  32.9 0.6 fusion
  34.8 0.0 copy-done
  34.8 68.3 %towers.1 = (bf16[4,1024,128]{2,1,0:T(8,128)(2,1)S(1)}, bf16[1728,128]{1,0:T(8,128)(2,1)S(1)}, f32[8,128]{1,0:T(8,128)S(1)}, f32[1,1]{1,0:T(1,128)}) custom-call(s32[2,64]{1,0:T(2,128)} %bitcast.95, bf16[2,512,128]{2,1,0:T(8,128)(2,1)S(1)} %get-tuple-element.211.x, f32[2,128,256]{2,1,0:T(8,128)} %w_in.1, f32[2,256]{1,0:T(2,128)} %refs_21_.1, ...), custom_call_target="tpu_custom_call" | custom-call | tf_op jit(solution)/shard_map/towers/pallas_call | solution.py:1289
  103.1 43.7 %conditional.3 = ((f32[4096,128]{1,0:T(8,128)}, bf16[8,960,128]{2,1,0:T(8,128)(2,1)}, f32[8,128]{1,0:T(8,128)S(1)}, f32[8,128]{1,0:T(8,128)S(1)})) conditional(s32[]{:T(128)} %bitcast.12, (s32[8,8,128]{2,1,0:T(8,128)S(1)}, s32[8,16,128]{2,1,0:T(8,128)S(1)}, bf16[4096,128]{1,0:T(8,128)(2,1)S(1)}, bf16[1728,128]{1,0:T(8,128)(2,1)S(1)}, ...), branch_computations={%region_3.0_spmd, %region_4.0_spmd} | conditional | bytes 8 | solution.py:1418
  103.1 43.7 %tail.2 = (f32[4096,128]{1,0:T(8,128)}, bf16[8,960,128]{2,1,0:T(8,128)(2,1)}, f32[8,128]{1,0:T(8,128)S(1)}, f32[8,128]{1,0:T(8,128)S(1)}) custom-call(s32[8,5,128]{2,1,0:T(8,128)S(1)} %bitcast.90, s32[8,16,128]{2,1,0:T(8,128)S(1)} %get-tuple-element.36.ids, bf16[4096,128]{1,0:T(8,128)(2,1)S(1)} %get-tuple-element.37.rows, ...), custom_call_target="tpu_custom_call" | custom-call | tf_op jit(solution)/shard_map/cond/branch_0_fun/tail/pallas_call | solution.py:1379
  146.8 14.3 %update.1 = (f32[4096,128]{1,0:T(8,128)}, f32[4096,128]{1,0:T(8,128)}, f32[4096,128]{1,0:T(8,128)}, f32[1536,128]{1,0:T(8,128)}, f32[1536,128]{1,0:T(8,128)}, /*...) custom-call(f32[8,128]{1,0:T(8,128)S(1)} %get-tuple-element.120.norm, ...), custom_call_target="tpu_custom_call" | custom-call | tf_op jit(solution)/shard_map/update/pallas_call | solution.py:1439
  (1 shorter events, 0.0 us)
Async XLA Ops:
  0.7 34.1 %copy-start = (f32[4096,128]{1,0:T(8,128)S(1)}, f32[4096,128]{1,0:T(8,128)}, u32[]{:S(2)}) copy-start(f32[4096,128]{1,0:T(8,128)} %refs_0_.1) | copy-start | bytes 6291460

commit v8 on v7

--- a/solution.py
+++ b/solution.py
@@ -1,4 +1,5 @@
 import functools
+import math
 
 import jax
 import jax.numpy as jnp
@@ -185,7 +186,7 @@
         target[pl.ds(pl.multiple_of(i * 16, 16), 16), :] = jnp.concatenate(rows, 0).astype(BF16)
         return carry
 
-    lax.fori_loop(0, target.shape[0] // 16, body, 0)
+    lax.fori_loop(0, target.shape[0] // 16, body, 0, unroll=2)
 
 
 def listed(ids, first):
@@ -433,6 +434,26 @@
         far.append(send(source, target, far_out.at[2, k], far_in.at[2, k], (me, peer)))
         far.append(send(gain, gains.at[part], gain_out.at[k], gain_in.at[k], (me, peer)))
     gains[part] = gain[...]
+    split_rows = sum(count for _, count in split_cuts)
+    done = split_rows + whole_rows
+    dense_all[me, done:, :] = summed[last_at : last_at + last_rows, :]
+    spread, near = [], []
+
+    def gather_shares(stage, begin, end):
+        block = dense_all.at[me, begin:end]
+        for k in range(1, chips):
+            to = 2 * lax.rem(chip + k, chips) + core
+            spread.append(send(block, block, chip_out.at[stage, k], chip_in.at[stage, k], (to, part)))
+        near.append(send(block, block, near_out.at[stage, 0], near_in.at[stage, 0], (sibling, part)))
+
+    def pass_shares(stage, begin, end):
+        for k in range(1, chips):
+            peer = 2 * lax.rem(chip - k + chips, chips) + core
+            spread[stage * (chips - 1) + k - 1].wait_recv()
+            block = dense_all.at[peer, begin:end]
+            near.append(send(block, block, near_out.at[stage, k], near_in.at[stage, k], (sibling, part)))
+
+    gather_shares(0, done, done + last_rows)
     wide[...] = rows[...].astype(F32)
     copies = []
     others = partners(me, plane)
@@ -451,9 +472,6 @@
     for m in range(1, line):
         share = share + got[m].astype(F32)
     dense_all[me, 0 : to + whole_rows, :] = share.astype(BF16)
-    dense_all[me, to + whole_rows :, :] = summed[last_at : last_at + last_rows, :]
-    dense = dense_all.at[me]
-    spread, near = [], []
     group = max(1, 1280 // capacity)
     order = [me] + others
     for first in range(0, plane, group):
@@ -462,10 +480,8 @@
         for k in range(max(first, 1), min(first + group, plane)):
             copies[k - 1].wait_recv()
         if first + group >= plane:
-            for k in range(1, chips):
-                other = lax.rem(chip + k, chips)
-                spread.append(send(dense, dense, chip_out.at[k], chip_in.at[k], (2 * other + core, part)))
-            near.append(send(dense, dense, near_out.at[0], near_in.at[0], (sibling, part)))
+            gather_shares(1, 0, done)
+            pass_shares(0, done, done + last_rows)
         add_rows(ids, capacity, blocks, grads, total, first == 0)
     square = jnp.zeros((8, LANES), F32)
     for begin, count, weight in ((0, to, 1.0), (to, whole_rows, 1.0 / line), (to + whole_rows, last_rows, 1.0)):
@@ -499,10 +515,7 @@
     tiny = [
         send(along.at[part], along.at[part], along_out.at[k], along_in.at[k], (me, peer)) for k, peer in enumerate(peers)
     ]
-    for k in range(1, chips):
-        peer = 2 * lax.rem(chip - k + chips, chips) + core
-        spread[k - 1].wait_recv()
-        near.append(send(dense_all.at[peer], dense_all.at[peer], near_out.at[k], near_in.at[k], (sibling, part)))
+    pass_shares(1, 0, done)
     gain_sum = gains[0]
     for m in range(1, line):
         gain_sum = gain_sum + gains[m]
@@ -524,6 +537,11 @@
     for k in range(1, len(values)):
         out = jnp.where(index >= k, values[k], out)
     return out
+
+
+def two_by_two(parts):
+    blocks = [(c, m) for m in range(parts) for c in range(2)] + [(2, m) for m in range(parts)]
+    return list(zip(blocks[::2], blocks[1::2]))
 
 
 def forward_tower(tower, slots, cnt, x, w_in, gain, w_all, pooled, pm_out, normed_out, qkv, prob, a_out, pm_acc):
@@ -538,9 +556,11 @@
     inverse = lax.rsqrt(jnp.mean(hidden * hidden, -1, keepdims=True) + EPS)
     normed = (hidden * inverse * gain[tower : tower + 1, :]).astype(BF16)
     normed_out[tower] = normed
-    for c in range(3):
-        for m in range(parts):
-            qkv[tower, c * parts + m] = nn(normed, w_all[m, tower, c]).astype(BF16)
+    for (c, m), (d, n) in two_by_two(parts):
+        both = jnp.concatenate([w_all[m, tower, c], w_all[n, tower, d]], 1)
+        both = nn(normed, both).astype(BF16)
+        qkv[tower, c * parts + m] = both[:, :LANES]
+        qkv[tower, d * parts + n] = both[:, LANES:]
     lane = iota((LANES, LANES), 1)
     line = iota((LANES, LANES), 0)
     shift = slots.bit_length() - 1
@@ -674,11 +694,12 @@
             dqkv[2 * parts + m, rows, :] = tn(a_in[tower, g], stacks[m]).astype(BF16)
     normed = normed_in[tower]
     dnormed = jnp.zeros((tokens, width), F32)
-    for m in range(parts):
-        for c in range(3):
-            grad = dqkv[c * parts + m]
-            dnormed = dnormed + nt(grad, w_all[m, tower, c])
-            put(d_qkv.at[m], d_qkv.shape[3], (tower * 3 + c) * width, tn(normed, grad).astype(BF16))
+    for (c, m), (d, n) in two_by_two(parts):
+        both = jnp.concatenate([dqkv[c * parts + m], dqkv[d * parts + n]], 1)
+        dnormed = dnormed + nt(both, jnp.concatenate([w_all[m, tower, c], w_all[n, tower, d]], 1))
+        both = tn(normed, both).astype(BF16)
+        put(d_qkv.at[m], d_qkv.shape[3], (tower * 3 + c) * width, both[:, :LANES])
+        put(d_qkv.at[n], d_qkv.shape[3], (tower * 3 + d) * width, both[:, LANES:])
     dnormed = dnormed.astype(BF16).astype(F32)
     xs = x[tower]
     w = w_in[tower].astype(BF16)
@@ -1081,15 +1102,13 @@
     sources, targets, norm = refs[:arrays], refs[arrays : 2 * arrays], refs[2 * arrays]
     held, in_sems, out_sems = refs[2 * arrays + 1 : 3 * arrays + 1], refs[-2], refs[-1]
     loads = [pltpu.make_async_copy(sources[k], held[k], in_sems.at[k]) for k in range(arrays)]
-    ahead = 8
-
-    def load(k):
-        if k < arrays // 3:
-            for copy in loads[3 * k : 3 * k + 3]:
-                copy.start()
-
-    for k in range(ahead):
-        load(k)
+    starts = {}
+    for k, size, _, _ in blocks:
+        starts[k] = sum(other[1] for other in blocks[: k - 1])
+    order = sorted(blocks, key=lambda block: -block[1])
+    for k in [0] + [block[0] for block in order] + [arrays // 3 - 1]:
+        for copy in loads[3 * k : 3 * k + 3]:
+            copy.start()
     root = jnp.sqrt(norm_sq[...])
     norm[0, 0] = jnp.max(root)
     factor = jnp.minimum(1.0, CLIP_NORM / root[0:1, :])
@@ -1110,22 +1129,20 @@
     def wait(k):
         for copy in loads[3 * k : 3 * k + 3]:
             copy.wait()
-        load(k + ahead)
-
-    wait(0)
 
     def rows(i, carry):
-        at = pl.ds(pl.multiple_of(i * 32, 32), 32)
+        at = pl.ds(pl.multiple_of(i * 64, 64), 64)
         apply(0, at, slice(0, LANES), table_grad[at, :], ROW_RATE)
         return carry
 
-    lax.fori_loop(0, table_grad.shape[0] // 32, rows, 0, unroll=2)
+    wait(0)
+    lax.fori_loop(0, table_grad.shape[0] // 64, rows, 0, unroll=2)
     finish(0)
-    at = 0
-    for k, size, height, wide in blocks:
+    for k, size, height, wide in order:
         wait(k)
+        at = starts[k]
         total = dense.shape[0] * size
-        step = 32 if size % 32 == 0 else 16
+        step = math.gcd(size, 64)
         for first in range(0, total, min(size, height)):
             count = min(size, height)
             share, inside = first // size, first % size
@@ -1141,7 +1158,6 @@
                 return carry
 
             lax.fori_loop(0, count // step, piece, 0, unroll=2)
-        at += size
         finish(k)
     last = 7
     wait(last)
@@ -1405,10 +1421,10 @@
                 DMA((line,)),
                 DMA((plane,)),
                 DMA((plane,)),
-                DMA((plane // 2,)),
-                DMA((plane // 2,)),
-                DMA((plane // 2,)),
-                DMA((plane // 2,)),
+                DMA((2, plane // 2)),
+                DMA((2, plane // 2)),
+                DMA((2, plane // 2)),
+                DMA((2, plane // 2)),
             ],
             compiler_params=params(36, collective_id=number, has_side_effects=True),
             name="tail",

time: 163 us -> 160 us (0.982)
  Pallas kernels: 158 us -> 155 us
    pallas_call x1, Pallas kernels: 68.3 us -> 66.2 us  [shards(): pl.pallas_call(functools.partial(towers_kernel, plane, line, slots), out_...]
where the time goes in v8:
time: 160 us; the launch traced here: 159 us
  Pallas kernels  155 us (97%)
  between operations  3.76 us (2%)
    pallas_call x1, Pallas kernels, shards(): pl.pallas_call(functools.partial(towers_kernel, plane, line, slots), out_...  66.2 us
    pallas_call x1, Pallas kernels, tail(): pl.pallas_call(functools.partial(tail_kernel, plane, line, count, cuts),...  42.5 us
    pallas_call x1, Pallas kernels, shards(): pl.pallas_call(functools.partial(fetch_kernel, plane, line, dims, capacit...  32 us
    pallas_call x1, Pallas kernels, shards(): pl.pallas_call(functools.partial(update_kernel, blocks), out_shape=[shape...  13.9 us

profile of v8, /device:TPU:0, one launch (start us, length us, event | category | flops | bytes accessed | tf_op | source)
XLA Modules:
  0.0 159.3 jit_solution(12735957059293642205)
XLA Ops:
  0.7 0.0 copy-start
  0.7 32.0 %fetch.1 = (bf16[1024,128]{1,0:T(8,128)(2,1)S(1)}, s32[8,8,128]{2,1,0:T(8,128)S(1)}, s32[8,16,128]{2,1,0:T(8,128)S(1)}, bf16[4,2,4,256,128]{4,3,2,1,0:T(8,128)(2...) custom-call(s32[2,32,64]{2,1,0:T(8,128)} %bitcast.91, s32[2,32,64]{2,1,0:T(8,128)} %bitcast.92, s32[2,64]{1,0:T(2,128)} %bitcast.94, ...), custom_call_target="tpu_custom_call" | custom-call | tf_op jit(solution)/shard_map/fetch/pallas_call | solution.py:1233
  32.7 0.1 slice_reduce_fusion
  32.8 0.6 fusion
  34.7 0.0 copy-done
  34.7 66.2 %towers.1 = (bf16[4,1024,128]{2,1,0:T(8,128)(2,1)S(1)}, bf16[1728,128]{1,0:T(8,128)(2,1)S(1)}, f32[8,128]{1,0:T(8,128)S(1)}, f32[1,1]{1,0:T(1,128)}) custom-call(s32[2,64]{1,0:T(2,128)} %bitcast.95, bf16[2,512,128]{2,1,0:T(8,128)(2,1)S(1)} %get-tuple-element.211.x, f32[2,128,256]{2,1,0:T(8,128)} %w_in.1, f32[2,256]{1,0:T(2,128)} %refs_21_.1, ...), custom_call_target="tpu_custom_call" | custom-call | tf_op jit(solution)/shard_map/towers/pallas_call | solution.py:1305
  101.0 42.7 %conditional.3 = ((f32[4096,128]{1,0:T(8,128)}, bf16[8,960,128]{2,1,0:T(8,128)(2,1)}, f32[8,128]{1,0:T(8,128)S(1)}, f32[8,128]{1,0:T(8,128)S(1)})) conditional(s32[]{:T(128)} %bitcast.12, (s32[8,8,128]{2,1,0:T(8,128)S(1)}, s32[8,16,128]{2,1,0:T(8,128)S(1)}, bf16[4096,128]{1,0:T(8,128)(2,1)S(1)}, bf16[1728,128]{1,0:T(8,128)(2,1)S(1)}, ...), branch_computations={%region_3.0_spmd, %region_4.0_spmd} | conditional | bytes 8 | solution.py:1434
  101.0 42.5 %tail.2 = (f32[4096,128]{1,0:T(8,128)}, bf16[8,960,128]{2,1,0:T(8,128)(2,1)}, f32[8,128]{1,0:T(8,128)S(1)}, f32[8,128]{1,0:T(8,128)S(1)}) custom-call(s32[8,5,128]{2,1,0:T(8,128)S(1)} %bitcast.90, s32[8,16,128]{2,1,0:T(8,128)S(1)} %get-tuple-element.36.ids, bf16[4096,128]{1,0:T(8,128)(2,1)S(1)} %get-tuple-element.37.rows, ...), custom_call_target="tpu_custom_call" | custom-call | tf_op jit(solution)/shard_map/cond/branch_0_fun/tail/pallas_call | solution.py:1395
  143.7 13.9 %update.1 = (f32[4096,128]{1,0:T(8,128)}, f32[4096,128]{1,0:T(8,128)}, f32[4096,128]{1,0:T(8,128)}, f32[1536,128]{1,0:T(8,128)}, f32[1536,128]{1,0:T(8,128)}, /*...) custom-call(f32[8,128]{1,0:T(8,128)S(1)} %get-tuple-element.120.norm, ...), custom_call_target="tpu_custom_call" | custom-call | tf_op jit(solution)/shard_map/update/pallas_call | solution.py:1455
  (1 shorter events, 0.0 us)
Async XLA Ops:
  0.7 34.0 %copy-start = (f32[4096,128]{1,0:T(8,128)S(1)}, f32[4096,128]{1,0:T(8,128)}, u32[]{:S(2)}) copy-start(f32[4096,128]{1,0:T(8,128)} %refs_0_.1) | copy-start | bytes 6291460

commit v9 on v8

--- a/solution.py
+++ b/solution.py
@@ -479,7 +479,7 @@
         grads = [sent.at[blocks[0]] if first == 0 else back.at[blocks[0]]] + [back.at[block] for block in blocks[1:]]
         for k in range(max(first, 1), min(first + group, plane)):
             copies[k - 1].wait_recv()
-        if first + group >= plane:
+        if first == 0:
             gather_shares(1, 0, done)
             pass_shares(0, done, done + last_rows)
         add_rows(ids, capacity, blocks, grads, total, first == 0)
@@ -577,8 +577,10 @@
         sums = []
         for m in range(parts):
             query, key = qkv[tower, m, rows, :], qkv[tower, parts + m, rows, :]
+            none = jnp.zeros_like(key)
+            both = nt(query, jnp.concatenate([jnp.where(side, key, none) for side in halves], 0)) * 0.125
             for half in range(2):
-                scores = nt(jnp.where(halves[half], query, jnp.zeros_like(query)), key) * 0.125
+                scores = both[:, half * LANES : (half + 1) * LANES]
                 scores = jnp.where(live_r, scores, -1000000000.0)
                 expo = jnp.exp(scores - jnp.max(scores, 1, keepdims=True))
                 p = (expo * (1.0 / jnp.sum(expo, 1, keepdims=True))).astype(BF16)
@@ -680,15 +682,16 @@
         for m in range(parts):
             query, key = qkv[tower, m, rows, :], qkv[tower, parts + m, rows, :]
             none = jnp.zeros_like(query)
-            dq = jnp.zeros((LANES, LANES), F32)
-            dk = jnp.zeros((LANES, LANES), F32)
+            pulls = []
             for half in range(2):
                 h = 2 * m + half
                 p = prob[tower, g, h].astype(F32)
                 t = p * pull[h : h + 1, :]
-                ds = ((t - p * jnp.sum(t, 1, keepdims=True)) * scale).astype(BF16)
-                dq = dq + nn(ds, jnp.where(halves[half], key, none))
-                dk = dk + tn(ds, jnp.where(halves[half], query, none))
+                pulls.append(((t - p * jnp.sum(t, 1, keepdims=True)) * scale).astype(BF16))
+            keys = jnp.concatenate([jnp.where(side, key, none) for side in halves], 0)
+            queries = jnp.concatenate([jnp.where(side, query, none) for side in halves], 0)
+            dq = nn(jnp.concatenate(pulls, 1), keys)
+            dk = tn(jnp.concatenate(pulls, 0), queries)
             dqkv[m, rows, :] = dq.astype(BF16)
             dqkv[parts + m, rows, :] = dk.astype(BF16)
             dqkv[2 * parts + m, rows, :] = tn(a_in[tower, g], stacks[m]).astype(BF16)

time: 160 us -> 156 us (0.975)
  Pallas kernels: 155 us -> 151 us
    pallas_call x1, Pallas kernels: 42.5 us -> 39.3 us  [tail(): pl.pallas_call(functools.partial(tail_kernel, plane, line, count, cuts),...]
where the time goes in v9:
time: 156 us
  Pallas kernels  151 us (97%)
  between operations  3.76 us (2%)
    pallas_call x1, Pallas kernels, shards(): pl.pallas_call(functools.partial(towers_kernel, plane, line, slots), out_...  66.1 us
    pallas_call x1, Pallas kernels, tail(): pl.pallas_call(functools.partial(tail_kernel, plane, line, count, cuts),...  39.3 us
    pallas_call x1, Pallas kernels, shards(): pl.pallas_call(functools.partial(fetch_kernel, plane, line, dims, capacit...  32 us
    pallas_call x1, Pallas kernels, shards(): pl.pallas_call(functools.partial(update_kernel, blocks), out_shape=[shape...  13.9 us

profile of v9, /device:TPU:0, one launch (start us, length us, event | category | flops | bytes accessed | tf_op | source)
XLA Modules:
  0.0 156.0 jit_solution(3526823770865567722)
XLA Ops:
  0.7 0.0 copy-start
  0.7 32.0 %fetch.1 = (bf16[1024,128]{1,0:T(8,128)(2,1)S(1)}, s32[8,8,128]{2,1,0:T(8,128)S(1)}, s32[8,16,128]{2,1,0:T(8,128)S(1)}, bf16[4,2,4,256,128]{4,3,2,1,0:T(8,128)(2...) custom-call(s32[2,32,64]{2,1,0:T(8,128)} %bitcast.91, s32[2,32,64]{2,1,0:T(8,128)} %bitcast.92, s32[2,64]{1,0:T(2,128)} %bitcast.94, ...), custom_call_target="tpu_custom_call" | custom-call | tf_op jit(solution)/shard_map/fetch/pallas_call | solution.py:1236
  32.7 0.1 slice_reduce_fusion
  32.8 0.6 fusion
  34.7 0.0 copy-done
  34.7 66.1 %towers.1 = (bf16[4,1024,128]{2,1,0:T(8,128)(2,1)S(1)}, bf16[1728,128]{1,0:T(8,128)(2,1)S(1)}, f32[8,128]{1,0:T(8,128)S(1)}, f32[1,1]{1,0:T(1,128)}) custom-call(s32[2,64]{1,0:T(2,128)} %bitcast.95, bf16[2,512,128]{2,1,0:T(8,128)(2,1)S(1)} %get-tuple-element.211.x, f32[2,128,256]{2,1,0:T(8,128)} %w_in.1, f32[2,256]{1,0:T(2,128)} %refs_21_.1, ...), custom_call_target="tpu_custom_call" | custom-call | tf_op jit(solution)/shard_map/towers/pallas_call | solution.py:1308
  100.8 39.6 %conditional.3 = ((f32[4096,128]{1,0:T(8,128)}, bf16[8,960,128]{2,1,0:T(8,128)(2,1)}, f32[8,128]{1,0:T(8,128)S(1)}, f32[8,128]{1,0:T(8,128)S(1)})) conditional(s32[]{:T(128)} %bitcast.12, (s32[8,8,128]{2,1,0:T(8,128)S(1)}, s32[8,16,128]{2,1,0:T(8,128)S(1)}, bf16[4096,128]{1,0:T(8,128)(2,1)S(1)}, bf16[1728,128]{1,0:T(8,128)(2,1)S(1)}, ...), branch_computations={%region_3.0_spmd, %region_4.0_spmd} | conditional | bytes 8 | solution.py:1437
  100.8 39.3 %tail.2 = (f32[4096,128]{1,0:T(8,128)}, bf16[8,960,128]{2,1,0:T(8,128)(2,1)}, f32[8,128]{1,0:T(8,128)S(1)}, f32[8,128]{1,0:T(8,128)S(1)}) custom-call(s32[8,5,128]{2,1,0:T(8,128)S(1)} %bitcast.90, s32[8,16,128]{2,1,0:T(8,128)S(1)} %get-tuple-element.36.ids, bf16[4096,128]{1,0:T(8,128)(2,1)S(1)} %get-tuple-element.37.rows, ...), custom_call_target="tpu_custom_call" | custom-call | tf_op jit(solution)/shard_map/cond/branch_0_fun/tail/pallas_call | solution.py:1398
  140.4 13.9 %update.1 = (f32[4096,128]{1,0:T(8,128)}, f32[4096,128]{1,0:T(8,128)}, f32[4096,128]{1,0:T(8,128)}, f32[1536,128]{1,0:T(8,128)}, f32[1536,128]{1,0:T(8,128)}, /*...) custom-call(f32[8,128]{1,0:T(8,128)S(1)} %get-tuple-element.120.norm, ...), custom_call_target="tpu_custom_call" | custom-call | tf_op jit(solution)/shard_map/update/pallas_call | solution.py:1458
  (1 shorter events, 0.0 us)
Async XLA Ops:
  0.7 34.0 %copy-start = (f32[4096,128]{1,0:T(8,128)S(1)}, f32[4096,128]{1,0:T(8,128)}, u32[]{:S(2)}) copy-start(f32[4096,128]{1,0:T(8,128)} %refs_0_.1) | copy-start | bytes 6291460
